TPU v7x, 128 devices: a whole 4x4x4 slice. The times are simulated.
128 devices in a mesh: replica: 16 (over x_hi, y, core), fsdp: 8 (over x_lo, z).
Axes of the slice: x: 4 (x_hi: 2, x_lo: 2; x = x_hi * 2 + x_lo), y: 4, z: 4, core: 2. Of those that a mesh axis runs over, the one named last changes fastest.
Arguments:
- latents: bfloat16 [262144, 64], P(('replica', 'fsdp')), may hold values from -6 to 6
- target: bfloat16 [262144, 64], P(('replica', 'fsdp')), may hold values from -6 to 6
- timesteps: int32 [512], P(('replica', 'fsdp')), may hold values from 0 to 999
- patch_weight: float32 [16, 64, 5120], P('replica', None, 'fsdp'), may hold values from -0.75 to 0.75
- head_weight: float32 [16, 64, 5120], P('replica', None, 'fsdp'), may hold values from -0.078125 to 0.078125
- modulation: float32 [16, 2, 5120], P('replica', None, 'fsdp'), may hold values from -3 to 3
- time_weight: float32 [16, 256, 5120], P('replica', None, 'fsdp'), may hold values from -0.375 to 0.375
- anchor: float32 [5120, 5120], P('fsdp', 'replica'), may hold values from -6 to 6
- momentum: float32 [5120, 5120], P('fsdp', 'replica'), may hold values from -4 to 4
- frag_start: bfloat16 [5120, 5120], P('fsdp'), may hold values from -4.1 to 4.1, as said below
- frag_current: bfloat16 [16, 5120, 5120], P('replica', 'fsdp'), may hold values from -10.1 to 10.1, as said below
Outputs:
- patch_new: float32 [16, 64, 5120], P('replica', None, 'fsdp')
- head_new: float32 [16, 64, 5120], P('replica', None, 'fsdp')
- modulation_new: float32 [16, 2, 5120], P('replica', None, 'fsdp')
- time_new: float32 [16, 256, 5120], P('replica', None, 'fsdp')
- new_anchor: float32 [5120, 5120], P('fsdp', 'replica')
- new_momentum: float32 [5120, 5120], P('fsdp', 'replica')
- new_params: bfloat16 [5120, 5120], P('fsdp')
Inputs may be any that keep to these rules, and one draw needn't show every extreme that they name: `frag_start`: every entry is at least 0.02 in magnitude. `frag_current`: every entry is at least 0.02 in magnitude.
All inputs are finite; a program needn't handle non-finite values.
Results may differ from a plain program's by a relative error of at most 0.028.
Values may be sent and summed in bfloat16 or wider, within the bound.
No kernel may reach another device: no remote copies, remote signals or barrier semaphores. Data moves between devices by JAX's collectives and lax.ppermute only.
A program may use at most 192 MiB of HBM per device.

v0:
```python
import math

import jax
import jax.numpy as jnp
from jax import lax
from jax.sharding import PartitionSpec as P

FREQ_DIM = 256
PATCH_DIM = 64
QBLOCK = 128
SAMPLE_TOKENS = 512


epsilon = 1e-06
inner_rate = 0.5
outer_rate = 0.7
momentum_decay = 0.9


def sinusoid(time_steps):
    index = jnp.arange(FREQ_DIM // 2, dtype=jnp.float32)
    frequency = jnp.exp(-math.log(10000.0) * index / (FREQ_DIM // 2))
    angles = time_steps.astype(jnp.float32)[:, None] * frequency[None, :]
    return jnp.concatenate([jnp.cos(angles), jnp.sin(angles)], axis=1)


def silu_slope(pre_act):
    sigmoid_val = jax.nn.sigmoid(pre_act)
    return sigmoid_val * (1.0 + pre_act * (1.0 - sigmoid_val))


def quantize(blocks, scale_bf):
    scale_f = scale_bf.astype(jnp.float32)[:, None, :]
    seven_abs = 7.0 * jnp.abs(blocks)
    levels = jnp.zeros_like(blocks)
    for rung_index in range(7):
        levels = levels + (seven_abs >= (rung_index + 0.5) * scale_f).astype(jnp.float32)
    return (jnp.sign(blocks) * levels).astype(jnp.bfloat16)


def make_visitor(patch_bf, head_bf, mod_bf, tok_count):

    def visit_block(totals, inputs):
        latent_blk, target_blk, embed_row = inputs
        hidden = jnp.dot(latent_blk, patch_bf, preferred_element_type=jnp.float32)
        center = hidden - jnp.mean(hidden, axis=1, keepdims=True)
        inv_std = lax.rsqrt(jnp.mean(center * center, axis=1, keepdims=True) + epsilon)
        normed = center * inv_std
        gain_row = 1.0 + mod_bf[1].astype(jnp.float32) + embed_row
        modulated = (normed * gain_row + mod_bf[0].astype(jnp.float32) + embed_row).astype(
            jnp.bfloat16
        )
        output = lax.dot_general(
            modulated, head_bf, (((1,), (1,)), ((), ())), preferred_element_type=jnp.float32
        )
        grad_out = (2.0 * (output - target_blk.astype(jnp.float32)) / tok_count).astype(
            jnp.bfloat16
        )
        grad_head = lax.dot_general(
            grad_out, modulated, (((0,), (0,)), ((), ())), preferred_element_type=jnp.float32
        )
        grad_mixed = jnp.dot(grad_out, head_bf, preferred_element_type=jnp.float32)
        grad_shift = jnp.sum(grad_mixed, axis=0)
        grad_scale = jnp.sum(grad_mixed * normed, axis=0)
        grad_normed = grad_mixed * gain_row
        grad_hidden = (
            (
                grad_normed
                - jnp.mean(grad_normed, axis=1, keepdims=True)
                - normed * jnp.mean(grad_normed * normed, axis=1, keepdims=True)
            )
            * inv_std
        ).astype(jnp.bfloat16)
        grad_patch = lax.dot_general(
            latent_blk, grad_hidden, (((0,), (0,)), ((), ())), preferred_element_type=jnp.float32
        )
        new_totals = (
            totals[0] + grad_patch,
            totals[1] + grad_head,
            totals[2] + jnp.stack([grad_shift, grad_scale]),
        )
        return (new_totals, grad_shift + grad_scale)

    return visit_block


def per_device(
    latents,
    target,
    timesteps,
    patch_weight,
    head_weight,
    modulation,
    time_weight,
    anchor,
    momentum,
    frag_start,
    frag_current,
):
    fsdp_count = lax.axis_size("fsdp")
    replica_count = lax.axis_size("replica")
    delta = frag_start.astype(jnp.float32) - frag_current[0].astype(jnp.float32)
    row_count = delta.shape[0]
    block_count = row_count // QBLOCK
    blocks = delta.reshape(block_count, QBLOCK, delta.shape[1])
    scale = (jnp.max(jnp.abs(blocks), axis=1) + epsilon).astype(jnp.bfloat16)
    code = quantize(blocks, scale)
    terms = (code.astype(jnp.float32) * scale.astype(jnp.float32)[:, None, :] / 7.0).reshape(
        delta.shape
    )
    total = lax.psum_scatter(
        terms.astype(jnp.bfloat16), "replica", scatter_dimension=1, tiled=True
    ).astype(jnp.float32)
    average = total / replica_count
    new_momentum = momentum_decay * momentum + average
    new_anchor = anchor - outer_rate * (average + momentum_decay * new_momentum)
    new_params = lax.all_gather(new_anchor.astype(jnp.bfloat16), "replica", axis=1, tiled=True)
    samples_here = timesteps.shape[0]
    tok_count = latents.shape[0] * fsdp_count * 1.0
    sines = sinusoid(timesteps).astype(jnp.bfloat16)
    sines_cols = sines.T
    patch_local = patch_weight[0].astype(jnp.bfloat16)
    head_local = head_weight[0].astype(jnp.bfloat16)
    mod_local = modulation[0].astype(jnp.bfloat16)
    time_local = time_weight[0].astype(jnp.bfloat16)
    patch_bf, head_bf, mod_bf, time_bf = (
        lax.all_gather(patch_local, "fsdp", axis=1, tiled=True),
        lax.all_gather(head_local, "fsdp", axis=1, tiled=True),
        lax.all_gather(mod_local, "fsdp", axis=1, tiled=True),
        lax.all_gather(time_local, "fsdp", axis=1, tiled=True),
    )
    pre_act = jnp.dot(sines, time_bf, preferred_element_type=jnp.float32)
    embed = jax.nn.silu(pre_act)
    width = patch_bf.shape[1]
    latent_blocks = latents.reshape(samples_here, SAMPLE_TOKENS, PATCH_DIM)
    target_blocks = target.reshape(samples_here, SAMPLE_TOKENS, PATCH_DIM)
    start_totals = (
        jnp.zeros((PATCH_DIM, width), jnp.float32),
        jnp.zeros((PATCH_DIM, width), jnp.float32),
        jnp.zeros((2, width), jnp.float32),
    )
    totals, grad_embed = lax.scan(
        make_visitor(patch_bf, head_bf, mod_bf, tok_count),
        start_totals,
        (latent_blocks, target_blocks, embed),
    )
    grad_pre = (grad_embed * silu_slope(pre_act)).astype(jnp.bfloat16)
    grad_time_full = jnp.dot(sines_cols, grad_pre, preferred_element_type=jnp.float32)
    grad_patch, grad_head, grad_mod, grad_time = (
        lax.psum_scatter(
            totals[0].astype(jnp.bfloat16), "fsdp", scatter_dimension=1, tiled=True
        ).astype(jnp.float32),
        lax.psum_scatter(
            totals[1].astype(jnp.bfloat16), "fsdp", scatter_dimension=1, tiled=True
        ).astype(jnp.float32),
        lax.psum_scatter(
            totals[2].astype(jnp.bfloat16), "fsdp", scatter_dimension=1, tiled=True
        ).astype(jnp.float32),
        lax.psum_scatter(
            grad_time_full.astype(jnp.bfloat16), "fsdp", scatter_dimension=1, tiled=True
        ).astype(jnp.float32),
    )
    patch_new = patch_weight - inner_rate * grad_patch[None]
    head_new = head_weight - inner_rate * grad_head[None]
    modulation_new = modulation - inner_rate * grad_mod[None]
    time_new = time_weight - inner_rate * grad_time[None]
    return (patch_new, head_new, modulation_new, time_new, new_anchor, new_momentum, new_params)


def solution(mesh):
    in_specs = (
        P(("replica", "fsdp"), None),
        P(("replica", "fsdp"), None),
        P(("replica", "fsdp")),
        P("replica", None, "fsdp"),
        P("replica", None, "fsdp"),
        P("replica", None, "fsdp"),
        P("replica", None, "fsdp"),
        P("fsdp", "replica"),
        P("fsdp", "replica"),
        P("fsdp", None),
        P("replica", "fsdp", None),
    )
    out_specs = (
        P("replica", None, "fsdp"),
        P("replica", None, "fsdp"),
        P("replica", None, "fsdp"),
        P("replica", None, "fsdp"),
        P("fsdp", "replica"),
        P("fsdp", "replica"),
        P("fsdp", None),
    )
    return jax.shard_map(
        per_device, mesh=mesh, in_specs=in_specs, out_specs=out_specs, check_vma=False
    )
```

profile of v0, /device:TPU:1, one launch (start us, length us, event | category | flops | bytes accessed | tf_op | source)
XLA Modules:
  0.0 518.9 jit_solution(11794583616767255501)
XLA Ops:
  10.0 12.0 %fusion.11 = f32[640,5120]{1,0:T(8,128)} fusion(bf16[640,5120]{1,0:T(8,128)(2,1)} %param.22, bf16[1,640,5120]{2,1,0:T(8,128)(2,1)} %param.23), kind=kLoop, calls=%fused_computation.39 | loop fusion | flops 13107200 | bytes 26214400 | tf_op jit(solution)/shard_map/abs | solution.py:34
  22.0 5.7 %reduce_max.9 = f32[5,5120]{1,0:T(8,128)S(1)} reduce(f32[5,128,5120]{2,1,0:T(8,128)} %bitcast.140, f32[]{:T(128)} %constant.92.clone.1), dimensions={1}, to_apply=%region_12.13 | reduce | flops 3251200 | bytes 13209604 | tf_op jit(solution)/shard_map/reduce_max | solution.py:106
  27.8 18.2 %fusion.10 = bf16[640,5120]{1,0:T(8,128)(2,1)} fusion(f32[5,5120]{1,0:T(8,128)S(1)} %convert_element_type.227, f32[5,5120]{1,0:T(8,128)S(1)} %get-tuple-element.266, f32[5,5120]{1,0:T(8,128)S(1)} %get-tuple-element.265, f32[5,5120]{1,0:T(8,128)S(1)} %get-tuple-element.264, f32[5,5120]{1,0:T(8,128)S(1)} %get-tuple-element.263, ...), kind=kLoop, calls=%fused_computation.30 | loop fusion | flops 104857600 | bytes 20480000 | tf_op jit(solution)/shard_map/convert_element_type | solution.py:112
  46.0 9.6 %copy.44 = bf16[640,5120]{0,1:T(8,128)(2,1)} copy(bf16[640,5120]{1,0:T(8,128)(2,1)} %fusion.10) | data formatting | bytes 13107200
  55.8 23.5 %all-gather.1 = bf16[1,2,5120]{2,1,0:T(2,128)(2,1)S(1)} all-gather(bf16[1,2,640]{2,1,0:T(2,128)(2,1)S(1)} %convert_element_type.207), channel_id=3, replica_groups=mesh['replica'=16,'fsdp'=8] {'fsdp'}, dimensions={2}, use_global_device_ids=true | all-gather | bytes 23040 | tf_op jit(solution)/shard_map/all_gather | solution.py:129
  80.4 26.9 %all-gather.3 = bf16[1,64,5120]{2,1,0:T(8,128)(2,1)} all-gather(bf16[1,64,640]{2,1,0:T(8,128)(2,1)S(1)} %convert_element_type.212), channel_id=5, replica_groups=mesh['replica'=16,'fsdp'=8] {'fsdp'}, dimensions={2}, use_global_device_ids=true | all-gather | bytes 737280 | tf_op jit(solution)/shard_map/all_gather | solution.py:128
  107.2 25.3 %all-gather = bf16[1,64,5120]{2,1,0:T(8,128)(2,1)S(1)} all-gather(bf16[1,64,640]{2,1,0:T(8,128)(2,1)S(1)} %convert_element_type.205), channel_id=2, replica_groups=mesh['replica'=16,'fsdp'=8] {'fsdp'}, dimensions={2}, use_global_device_ids=true | all-gather | bytes 737280 | tf_op jit(solution)/shard_map/all_gather | solution.py:127
  135.5 110.0 %while.19 = (s32[]{:T(128)}, f32[64,5120]{1,0:T(8,128)}, f32[64,5120]{1,0:T(8,128)S(1)}, f32[2,5120]{1,0:T(2,128)}, f32[4,5120]{1,0:T(4,128)}, /*index=5*/bf16[4...) while((s32[]{:T(128)}, f32[64,5120]{1,0:T(8,128)}, ...), condition=%wide.region_7.8_spmd.clone, body=%wide.region_0.7_spmd.clone.sunk | while | flops 1749988864 | bytes 100325632 | solution.py:142
  139.3 5.0 add_convert_fusion.4
  144.2 4.5 fusion.49
  148.7 3.7 convolution_add_fusion.5
  152.4 3.7 multiply_reduce_fusion.7
  156.2 4.2 convolution_add_fusion.4
  165.8 5.0 add_convert_fusion.4
  170.8 4.5 fusion.49
  178.9 3.7 multiply_reduce_fusion.7
  182.7 5.5 %convolution_add_fusion.4 = f32[64,5120]{1,0:T(8,128)} fusion(f32[512,5120]{1,0:T(8,128)S(1)} %get-tuple-element.353, f32[512,5120]{1,0:T(8,128)S(1)} %get-tuple-element.349, f32[512]{0:T(512)S(1)} %get-tuple-element.356, f32[512]{0:T(512)S(1)} %get-tuple-element.357, f32[5120]{0:T(1024)S(1)} %bitcast.151, f32[512]{0:T(512)S(1)} %add_rsqrt_fusion.2, ...), kind=kOutput, calls=%fused_computation.7.clone.1 | convolution fusion | flops 357171200 | bytes 23752708 | tf_op jit(solution)/shard_map/while/body/eval_jaxpr/dot_general | solution.py:74
  193.6 5.0 add_convert_fusion.4
  198.6 4.5 fusion.49
  206.7 3.7 multiply_reduce_fusion.7
  210.5 5.5 %convolution_add_fusion.4 = f32[64,5120]{1,0:T(8,128)} fusion(f32[512,5120]{1,0:T(8,128)S(1)} %get-tuple-element.353, f32[512,5120]{1,0:T(8,128)S(1)} %get-tuple-element.349, f32[512]{0:T(512)S(1)} %get-tuple-element.356, f32[512]{0:T(512)S(1)} %get-tuple-element.357, f32[5120]{0:T(1024)S(1)} %bitcast.151, f32[512]{0:T(512)S(1)} %add_rsqrt_fusion.2, ...), kind=kOutput, calls=%fused_computation.7.clone.1 | convolution fusion | flops 357171200 | bytes 23752708 | tf_op jit(solution)/shard_map/while/body/eval_jaxpr/dot_general | solution.py:74
  221.5 5.0 add_convert_fusion.4
  226.4 4.5 fusion.49
  230.9 3.7 convolution_add_fusion.5
  234.6 3.7 multiply_reduce_fusion.7
  238.3 5.5 %convolution_add_fusion.4 = f32[64,5120]{1,0:T(8,128)} fusion(f32[512,5120]{1,0:T(8,128)S(1)} %get-tuple-element.353, f32[512,5120]{1,0:T(8,128)S(1)} %get-tuple-element.349, f32[512]{0:T(512)S(1)} %get-tuple-element.356, f32[512]{0:T(512)S(1)} %get-tuple-element.357, f32[5120]{0:T(1024)S(1)} %bitcast.151, f32[512]{0:T(512)S(1)} %add_rsqrt_fusion.2, ...), kind=kOutput, calls=%fused_computation.7.clone.1 | convolution fusion | flops 357171200 | bytes 23752708 | tf_op jit(solution)/shard_map/while/body/eval_jaxpr/dot_general | solution.py:74
  265.6 35.8 %reduce-scatter.20.cloned.1.call-done = bf16[640,2]{1,0:T(8,128)(2,1)} async-done(((bf16[5120,2]{1,0:T(8,128)(2,1)}), bf16[640,2]{1,0:T(8,128)(2,1)}) %reduce-scatter.20.cloned.1.call-update) | async-done | bytes 2576
  303.1 39.4 %reduce-scatter.16.cloned.1.call-done = bf16[640,64]{1,0:T(8,128)(2,1)} async-done(((bf16[5120,64]{1,0:T(8,128)(2,1)}), bf16[640,64]{1,0:T(8,128)(2,1)}) %reduce-scatter.16.cloned.1.call-update) | async-done | bytes 81936
  343.5 40.2 %reduce-scatter.18.cloned.1.call-done = bf16[640,64]{1,0:T(8,128)(2,1)} async-done(((bf16[5120,64]{1,0:T(8,128)(2,1)}), bf16[640,64]{1,0:T(8,128)(2,1)}) %reduce-scatter.18.cloned.1.call-update) | async-done | bytes 81936
  387.9 42.6 %reduce-scatter.22.cloned.1.call-done = bf16[640,256]{1,0:T(8,128)(2,1)} async-done(((bf16[5120,256]{1,0:T(8,128)(2,1)}), bf16[640,256]{1,0:T(8,128)(2,1)}) %reduce-scatter.22.cloned.1.call-update) | async-done | bytes 327696
  436.1 65.9 %all-gather.7.cloned.1.call-done = bf16[640,5120]{0,1:T(8,128)(2,1)} async-done(((bf16[640,320]{0,1:T(8,128)(2,1)}), bf16[640,5120]{0,1:T(8,128)(2,1)}) %all-gather.7.cloned.1.call-update) | async-done | bytes 6553616 | tf_op jit(solution)/shard_map/all_gather | solution.py:117
  501.9 9.5 %copy.35 = bf16[640,5120]{1,0:T(8,128)(2,1)} copy(bf16[640,5120]{0,1:T(8,128)(2,1)} %all-gather.7.cloned.1.call-done) | data formatting | bytes 13107200
  (146 shorter events, 67.8 us)
Async XLA Ops:
  8.0 124.6 %all-gather.9.cloned.1.call-start = ((), (), s32[]{:S(2)}) async-start(), calls=%async_computation.6 | async-start | bytes 2949120 | tf_op jit(solution)/shard_map/all_gather | solution.py:130
  9.9 250.1 %reduce-scatter.24.cloned.1.call-start = ((), (), s32[]{:S(2)}) async-start(), calls=%async_computation.11 | async-start | bytes 6963200
  46.0 9.8 %copy-start.14 = (s32[4]{0:T(128)S(1)}, s32[4]{0:T(128)}, u32[]{:S(2)}) copy-start(s32[4]{0:T(128)} %param.15) | copy-start | bytes 52
  46.0 9.8 %copy-start.9 = (f32[1,2,640]{2,1,0:T(2,128)S(1)}, f32[1,2,640]{2,1,0:T(2,128)}, u32[]{:S(2)}) copy-start(f32[1,2,640]{2,1,0:T(2,128)} %param.18) | copy-start | bytes 15364
  46.0 33.3 %copy-start.3 = (f32[1,64,640]{2,1,0:T(8,128)S(1)}, f32[1,64,640]{2,1,0:T(8,128)}, u32[]{:S(2)}) copy-start(f32[1,64,640]{2,1,0:T(8,128)} %param.16) | copy-start | bytes 491524
  46.0 33.3 %copy-start.4 = (f32[1,64,640]{2,1,0:T(8,128)S(1)}, f32[1,64,640]{2,1,0:T(8,128)}, u32[]{:S(2)}) copy-start(f32[1,64,640]{2,1,0:T(8,128)} %param.17) | copy-start | bytes 491524
  46.0 33.4 %copy-start.7 = (bf16[2048,64]{0,1:T(8,128)(2,1)S(1)}, bf16[2048,64]{0,1:T(8,128)(2,1)}, u32[]{:S(2)}) copy-start(bf16[2048,64]{0,1:T(8,128)(2,1)} %param.14) | copy-start | bytes 786436
  46.0 34.1 %copy-start.6 = (bf16[2048,64]{0,1:T(8,128)(2,1)S(1)}, bf16[2048,64]{0,1:T(8,128)(2,1)}, u32[]{:S(2)}) copy-start(bf16[2048,64]{0,1:T(8,128)(2,1)} %param.13) | copy-start | bytes 786436
  55.6 245.8 %reduce-scatter.20.cloned.1.call-start = ((), (), s32[]{:S(2)}) async-start(), calls=%async_computation.9 | async-start | bytes 1474560
  132.6 2.9 copy-start.10
  132.6 2.9 copy-start.12
  144.2 8.2 %copy-start = (bf16[64,5120]{1,0:T(8,128)(2,1)S(1)}, bf16[64,5120]{1,0:T(8,128)(2,1)}, u32[]{:S(2)}) copy-start(bf16[64,5120]{1,0:T(8,128)(2,1)} %get-tuple-element.395) | copy-start | bytes 1966084 | tf_op jit(solution)/shard_map/while
  156.1 4.2 copy-start.1
  160.4 1.6 copy-start.2
  170.8 8.1 %copy-start = (bf16[64,5120]{1,0:T(8,128)(2,1)S(1)}, bf16[64,5120]{1,0:T(8,128)(2,1)}, u32[]{:S(2)}) copy-start(bf16[64,5120]{1,0:T(8,128)(2,1)} %get-tuple-element.395) | copy-start | bytes 1966084 | tf_op jit(solution)/shard_map/while
  182.7 5.5 %copy-start.1 = (f32[2,5120]{1,0:T(2,128)S(1)}, f32[2,5120]{1,0:T(2,128)}, u32[]{:S(2)}) copy-start(f32[2,5120]{1,0:T(2,128)} %get-tuple-element.376) | copy-start | bytes 122884 | tf_op jit(solution)/shard_map/while
  188.3 1.6 copy-start.2
  198.6 8.1 %copy-start = (bf16[64,5120]{1,0:T(8,128)(2,1)S(1)}, bf16[64,5120]{1,0:T(8,128)(2,1)}, u32[]{:S(2)}) copy-start(bf16[64,5120]{1,0:T(8,128)(2,1)} %get-tuple-element.395) | copy-start | bytes 1966084 | tf_op jit(solution)/shard_map/while
  210.5 5.5 %copy-start.1 = (f32[2,5120]{1,0:T(2,128)S(1)}, f32[2,5120]{1,0:T(2,128)}, u32[]{:S(2)}) copy-start(f32[2,5120]{1,0:T(2,128)} %get-tuple-element.376) | copy-start | bytes 122884 | tf_op jit(solution)/shard_map/while
  216.1 1.6 copy-start.2
  226.4 8.1 %copy-start = (bf16[64,5120]{1,0:T(8,128)(2,1)S(1)}, bf16[64,5120]{1,0:T(8,128)(2,1)}, u32[]{:S(2)}) copy-start(bf16[64,5120]{1,0:T(8,128)(2,1)} %get-tuple-element.395) | copy-start | bytes 1966084 | tf_op jit(solution)/shard_map/while
  238.3 5.5 %copy-start.1 = (f32[2,5120]{1,0:T(2,128)S(1)}, f32[2,5120]{1,0:T(2,128)}, u32[]{:S(2)}) copy-start(f32[2,5120]{1,0:T(2,128)} %get-tuple-element.376) | copy-start | bytes 122884 | tf_op jit(solution)/shard_map/while
  243.9 1.6 copy-start.2
  245.5 7.0 %copy-start.5 = (f32[4,5120]{1,0:T(4,128)S(1)}, f32[4,5120]{1,0:T(4,128)}, u32[]{:S(2)}) copy-start(f32[4,5120]{1,0:T(4,128)} %get-tuple-element.270) | copy-start | bytes 245764
  245.5 7.0 %copy-start.8 = (f32[4,5120]{1,0:T(4,128)S(1)}, f32[4,5120]{1,0:T(4,128)}, u32[]{:S(2)}) copy-start(f32[4,5120]{1,0:T(4,128)} %get-tuple-element.150) | copy-start | bytes 245764
  245.5 7.0 %copy-start.11 = (bf16[4,128]{1,0:T(4,128)(2,1)S(1)}, bf16[4,128]{1,0:T(4,128)(2,1)}, u32[]{:S(2)}) copy-start(bf16[4,128]{1,0:T(4,128)(2,1)} %copy-done.10) | copy-start | bytes 3076
  245.6 7.0 %copy-start.13 = (bf16[4,128]{1,0:T(4,128)(2,1)S(1)}, bf16[4,128]{1,0:T(4,128)(2,1)}, u32[]{:S(2)}) copy-start(bf16[4,128]{1,0:T(4,128)(2,1)} %copy-done.12) | copy-start | bytes 3076
  248.0 94.5 %reduce-scatter.16.cloned.1.call-start = ((), (), s32[]{:S(2)}) async-start(), calls=%async_computation.7 | async-start | bytes 1474560
  250.9 132.8 %reduce-scatter.18.cloned.1.call-start = ((), (), s32[]{:S(2)}) async-start(), calls=%async_computation.8 | async-start | bytes 1474560
  252.5 178.0 %reduce-scatter.22.cloned.1.call-start = ((), (), s32[]{:S(2)}) async-start(), calls=%async_computation.10 | async-start | bytes 2949120
  256.1 245.9 %all-gather.7.cloned.1.call-start = ((), (), s32[]{:S(2)}) async-start(), calls=%async_computation.5 | async-start | bytes 6963200 | tf_op jit(solution)/shard_map/all_gather | solution.py:117
Sparse Core Ops, SparseCore 0:
  11.2 42.7 all-gather.8
Sparse Core Ops, SparseCore 1:
  55.7 99.0 reduce-scatter.23
  248.1 53.3 reduce-scatter.19
  303.8 38.6 reduce-scatter.15
  345.0 38.6 reduce-scatter.17
  386.8 43.6 reduce-scatter.21
  433.3 68.6 all-gather.6
where the time goes:
time: 521 us; the launch traced here: 519 us
  waiting for transfers between devices  224 us (43%)
  matrix products  78.1 us (15%)
  other arithmetic  77.2 us (15%)
  blocking collectives  75.7 us (15%)
  local copies, waits for them, and re-layouts  47.5 us (9%)
  between operations  15.8 us (3%)
    unnamed x12, waiting for transfers between devices  158 us
    all_gather x1, waiting for transfers between devices, per_device(): lax.all_gather(new_anchor.astype(jnp.bfloat16), 'replica', axis=1, tiled=...  65.9 us
    unnamed x40, local copies, waits for them, and re-layouts  38.3 us
    all_gather x1, blocking collectives, per_device(): lax.all_gather(head_local, 'fsdp', axis=1, tiled=True)  26.9 us
    all_gather x1, blocking collectives, per_device(): lax.all_gather(patch_local, 'fsdp', axis=1, tiled=True)  25.3 us
    all_gather x1, blocking collectives, per_device(): lax.all_gather(mod_local, 'fsdp', axis=1, tiled=True)  23.5 us
    dot_general x4, matrix products, visit_block(): lax.dot_general(latent_blk, grad_hidden, (((0,), (0,)), ((), ())), prefer...  20.6 us
    convert_element_type x4, other arithmetic, visit_block(): (normed * gain_row + mod_bf[0].astype(jnp.float32) + embed_row).astype(jn...  19.8 us
  transfers between devices with their start and end apart: 7, of which 5 were waited for; matrix products, arithmetic and copies ran while one was open for 37% of the time, Pallas kernels for 0%

commit v1 on v0

v1 whole, which is shorter than its diff:
```python
import functools
import math

import jax
import jax.numpy as jnp
from jax import lax
from jax.experimental import pallas as pl
from jax.experimental.pallas import tpu as pltpu
from jax.sharding import PartitionSpec as P

FREQ_DIM = 256
PATCH_DIM = 64
QBLOCK = 128
SAMPLE_TOKENS = 512

epsilon = 1e-06
inner_rate = 0.5
outer_rate = 0.7
momentum_decay = 0.9

f32 = jnp.float32
bf16 = jnp.bfloat16

N_Y, N_XH, N_CORE = 4, 2, 2
COL = 320
PAIR = 640
ROWS = 640
ROUND = 1.5 * 2.0**23
NUDGE = 1.0 + 2.0**-21

NT = (((1,), (1,)), ((), ()))
TN = (((0,), (0,)), ((), ()))
NN = (((1,), (0,)), ((), ()))


def dot(a, b, dims):
    return lax.dot_general(a, b, dims, preferred_element_type=f32)


def split2(x):
    hi = x.astype(bf16)
    return hi, (x - hi.astype(f32)).astype(bf16)


def quantized(delta):
    peak = jnp.max(jnp.abs(delta), axis=0, keepdims=True)
    scale = (peak + epsilon).astype(bf16).astype(f32)
    ratio = (7.0 / scale) * NUDGE
    shifted = delta * ratio + ROUND
    code = jnp.clip(shifted, ROUND - 7.0, ROUND + 7.0) - ROUND
    return code * (scale / 7.0)


def quant_kernel(keep, segments, pos_ref, *refs):
    start_main, start_rest, cur_main, cur_rest = refs[0:4]
    refs = refs[4:]
    if keep:
        other, refs = refs[0], refs[1:]
    outs = refs
    first_core = pos_ref[0] == 0
    low_side = first_core if keep else jnp.logical_not(first_core)
    low_lane = lax.broadcasted_iota(jnp.int32, (64, 128), 1) < 64
    straight = low_lane == low_side

    def put(row, lane, value):
        if keep:
            value = value + other[0, 0, row : row + 64, lane : lane + 128].astype(f32)
        value = value.astype(bf16)
        at = 0
        for out, size in zip(outs, segments):
            begin, end = max(row, at), min(row + 64, at + size)
            if begin < end:
                out[0, 0, begin - at : end - at, lane : lane + 128] = value[
                    begin - row : end - row
                ]
            at += size

    for block in range(ROWS // QBLOCK):
        rows = slice(block * QBLOCK, (block + 1) * QBLOCK)
        for tile in range(2):
            lanes = slice(tile * 128, (tile + 1) * 128)
            delta = start_main[rows, lanes].astype(f32) - cur_main[rows, lanes].astype(f32)
            term = quantized(delta)
            put(block * 64, tile * 128, term[:64])
            put(block * 64, 256 + tile * 128, term[64:])
        term = quantized(start_rest[rows].astype(f32) - cur_rest[rows].astype(f32))
        top, bottom = term[:64], term[64:]
        moved = pltpu.roll(jnp.where(low_side, bottom, top), 64, 1)
        still = jnp.where(low_side, top, bottom)
        put(block * 64, 512, jnp.where(straight, still, moved))


def quantize(pos, frag_start, frag_current, other, y_first, y_step, y_count, segments):
    keep = other is not None

    def chip(i, j, pos):
        return lax.rem(pos[2] + j, N_XH) * N_Y + lax.rem(pos[1] + y_first + i * y_step, N_Y)

    def high(pos):
        return pos[0] if keep else 1 - pos[0]

    main = pl.BlockSpec(
        (pl.Element(ROWS), pl.Element(256)),
        lambda i, j, pos: (0, (chip(i, j, pos) * 5 + 3 * high(pos)) * 128),
    )
    rest = pl.BlockSpec((ROWS, 128), lambda i, j, pos: (0, chip(i, j, pos) * 5 + 2))
    whole = pl.BlockSpec((1, 1, ROWS // 2, PAIR), lambda i, j, pos: (i, j, 0, 0))
    out_specs = [pl.BlockSpec((1, 1, n, PAIR), lambda i, j, pos: (i, j, 0, 0)) for n in segments]
    cells = y_count * N_XH * ROWS * COL
    return pl.pallas_call(
        functools.partial(quant_kernel, keep, segments),
        grid_spec=pltpu.PrefetchScalarGridSpec(
            num_scalar_prefetch=1,
            grid=(y_count, N_XH),
            in_specs=[main, rest, main, rest] + ([whole] if keep else []),
            out_specs=out_specs,
        ),
        out_shape=[jax.ShapeDtypeStruct((y_count, N_XH, n, PAIR), bf16) for n in segments],
        compiler_params=pltpu.CompilerParams(vmem_limit_bytes=24 * 2**20),
        cost_estimate=pl.CostEstimate(flops=16 * cells, bytes_accessed=6 * cells, transcendentals=0),
        name="keep_terms" if keep else "send_terms",
    )(pos, frag_start, frag_start, frag_current, frag_current, *([other] if keep else []))


def outer_kernel(pos_ref, own_ref, far_ref, anchor_ref, momentum_ref, new_anchor, new_momentum, params, native, fresh):
    low_lane = lax.broadcasted_iota(jnp.int32, (64, 128), 1) < 64
    first_core = pos_ref[0] == 0
    total = own_ref[...].astype(f32) + far_ref[...].astype(f32)
    rest = total[:, 512:640]
    swapped = pltpu.roll(rest, 64, 1)
    for half, tail in ((0, rest), (1, swapped)):
        rows = slice(half * 64, half * 64 + 64)
        main0 = total[:, half * 256 : half * 256 + 128]
        main1 = total[:, half * 256 + 128 : half * 256 + 256]

        @pl.when(first_core)
        def _():
            native[rows, 0:128] = main0
            native[rows, 128:256] = main1
            native[rows, 256:384] = tail

        @pl.when(jnp.logical_not(first_core))
        def _():
            turn0, turn1 = pltpu.roll(main0, 64, 1), pltpu.roll(main1, 64, 1)
            native[rows, 0:128] = jnp.where(low_lane, tail, turn0)
            native[rows, 128:256] = jnp.where(low_lane, turn0, turn1)
            native[rows, 256:384] = turn1

    average = native[:, 0:COL] / float(N_Y * N_XH * N_CORE)
    momentum = momentum_decay * momentum_ref[...] + average
    anchor = anchor_ref[...] - outer_rate * (average + momentum_decay * momentum)
    new_momentum[...] = momentum
    new_anchor[...] = anchor
    fresh[:, 0:COL] = anchor

    @pl.when(first_core)
    def _():
        for half in range(2):
            rows = slice(half * 64, half * 64 + 64)
            params[:, half * 256 : half * 256 + 256] = fresh[rows, 0:256].astype(bf16)
        top, bottom = fresh[0:64, 256:384], pltpu.roll(fresh[64:128, 256:384], 64, 1)
        params[:, 512:640] = jnp.where(low_lane, top, bottom).astype(bf16)

    @pl.when(jnp.logical_not(first_core))
    def _():
        for half in range(2):
            rows = slice(half * 64, half * 64 + 64)
            turn = [pltpu.roll(fresh[rows, t * 128 : t * 128 + 128], 64, 1) for t in range(3)]
            params[:, half * 256 : half * 256 + 128] = jnp.where(low_lane, turn[0], turn[1]).astype(bf16)
            params[:, half * 256 + 128 : half * 256 + 256] = jnp.where(low_lane, turn[1], turn[2]).astype(bf16)
        top, bottom = fresh[0:64, 0:128], pltpu.roll(fresh[64:128, 0:128], 64, 1)
        params[:, 512:640] = jnp.where(low_lane, top, bottom).astype(bf16)


def outer_update(pos, own, far, anchor, momentum):
    block = pl.BlockSpec((64, PAIR), lambda i, pos: (i, 0))
    plain = pl.BlockSpec((128, COL), lambda i, pos: (i, 0))
    cells = ROWS * COL
    return pl.pallas_call(
        outer_kernel,
        grid_spec=pltpu.PrefetchScalarGridSpec(
            num_scalar_prefetch=1,
            grid=(ROWS // 128,),
            in_specs=[block, block, plain, plain],
            out_specs=[plain, plain, block],
            scratch_shapes=[pltpu.VMEM((128, 384), f32), pltpu.VMEM((128, 384), f32)],
        ),
        out_shape=[
            jax.ShapeDtypeStruct((ROWS, COL), f32),
            jax.ShapeDtypeStruct((ROWS, COL), f32),
            jax.ShapeDtypeStruct((ROWS // 2, PAIR), bf16),
        ],
        cost_estimate=pl.CostEstimate(flops=10 * cells, bytes_accessed=22 * cells, transcendentals=0),
        name="outer_update",
    )(pos, own, far, anchor, momentum)


def place_kernel(row_count, pos_ref, mine, theirs, into, out):
    del into
    low_lane = lax.broadcasted_iota(jnp.int32, (64, 128), 1) < 64

    def write(low, high):
        for block in range(row_count // 64):
            rows = slice(block * 64, block * 64 + 64)
            base = block * 128
            for half in range(2):
                to = slice(base + half * 64, base + half * 64 + 64)
                out[to, 0:256] = low[rows, half * 256 : half * 256 + 256]
                out[to, 384:640] = high[rows, half * 256 : half * 256 + 256]
            low_rest, high_rest = low[rows, 512:640].astype(f32), high[rows, 512:640].astype(f32)
            top = jnp.where(low_lane, low_rest, pltpu.roll(high_rest, 64, 1))
            bottom = jnp.where(low_lane, pltpu.roll(low_rest, 64, 1), high_rest)
            out[base : base + 64, 256:384] = top.astype(bf16)
            out[base + 64 : base + 128, 256:384] = bottom.astype(bf16)

    @pl.when(pos_ref[0] == 0)
    def _():
        write(mine, theirs)

    @pl.when(pos_ref[0] != 0)
    def _():
        write(theirs, mine)


def place(pos, into, mine, theirs, dy, dx):
    rows = 64

    def spot(i, pos):
        return (i, lax.rem(pos[2] + dx, N_XH) * N_Y + lax.rem(pos[1] + dy, N_Y))

    block = pl.BlockSpec((rows, PAIR), lambda i, pos: (i, 0))
    out_shape = jax.ShapeDtypeStruct((ROWS, N_Y * N_XH * PAIR), bf16)
    first = into is None
    args = (pos, mine, theirs) + (() if first else (into,))
    kernel = functools.partial(place_kernel, rows)
    if first:
        body = lambda pos_ref, a, b, out: kernel(pos_ref, a, b, None, out)
    else:
        body = kernel
    return pl.pallas_call(
        body,
        grid_spec=pltpu.PrefetchScalarGridSpec(
            num_scalar_prefetch=1,
            grid=(ROWS // 128,),
            in_specs=[block, block] + ([] if first else [pl.BlockSpec(memory_space=pl.ANY)]),
            out_specs=pl.BlockSpec((rows * 2, PAIR), spot),
        ),
        out_shape=out_shape,
        input_output_aliases={} if first else {3: 0},
        cost_estimate=pl.CostEstimate(flops=0, bytes_accessed=4 * ROWS * PAIR, transcendentals=0),
        name="place",
    )(*args)


def fragment_sync(pos, anchor, momentum, frag_start, frag_current):
    to_core = [(r, r ^ 1) for r in range(16)]
    to_x = [(r, r ^ 8) for r in range(16)]

    def to_y(step):
        return [
            (xh * 8 + y * 2 + c, xh * 8 + ((y + step) % N_Y) * 2 + c)
            for xh in range(N_XH)
            for y in range(N_Y)
            for c in range(N_CORE)
        ]

    send = functools.partial(lax.ppermute, axis_name="replica")
    up, down = to_y(1), to_y(-1)
    half = ROWS // 4
    halves = (half, half)

    def sends(first, step, count):
        return quantize(pos, frag_start, frag_current, None, first, step, count, (2 * half,))[0]

    def keeps(dy, other):
        return quantize(pos, frag_start, frag_current, other, dy, 1, 1, halves)

    s2 = sends(2, 1, 1)
    r2 = send(s2, perm=to_core)
    s13 = sends(1, 2, 2)
    r13 = send(s13, perm=to_core)
    a2, b2 = keeps(2, r2)
    u1, d1 = send(a2, perm=up), send(b2, perm=down)
    s0 = sends(0, 1, 1)
    r0 = send(s0, perm=to_core)
    a1, b1 = keeps(1, r13[0:1])
    a3, b3 = keeps(3, r13[1:2])
    u2, d2 = send(b1, perm=up), send(a3, perm=down)
    a0, b0 = keeps(0, r0)

    def add(*parts):
        return sum(p.astype(f32) for p in parts)

    fa = [add(a1[0, x], u1[0, x]).astype(bf16) for x in range(2)]
    fb = [add(b3[0, x], d1[0, x]).astype(bf16) for x in range(2)]
    u3, d3 = [None, None], [None, None]
    for x in (1, 0):
        u3[x], d3[x] = send(fa[x], perm=up), send(fb[x], perm=down)

    def reduced(x):
        return jnp.concatenate([add(a0[0, x], d2[0, x], u3[x]), add(b0[0, x], u2[0, x], d3[x])], axis=0)

    far = send(reduced(1).astype(bf16), perm=to_x)
    new_anchor, new_momentum, n0 = outer_update(pos, reduced(0), far, anchor, momentum)

    n1 = send(n0, perm=to_x)
    up0, down0 = send(n0, perm=up), send(n0, perm=down)
    up1, down1 = send(n1, perm=up), send(n1, perm=down)
    ahead = {}
    ahead[0, 0], ahead[0, 1] = n0, n1
    ahead[3, 0], ahead[1, 0], ahead[3, 1], ahead[1, 1] = up0, down0, up1, down1
    rest = []
    for x, below, above in ((0, up0, down0), (1, up1, down1)):
        rest.append((x, send(below[0 : 2 * half // 2], perm=up), send(above[half:], perm=down)))
    for x, first, second in rest:
        ahead[2, x] = jnp.concatenate([first, second], axis=0)
    new_params = None
    for dy, dx in ((0, 0), (0, 1), (3, 0), (1, 0), (3, 1), (1, 1), (2, 0), (2, 1)):
        mine = ahead[dy, dx]
        new_params = place(pos, new_params, mine, send(mine, perm=to_core), dy, dx)
    return new_anchor, new_momentum, new_params


def column(row):
    eye = lax.broadcasted_iota(jnp.int32, (64, 128), 0) == lax.broadcasted_iota(jnp.int32, (64, 128), 1)
    return jnp.sum(jnp.where(eye, row, 0.0), axis=1, keepdims=True)


def gains(pre, mod_ref):
    embed = pre * jax.nn.sigmoid(pre)
    mod = mod_ref[...].astype(bf16).astype(f32)
    return 1.0 + mod[1:2] + embed, mod[0:1] + embed


def weights_kernel(width, *refs):
    count = 8
    heads = refs[:count]
    patch_ref, head_ref, mod_ref, time_ref = refs[count : count + 4]
    outs = refs[count + 4 : 2 * count + 4]
    pre_ref, center_ref, sines_ref, high, low = refs[2 * count + 4 :]
    total = heads[0][8:9, :]
    for k in range(1, count):
        total = total + heads[k][8:9, :]
    for k in range(count):
        sines_ref[4 * k : 4 * k + 4, 0:128] = heads[k][0:4, :]
        sines_ref[4 * k : 4 * k + 4, 128:256] = heads[k][4:8, :]
    pre = dot(sines_ref[...].astype(bf16), time_ref[...].astype(bf16), NN)
    pre_ref[...] = pre
    gain, shift = gains(pre, mod_ref)
    center = patch_ref[...].astype(bf16).astype(f32) - column(total / width)
    center_ref[...] = center
    samples = 4 * count
    for s in range(samples):
        k, i = s // 4, s % 4
        at = (i // 2) * (samples // 2 * 64) + (2 * k + i % 2) * 64
        hi, lo = split2(center * gain[s : s + 1])
        high[at : at + 64, :] = hi
        low[at : at + 64, :] = lo
    head = head_ref[...].astype(bf16)
    blank = jnp.zeros_like(head)
    left = jnp.concatenate([head, blank], axis=0)
    right = jnp.concatenate([blank, head], axis=0)
    part = samples // 2 * 64
    packed = dot(high[0:part], left, NT) + dot(low[0:part], left, NT)
    packed = packed + dot(high[part:], right, NT) + dot(low[part:], right, NT)
    chi, clo = split2(center)
    blank_left = jnp.zeros_like(chi)
    chi_left = jnp.concatenate([chi, blank_left], axis=0)
    clo_left = jnp.concatenate([clo, blank_left], axis=0)
    gram = dot(chi, chi_left, NT) + dot(clo, chi_left, NT) + dot(chi, clo_left, NT)
    for k in range(count):
        rows = jnp.concatenate([shift[4 * k : 4 * k + 4], gain[4 * k : 4 * k + 4]], axis=0)
        hi, lo = split2(rows)
        extra = dot(hi, right, NT) + dot(lo, right, NT)
        outs[k][0:128, :] = packed[128 * k : 128 * k + 128]
        outs[k][128:136, :] = gram[0:8] + extra
        outs[k][136:192, :] = gram[8:64]


def tokens_kernel(width, tokens, *refs):
    count = 8
    parts = refs[:count]
    latent_ref, target_ref, out, wide = refs[count:]
    total = parts[0][...]
    for k in range(1, count):
        total = total + parts[k][...]
    turned = pltpu.roll(total, 64, 1)
    gram = total[128:192, 0:64] / width
    g0 = gram.astype(bf16)
    g1, g2 = split2(gram - g0.astype(f32))
    shift_rows = turned[128:132, 0:64]
    gain_means = turned[132:136, :] / width
    wide[...] = jnp.zeros_like(wide)
    curve = jnp.zeros((64, 64), f32)
    sums = []
    for s in range(4):
        rows = slice(s * SAMPLE_TOKENS, (s + 1) * SAMPLE_TOKENS)
        latent = latent_ref[rows, :]
        latent_f = latent.astype(f32)
        mix = (total if s < 2 else turned)[(s % 2) * 64 : (s % 2) * 64 + 64, 0:64]
        mix_hi, mix_lo = split2(mix)
        spread = dot(latent, g0, NN) + dot(latent, g1, NN) + dot(latent, g2, NN)
        variance = jnp.sum(spread * latent_f, axis=1, keepdims=True)
        inv_std = lax.rsqrt(jnp.maximum(variance, 0.0) + epsilon)
        varied = inv_std * (dot(latent, mix_hi, NN) + dot(latent, mix_lo, NN))
        output = varied + shift_rows[s : s + 1]
        grad_out = (2.0 * (output - target_ref[rows, :].astype(f32)) / tokens).astype(bf16)
        grad_f = grad_out.astype(f32)
        along = jnp.sum(grad_f * varied, axis=1, keepdims=True) / width
        scaled = latent_f * inv_std
        scaled_b = scaled.astype(bf16)
        cross = dot(grad_out, scaled_b, TN)
        curve = curve + dot(scaled_b, (scaled * along).astype(bf16), TN)
        sums.append(jnp.sum(grad_f, axis=0, keepdims=True))
        if s < 2:
            out[s * 64 : s * 64 + 64, 0:64] = cross
        else:
            wide[(s - 2) * 64 : (s - 2) * 64 + 64, 0:64] = cross
    for s in range(4):
        wide[128 + s : 129 + s, 0:64] = sums[s]
    wide[132:136, 0:64] = gain_means[:, 0:64]
    packed = pltpu.roll(wide[...], 64, 1)
    low_lane = lax.broadcasted_iota(jnp.int32, (128, 128), 1) < 64
    out[0:128, :] = jnp.where(low_lane, out[0:128, :], packed[0:128])
    wide[128:192, 0:64] = curve
    out[128:192, :] = jnp.where(low_lane[0:64], wide[128:192, :], packed[128:192])


def finish_kernel(*refs):
    count = 8
    parts = refs[:count]
    pre_ref, center_ref, sines_ref, patch_ref, head_ref, mod_ref, time_ref = refs[count : count + 7]
    patch_new, head_new, mod_new, time_new, sums, slope_rows = refs[count + 7 :]
    pre = pre_ref[...]
    gain, shift = gains(pre, mod_ref)
    head = head_ref[...].astype(bf16)
    head_f = head.astype(f32)
    center = center_ref[...]
    chi, clo = split2(center)
    curve = parts[0][128:192, 0:64]
    for k in range(1, count):
        curve = curve + parts[k][128:192, 0:64]
    curve_hi, curve_lo = split2(curve)
    grad_patch = -(dot(curve_hi, chi, NN) + dot(curve_lo, chi, NN) + dot(curve_hi, clo, NN))
    grad_head = jnp.zeros_like(center)
    grad_scale = jnp.zeros_like(gain[0:1])
    for k in range(count):
        plain = parts[k][...]
        turned = pltpu.roll(plain, 64, 1)
        sums[4 * k : 4 * k + 4, :] = turned[128:132]
        crosses = jnp.concatenate(
            [plain[0:128, 0:64], turned[0:128, 0:64]], axis=0
        ).astype(bf16)
        mixed = dot(crosses, chi, NN)
        pulls = []
        for i in range(4):
            s = 4 * k + i
            one = mixed[i * 64 : i * 64 + 64]
            grad_head = grad_head + one * gain[s : s + 1]
            slope = jnp.sum(head_f * one, axis=0, keepdims=True)
            slope_rows[s : s + 1, :] = slope
            grad_scale = grad_scale + slope
            pulls.append((head_f * gain[s : s + 1] - column(turned[132 + i : 133 + i])).astype(bf16))
        grad_patch = grad_patch + dot(crosses, jnp.concatenate(pulls, axis=0), TN)
    sum_hi, sum_lo = split2(sums[:, 0:64])
    shift_hi, shift_lo = split2(shift)
    grad_head = grad_head + dot(sum_hi, shift_hi, TN) + dot(sum_lo, shift_hi, TN) + dot(sum_hi, shift_lo, TN)
    mixed_sums = dot(sum_hi, head, NN) + dot(sum_lo, head, NN)
    grad_shift = jnp.sum(mixed_sums, axis=0, keepdims=True)
    grad_embed = mixed_sums + slope_rows[...]
    sigmoid = jax.nn.sigmoid(pre)
    grad_pre = (grad_embed * (sigmoid * (1.0 + pre * (1.0 - sigmoid)))).astype(bf16)
    grad_time = dot(sines_ref[...].astype(bf16), grad_pre, TN)
    patch_new[...] = patch_ref[...] - inner_rate * grad_patch
    head_new[...] = head_ref[...] - inner_rate * grad_head
    mod_new[0:1, :] = mod_ref[0:1, :] - inner_rate * grad_shift
    mod_new[1:2, :] = mod_ref[1:2, :] - inner_rate * grad_scale
    time_new[...] = time_ref[...] - inner_rate * grad_time


def sinusoid(time_steps):
    index = jnp.arange(FREQ_DIM // 2, dtype=f32)
    frequency = jnp.exp(-math.log(10000.0) * index / (FREQ_DIM // 2))
    angles = time_steps.astype(f32)[:, None] * frequency[None, :]
    return jnp.cos(angles), jnp.sin(angles)


def inner_step(latents, target, timesteps, patch, head, mod, time):
    count = 8
    columns = patch.shape[1]
    width = float(columns * count)
    tokens = float(latents.shape[0] * count)
    limit = pltpu.CompilerParams(vmem_limit_bytes=32 * 2**20)

    def gather(value):
        found = [value]
        for k in range(1, count):
            found.append(lax.ppermute(value, "fsdp", [(i, (i - k) % count) for i in range(count)]))
        return found

    cos, sin = sinusoid(timesteps)
    row_sums = jnp.sum(patch.astype(bf16).astype(f32), axis=1)
    first = jnp.concatenate(
        [cos, sin, jnp.pad(row_sums, (0, 64))[None], jnp.zeros((7, 128), f32)], axis=0
    )
    heads = gather(first)
    pay = jax.ShapeDtypeStruct((192, 128), f32)
    weights = pl.pallas_call(
        functools.partial(weights_kernel, width),
        out_shape=[pay] * count
        + [
            jax.ShapeDtypeStruct((4 * count, columns), f32),
            jax.ShapeDtypeStruct((PATCH_DIM, columns), f32),
            jax.ShapeDtypeStruct((4 * count, FREQ_DIM), f32),
        ],
        scratch_shapes=[pltpu.VMEM((4 * count * 64, columns), bf16)] * 2,
        compiler_params=limit,
        cost_estimate=pl.CostEstimate(flops=10**9, bytes_accessed=10**7, transcendentals=0),
        name="weight_products",
    )(*heads, patch, head, mod, time)
    partials, (pre, center, sines) = weights[:count], weights[count:]
    received = [partials[0]]
    for k in range(1, count):
        received.append(lax.ppermute(partials[k], "fsdp", [(i, (i + k) % count) for i in range(count)]))
    matrices = pl.pallas_call(
        functools.partial(tokens_kernel, width, tokens),
        out_shape=pay,
        scratch_shapes=[pltpu.VMEM((192, 128), f32)],
        compiler_params=limit,
        cost_estimate=pl.CostEstimate(flops=10**9, bytes_accessed=10**7, transcendentals=0),
        name="token_sums",
    )(*received, latents, target)
    return pl.pallas_call(
        finish_kernel,
        out_shape=[jax.ShapeDtypeStruct(a.shape, f32) for a in (patch, head, mod, time)],
        scratch_shapes=[pltpu.VMEM((4 * count, 128), f32), pltpu.VMEM((4 * count, columns), f32)],
        compiler_params=limit,
        cost_estimate=pl.CostEstimate(flops=10**9, bytes_accessed=10**7, transcendentals=0),
        name="finish",
    )(*gather(matrices), pre, center, sines, patch, head, mod, time)


def per_device(
    latents,
    target,
    timesteps,
    patch_weight,
    head_weight,
    modulation,
    time_weight,
    anchor,
    momentum,
    frag_start,
    frag_current,
):
    replica = lax.axis_index("replica")
    pos = jnp.stack([replica % 2, (replica // 2) % 4, replica // 8]).astype(jnp.int32)
    new_anchor, new_momentum, new_params = fragment_sync(
        pos, anchor, momentum, frag_start, frag_current[0]
    )
    inner = inner_step(
        latents, target, timesteps, patch_weight[0], head_weight[0], modulation[0], time_weight[0]
    )
    return tuple(a[None] for a in inner) + (new_anchor, new_momentum, new_params)


def solution(mesh):
    in_specs = (
        P(("replica", "fsdp"), None),
        P(("replica", "fsdp"), None),
        P(("replica", "fsdp")),
        P("replica", None, "fsdp"),
        P("replica", None, "fsdp"),
        P("replica", None, "fsdp"),
        P("replica", None, "fsdp"),
        P("fsdp", "replica"),
        P("fsdp", "replica"),
        P("fsdp", None),
        P("replica", "fsdp", None),
    )
    out_specs = (
        P("replica", None, "fsdp"),
        P("replica", None, "fsdp"),
        P("replica", None, "fsdp"),
        P("replica", None, "fsdp"),
        P("fsdp", "replica"),
        P("fsdp", "replica"),
        P("fsdp", None),
    )
    return jax.shard_map(
        per_device, mesh=mesh, in_specs=in_specs, out_specs=out_specs, check_vma=False
    )
```

time: 521 us -> 209 us (0.40)
  waiting for transfers between devices: 224 us -> 41.9 us
  matrix products: 78.1 us -> 0 us
  blocking collectives: 75.7 us -> 0 us
  other arithmetic: 77.2 us -> 1.86 us
  starting transfers between devices: 0.3 us -> 74 us
  Pallas kernels: 0 us -> 67.2 us
  local copies, waits for them, and re-layouts: 47.5 us -> 21.2 us
  between operations: 15.8 us -> 0.99 us
    unnamed x12 -> x0, waiting for transfers between devices: 158 us -> none
    dot_general x22 -> x0, matrix products: 78.1 us -> none  [the longest x4 20.6 us: visit_block(): lax.dot_general(latent_blk, grad_hidden, (((0,), (0,)), ((), ())), prefer...]
    all_gather x3 -> x0, blocking collectives: 75.7 us -> none  [the longest x1 26.9 us: per_device(): lax.all_gather(head_local, 'fsdp', axis=1, tiled=True)]
    ppermute x0 -> x50, starting transfers between devices: none -> 74 us  [the longest x14 26.7 us: gather(): lax.ppermute(value, 'fsdp', [(i, (i - k) % count) for i in range(count)])]
    pallas_call x0 -> x19, Pallas kernels: none -> 67.2 us  [the longest x8 36.6 us: place(): pl.pallas_call(body, grid_spec=pltpu.PrefetchScalarGridSpec(num_scalar_pr...]
    all_gather x2 -> x0, waiting for transfers between devices: 65.9 us -> none  [the longest x1 65.9 us: per_device(): lax.all_gather(new_anchor.astype(jnp.bfloat16), 'replica', axis=1, tiled=...]
    convert_element_type x15 -> x3, other arithmetic: 44.5 us -> 0.21 us  [the longest x1 0.11 us: fragment_sync(): fb = [add(b3[0, x], d1[0, x]).astype(bf16) for x in range(2)]]
    ppermute x0 -> x50, waiting for transfers between devices: none -> 41.9 us  [the longest x4 12.9 us: fragment_sync(): u3[x], d3[x] = (send(fa[x], perm=up), send(fb[x], perm=down))]
  transfers between devices with their start and end apart: 7 -> 50, of which waited for: 5 -> 20; matrix products, arithmetic and copies ran while one was open for 37% -> 8% of each run, Pallas kernels for 0% -> 25%
where the time goes in v1:
time: 209 us; the launch traced here: 207 us
  starting transfers between devices  74 us (35%)
  Pallas kernels  67.2 us (32%)
  waiting for transfers between devices  41.9 us (20%)
  local copies, waits for them, and re-layouts  21.2 us (10%)
    pallas_call x8, Pallas kernels, place(): pl.pallas_call(body, grid_spec=pltpu.PrefetchScalarGridSpec(num_scalar_pr...  36.6 us
    ppermute x14, starting transfers between devices, gather(): lax.ppermute(value, 'fsdp', [(i, (i - k) % count) for i in range(count)])  26.7 us
    ppermute x8, starting transfers between devices, fragment_sync(): new_params = place(pos, new_params, mine, send(mine, perm=to_core), dy, dx)  16.4 us
    unnamed x30, local copies, waits for them, and re-layouts  15.8 us
    pallas_call x7, Pallas kernels, quantize(): pl.pallas_call(functools.partial(quant_kernel, keep, segments), grid_spec...  15.4 us
    ppermute x4, waiting for transfers between devices, fragment_sync(): u3[x], d3[x] = (send(fa[x], perm=up), send(fb[x], perm=down))  12.9 us
    ppermute x14, waiting for transfers between devices, gather(): lax.ppermute(value, 'fsdp', [(i, (i - k) % count) for i in range(count)])  12.9 us
    ppermute x7, starting transfers between devices, inner_step(): lax.ppermute(partials[k], 'fsdp', [(i, (i + k) % count) for i in range(co...  7.53 us
  transfers between devices with their start and end apart: 50, of which 20 were waited for; matrix products, arithmetic and copies ran while one was open for 8% of the time, Pallas kernels for 25%

profile of v1, /device:TPU:1, one launch (start us, length us, event | category | flops | bytes accessed | tf_op | source)
XLA Modules:
  0.0 207.1 jit_solution(17289794285224188078)
XLA Ops:
  0.8 2.9 %copy-done = bf16[640,5120]{1,0:T(8,128)(2,1)S(1)} copy-done((bf16[640,5120]{1,0:T(8,128)(2,1)S(1)}, bf16[640,5120]{1,0:T(8,128)(2,1)}, u32[]{:S(2)}) %copy-start) | copy-done | bytes 6553624
  3.6 2.9 %copy-done.1 = bf16[1,640,5120]{2,1,0:T(8,128)(2,1)S(1)} copy-done((bf16[1,640,5120]{2,1,0:T(8,128)(2,1)S(1)}, bf16[1,640,5120]{2,1,0:T(8,128)(2,1)}, u32[]{:S(2)}) %copy-start.1) | copy-done | bytes 6553624
  6.5 3.2 %send_terms.4 = bf16[2,2,320,640]{3,2,1,0:T(8,128)(2,1)S(1)} custom-call(s32[3]{0:T(128)S(1)} %pad_add_fusion.pos_ref, bf16[640,5120]{1,0:T(8,128)(2,1)S(1)} %copy-done, bf16[640,5120]{1,0:T(8,128)(2,1)S(1)} %copy-done, bf16[640,5120]{1,0:T(8,128)(2,1)S(1)} %bitcast.35, bf16[640,5120]{1,0:T(8,128)(2,1)S(1)} %bitcast.36), custom_call_target="tpu_custom_call" | custom-call | flops 13107200 | bytes 4915200 | tf_op jit(solution)/shard_map/send_terms/pallas_call | solution.py:110
  34.7 3.0 %collective-permute-done.26 = bf16[160,640]{1,0:T(8,128)(2,1)S(1)} collective-permute-done((bf16[160,640]{1,0:T(8,128)(2,1)S(1)}, bf16[160,640]{1,0:T(8,128)(2,1)S(1)}, u32[]{:S(2)}, u32[]{:S(2)}) %collective-permute-start.26) | collective-permute-done | bytes 204832 | tf_op jit(solution)/shard_map/ppermute | solution.py:298
  37.8 4.4 %collective-permute-done.30 = bf16[160,640]{1,0:T(8,128)(2,1)S(1)} collective-permute-done((bf16[160,640]{1,0:T(8,128)(2,1)S(1)}, bf16[160,640]{1,0:T(8,128)(2,1)S(1)}, u32[]{:S(2)}, u32[]{:S(2)}) %collective-permute-start.30) | collective-permute-done | bytes 204832 | tf_op jit(solution)/shard_map/ppermute | solution.py:298
  43.4 4.4 %collective-permute-done.31 = bf16[160,640]{1,0:T(8,128)(2,1)S(1)} collective-permute-done((bf16[160,640]{1,0:T(8,128)(2,1)S(1)}, bf16[160,640]{1,0:T(8,128)(2,1)S(1)}, u32[]{:S(2)}, u32[]{:S(2)}) %collective-permute-start.31) | collective-permute-done | bytes 204832 | tf_op jit(solution)/shard_map/ppermute | solution.py:298
  47.8 3.1 %collective-permute-done.27 = bf16[1,2,160,640]{3,2,1,0:T(8,128)(2,1)S(1)} collective-permute-done((bf16[1,2,160,640]{3,2,1,0:T(8,128)(2,1)S(1)}, bf16[1,2,160,640]{3,2,1,0:T(8,128)(2,1)S(1)}, u32[]{:S(2)}, u32[]{:S(2)}) %collective-permute-start.27) | collective-permute-done | bytes 409632 | tf_op jit(solution)/shard_map/ppermute | solution.py:288
  58.6 3.6 %collective-permute-done.32.far_ref = bf16[320,640]{1,0:T(8,128)(2,1)} collective-permute-done((bf16[320,640]{1,0:T(8,128)(2,1)S(1)}, bf16[320,640]{1,0:T(8,128)(2,1)}, u32[]{:S(2)}, u32[]{:S(2)}) %collective-permute-start.32) | collective-permute-done | bytes 409632 | tf_op jit(solution)/shard_map/ppermute | solution.py:303
  62.2 6.5 %outer_update.1 = (f32[640,320]{1,0:T(8,128)}, f32[640,320]{1,0:T(8,128)}, bf16[320,640]{1,0:T(8,128)(2,1)}) custom-call(s32[3]{0:T(128)} %copy-done.3, f32[320,640]{1,0:T(8,128)} %pad_maximum_fusion.own_ref, bf16[320,640]{1,0:T(8,128)(2,1)} %collective-permute-done.32.far_ref, f32[640,320]{1,0:T(8,128)} %copy.27.anchor_ref, f32[640,320]{1,0:T(8,128)} %copy.28.momentum_ref), custom_call_target="tpu_custom_call" | custom-call | flops 2048000 | bytes 4505600 | tf_op jit(solution)/shard_map/outer_update/pallas_call | solution.py:179
  71.2 3.8 %collective-permute-start = (f32[16,128]{1,0:T(8,128)S(1)}, f32[16,128]{1,0:T(8,128)S(1)}, u32[]{:S(2)}, u32[]{:S(2)}) collective-permute-start(f32[16,128]{1,0:T(8,128)S(1)} %maximum_maximum_fusion.refs_0_), channel_id=1, source_target_pairs={{0,7},{1,0},{2,1},{3,2},{4,3},{5,4},{6,5},{7,6},{8,15},{9,8},{10,9... | collective-permute-start | bytes 24584 | tf_op jit(solution)/shard_map/ppermute | solution.py:498
  78.1 3.5 %collective-permute-start.4 = (f32[16,128]{1,0:T(8,128)S(1)}, f32[16,128]{1,0:T(8,128)S(1)}, u32[]{:S(2)}, u32[]{:S(2)}) collective-permute-start(f32[16,128]{1,0:T(8,128)S(1)} %maximum_maximum_fusion.refs_0_), channel_id=1, source_target_pairs={{0,3},{1,4},{2,5},{3,6},{4,7},{5,0},{6,1},{7,2},{8,11},{9,12},{10,... | collective-permute-start | bytes 24584 | tf_op jit(solution)/shard_map/ppermute | solution.py:498
  83.2 3.4 %collective-permute-done.5.refs_6_ = f32[16,128]{1,0:T(8,128)S(1)} collective-permute-done((f32[16,128]{1,0:T(8,128)S(1)}, f32[16,128]{1,0:T(8,128)S(1)}, u32[]{:S(2)}, u32[]{:S(2)}) %collective-permute-start.5) | collective-permute-done | bytes 8224 | tf_op jit(solution)/shard_map/ppermute | solution.py:498
  86.8 2.7 %weight_products.1 = (f32[192,128]{1,0:T(8,128)S(1)}, f32[192,128]{1,0:T(8,128)S(1)}, f32[192,128]{1,0:T(8,128)S(1)}, f32[192,128]{1,0:T(8,128)S(1)}, f32[192,12...) custom-call(f32[16,128]{1,0:T(8,128)S(1)} %maximum_maximum_fusion.re, ...), custom_call_target="tpu_custom_call" | custom-call | flops 1000000000 | bytes 10000000 | tf_op jit(solution)/shard_map/weight_products/pallas_call | solution.py:508
  98.0 2.9 %collective-permute-start.8 = (f32[192,128]{1,0:T(8,128)S(1)}, f32[192,128]{1,0:T(8,128)S(1)}, u32[]{:S(2)}, u32[]{:S(2)}) collective-permute-start(f32[192,128]{1,0:T(8,128)S(1)} %get-tuple-element.35), channel_id=1, source_target_pairs={{0,2},{1,3},{2,4},{3,5},{4,6},{5,7},{6,0},{7,1},{8,10},{9,11},{10,... | collective-permute-start | bytes 294920 | tf_op jit(solution)/shard_map/ppermute | solution.py:524
  111.1 4.2 %collective-permute-start.14 = (f32[192,128]{1,0:T(8,128)S(1)}, f32[192,128]{1,0:T(8,128)S(1)}, u32[]{:S(2)}, u32[]{:S(2)}) collective-permute-start(f32[192,128]{1,0:T(8,128)S(1)} %token_sums.1.refs_0_), channel_id=1, source_target_pairs={{0,7},{1,0},{2,1},{3,2},{4,3},{5,4},{6,5},{7,6},{8,15},{9,8},{10,9... | collective-permute-start | bytes 294920 | tf_op jit(solution)/shard_map/ppermute | solution.py:498
  118.9 3.0 %collective-permute-done.15.refs_2_ = f32[192,128]{1,0:T(8,128)S(1)} collective-permute-done((f32[192,128]{1,0:T(8,128)S(1)}, f32[192,128]{1,0:T(8,128)S(1)}, u32[]{:S(2)}, u32[]{:S(2)}) %collective-permute-start.15) | collective-permute-done | bytes 98336 | tf_op jit(solution)/shard_map/ppermute | solution.py:498
  121.9 2.6 %collective-permute-start.16 = (f32[192,128]{1,0:T(8,128)S(1)}, f32[192,128]{1,0:T(8,128)S(1)}, u32[]{:S(2)}, u32[]{:S(2)}) collective-permute-start(f32[192,128]{1,0:T(8,128)S(1)} %token_sums.1.refs_0_), channel_id=1, source_target_pairs={{0,5},{1,6},{2,7},{3,0},{4,1},{5,2},{6,3},{7,4},{8,13},{9,14},{10,... | collective-permute-start | bytes 294920 | tf_op jit(solution)/shard_map/ppermute | solution.py:498
  130.1 9.0 %collective-permute-start.49 = (bf16[320,640]{1,0:T(8,128)(2,1)}, bf16[320,640]{1,0:T(8,128)(2,1)}, u32[]{:S(2)}, u32[]{:S(2)}) collective-permute-start(bf16[320,640]{1,0:T(8,128)(2,1)} %get-tuple-element.58.a), channel_id=1, source_target_pairs={{0,8},{8,0},{16,24},{24,16},{32,40},{40,32},{48,56},{56,48},{64,72... | collective-permute-start | bytes 1228808 | tf_op jit(solution)/shard_map/ppermute | solution.py:320
  144.7 2.7 %collective-permute-done.35 = bf16[160,640]{1,0:T(8,128)(2,1)S(1)} collective-permute-done((bf16[160,640]{1,0:T(8,128)(2,1)S(1)}, bf16[160,640]{1,0:T(8,128)(2,1)S(1)}, u32[]{:S(2)}, u32[]{:S(2)}) %collective-permute-start.35) | collective-permute-done | bytes 204832 | tf_op jit(solution)/shard_map/ppermute | solution.py:314
  147.4 2.6 %collective-permute-start.18 = (f32[192,128]{1,0:T(8,128)S(1)}, f32[192,128]{1,0:T(8,128)S(1)}, u32[]{:S(2)}, u32[]{:S(2)}) collective-permute-start(f32[192,128]{1,0:T(8,128)S(1)} %token_sums.1.refs_0_), channel_id=1, source_target_pairs={{0,3},{1,4},{2,5},{3,6},{4,7},{5,0},{6,1},{7,2},{8,11},{9,12},{10,... | collective-permute-start | bytes 294920 | tf_op jit(solution)/shard_map/ppermute | solution.py:498
  151.8 2.8 %collective-permute-start.19 = (f32[192,128]{1,0:T(8,128)S(1)}, f32[192,128]{1,0:T(8,128)S(1)}, u32[]{:S(2)}, u32[]{:S(2)}) collective-permute-start(f32[192,128]{1,0:T(8,128)S(1)} %token_sums.1.refs_0_), channel_id=1, source_target_pairs={{0,2},{1,3},{2,4},{3,5},{4,6},{5,7},{6,0},{7,1},{8,10},{9,11},{10,... | collective-permute-start | bytes 294920 | tf_op jit(solution)/shard_map/ppermute | solution.py:498
  157.7 3.7 %collective-permute-start.46 = (bf16[320,640]{1,0:T(8,128)(2,1)}, bf16[320,640]{1,0:T(8,128)(2,1)}, u32[]{:S(2)}, u32[]{:S(2)}) collective-permute-start(bf16[320,640]{1,0:T(8,128)(2,1)} %collective-permute-done.41.mine), channel_id=1, source_target_pairs={{0,8},{8,0},{16,24},{24,16},{32,40},{40,32},{48,56},{56,48},{64,72... | collective-permute-start | bytes 1228808 | tf_op jit(solution)/shard_map/ppermute | solution.py:320
  161.3 2.7 %collective-permute-start.45 = (bf16[320,640]{1,0:T(8,128)(2,1)}, bf16[320,640]{1,0:T(8,128)(2,1)}, u32[]{:S(2)}, u32[]{:S(2)}) collective-permute-start(bf16[320,640]{1,0:T(8,128)(2,1)} %collective-permute-done.34.mine), channel_id=1, source_target_pairs={{0,8},{8,0},{16,24},{24,16},{32,40},{40,32},{48,56},{56,48},{64,72... | collective-permute-start | bytes 1228808 | tf_op jit(solution)/shard_map/ppermute | solution.py:320
  164.7 3.4 %finish.1 = (f32[64,640]{1,0:T(8,128)}, f32[64,640]{1,0:T(8,128)}, f32[2,640]{1,0:T(2,128)}, f32[256,640]{1,0:T(8,128)}) custom-call(f32[192,128]{1,0:T(8,128)S(1)} %token_sums.1.refs_0_, f32[192,128]{1,0:T(8,128)S(1)} %collective-permute-done.14.refs_1_, f32[192,128]{1,0:T(8,128)S(1)} %collective-permute-done.15.refs_2_, ...), custom_call_target="tpu_custom_call" | custom-call | flops 1000000000 | bytes 10000000 | tf_op jit(solution)/shard_map/finish/pallas_call | solution.py:533
  170.4 4.6 %place.8.into = bf16[640,5120]{1,0:T(8,128)(2,1)} custom-call(s32[3]{0:T(128)} %copy-done.3, bf16[320,640]{1,0:T(8,128)(2,1)} %get-tuple-element.58.a, bf16[320,640]{1,0:T(8,128)(2,1)} %collective-permute-done.49.b), custom_call_target="tpu_custom_call" | custom-call | bytes 1638400 | tf_op jit(solution)/shard_map/place/pallas_call | solution.py:240
  175.0 4.6 %place.9.into = bf16[640,5120]{1,0:T(8,128)(2,1)} custom-call(s32[3]{0:T(128)} %copy-done.3, bf16[320,640]{1,0:T(8,128)(2,1)} %collective-permute-done.33.mine, bf16[320,640]{1,0:T(8,128)(2,1)} %collective-permute-done.48.theirs, bf16[640,5120]{1,0:T(8,128)(2,1)} %place.8.into), custom_call_target="tpu_custom_call", output_to_operand_aliasing={{}: (3, {})} | custom-call | bytes 1638400 | tf_op jit(solution)/shard_map/place/pallas_call | solution.py:240
  179.6 4.6 %place.10.into = bf16[640,5120]{1,0:T(8,128)(2,1)} custom-call(s32[3]{0:T(128)} %copy-done.3, bf16[320,640]{1,0:T(8,128)(2,1)} %collective-permute-done.39.mine, bf16[320,640]{1,0:T(8,128)(2,1)} %collective-permute-done.47.theirs, bf16[640,5120]{1,0:T(8,128)(2,1)} %place.9.into), custom_call_target="tpu_custom_call", output_to_operand_aliasing={{}: (3, {})} | custom-call | bytes 1638400 | tf_op jit(solution)/shard_map/place/pallas_call | solution.py:240
  184.2 4.6 %place.11.into = bf16[640,5120]{1,0:T(8,128)(2,1)} custom-call(s32[3]{0:T(128)} %copy-done.3, bf16[320,640]{1,0:T(8,128)(2,1)} %collective-permute-done.41.mine, bf16[320,640]{1,0:T(8,128)(2,1)} %collective-permute-done.46.theirs, bf16[640,5120]{1,0:T(8,128)(2,1)} %place.10.into), custom_call_target="tpu_custom_call", output_to_operand_aliasing={{}: (3, {})} | custom-call | bytes 1638400 | tf_op jit(solution)/shard_map/place/pallas_call | solution.py:240
  188.8 4.6 %place.12.into = bf16[640,5120]{1,0:T(8,128)(2,1)} custom-call(s32[3]{0:T(128)} %copy-done.3, bf16[320,640]{1,0:T(8,128)(2,1)} %collective-permute-done.34.mine, bf16[320,640]{1,0:T(8,128)(2,1)} %collective-permute-done.45.theirs, bf16[640,5120]{1,0:T(8,128)(2,1)} %place.11.into), custom_call_target="tpu_custom_call", output_to_operand_aliasing={{}: (3, {})} | custom-call | bytes 1638400 | tf_op jit(solution)/shard_map/place/pallas_call | solution.py:240
  193.4 4.6 %place.13.into = bf16[640,5120]{1,0:T(8,128)(2,1)} custom-call(s32[3]{0:T(128)} %copy-done.3, bf16[320,640]{1,0:T(8,128)(2,1)} %collective-permute-done.36.mine, bf16[320,640]{1,0:T(8,128)(2,1)} %collective-permute-done.44.theirs, bf16[640,5120]{1,0:T(8,128)(2,1)} %place.12.into), custom_call_target="tpu_custom_call", output_to_operand_aliasing={{}: (3, {})} | custom-call | bytes 1638400 | tf_op jit(solution)/shard_map/place/pallas_call | solution.py:240
  197.9 4.6 %place.14.into = bf16[640,5120]{1,0:T(8,128)(2,1)} custom-call(s32[3]{0:T(128)} %copy-done.3, bf16[320,640]{1,0:T(8,128)(2,1)} %constant_dynamic-update-slice_fusion.2.mine, bf16[320,640]{1,0:T(8,128)(2,1)} %collective-permute-done.43.theirs, bf16[640,5120]{1,0:T(8,128)(2,1)} %place.13.into), custom_call_target="tpu_custom_call", output_to_operand_aliasing={{}: (3, {})} | custom-call | bytes 1638400 | tf_op jit(solution)/shard_map/place/pallas_call | solution.py:240
  202.5 4.6 %place.15 = bf16[640,5120]{1,0:T(8,128)(2,1)} custom-call(s32[3]{0:T(128)} %copy-done.3, bf16[320,640]{1,0:T(8,128)(2,1)} %constant_dynamic-update-slice_fusion.mine, bf16[320,640]{1,0:T(8,128)(2,1)} %collective-permute-done.38.theirs, bf16[640,5120]{1,0:T(8,128)(2,1)} %place.14.into), custom_call_target="tpu_custom_call", output_to_operand_aliasing={{}: (3, {})} | custom-call | bytes 1638400 | tf_op jit(solution)/shard_map/place/pallas_call | solution.py:240
  (139 shorter events, 82.3 us)
Async XLA Ops:
  9.7 13.4 %collective-permute-start.22 = (bf16[2,2,320,640]{3,2,1,0:T(8,128)(2,1)S(1)}, bf16[2,2,320,640]{3,2,1,0:T(8,128)(2,1)S(1)}, u32[]{:S(2)}, u32[]{:S(2)}) collective-permute-start(bf16[2,2,320,640]{3,2,1,0:T(8,128)(2,1)S(1)} %send_terms.4), channel_id=1, source_target_pairs={{0,8},{8,0},{16,24},{24,16},{32,40},{40,32},{48,56},{56,48},{64,72... | collective-permute-start | bytes 4915208 | tf_op jit(solution)/shard_map/ppermute | solution.py:281
  17.9 12.6 %collective-permute-start.25 = (bf16[1,2,160,640]{3,2,1,0:T(8,128)(2,1)S(1)}, bf16[1,2,160,640]{3,2,1,0:T(8,128)(2,1)S(1)}, u32[]{:S(2)}, u32[]{:S(2)}) collective-permute-start(bf16[1,2,160,640]{3,2,1,0:T(8,128)(2,1)S(1)} %get-tuple-element.51), channel_id=1, source_target_pairs={{0,16},{8,24},{16,32},{24,40},{32,48},{40,56},{48,0},{56,8},{64,80... | collective-permute-start | bytes 1228808 | tf_op jit(solution)/shard_map/ppermute | solution.py:283
  19.5 13.4 %collective-permute-start.28 = (bf16[1,2,160,640]{3,2,1,0:T(8,128)(2,1)S(1)}, bf16[1,2,160,640]{3,2,1,0:T(8,128)(2,1)S(1)}, u32[]{:S(2)}, u32[]{:S(2)}) collective-permute-start(bf16[1,2,160,640]{3,2,1,0:T(8,128)(2,1)S(1)} %get-tuple-element.55), channel_id=1, source_target_pairs={{0,48},{8,56},{16,0},{24,8},{32,16},{40,24},{48,32},{56,40},{64,11... | collective-permute-start | bytes 1228808 | tf_op jit(solution)/shard_map/ppermute | solution.py:283
  25.3 16.8 %collective-permute-start.23 = (bf16[1,2,160,640]{3,2,1,0:T(8,128)(2,1)S(1)}, bf16[1,2,160,640]{3,2,1,0:T(8,128)(2,1)S(1)}, u32[]{:S(2)}, u32[]{:S(2)}) collective-permute-start(bf16[1,2,160,640]{3,2,1,0:T(8,128)(2,1)S(1)} %get-tuple-element.49), channel_id=1, source_target_pairs={{0,48},{8,56},{16,0},{24,8},{32,16},{40,24},{48,32},{56,40},{64,11... | collective-permute-start | bytes 1228808 | tf_op jit(solution)/shard_map/ppermute | solution.py:288
  30.6 7.2 %collective-permute-start.26 = (bf16[160,640]{1,0:T(8,128)(2,1)S(1)}, bf16[160,640]{1,0:T(8,128)(2,1)S(1)}, u32[]{:S(2)}, u32[]{:S(2)}) collective-permute-start(bf16[160,640]{1,0:T(8,128)(2,1)S(1)} %get-tuple-element.71), channel_id=1, source_target_pairs={{0,16},{8,24},{16,32},{24,40},{32,48},{40,56},{48,0},{56,8},{64,80... | collective-permute-start | bytes 614408 | tf_op jit(solution)/shard_map/ppermute | solution.py:298
  30.7 11.5 %collective-permute-start.30 = (bf16[160,640]{1,0:T(8,128)(2,1)S(1)}, bf16[160,640]{1,0:T(8,128)(2,1)S(1)}, u32[]{:S(2)}, u32[]{:S(2)}) collective-permute-start(bf16[160,640]{1,0:T(8,128)(2,1)S(1)} %get-tuple-element.70), channel_id=1, source_target_pairs={{0,16},{8,24},{16,32},{24,40},{32,48},{40,56},{48,0},{56,8},{64,80... | collective-permute-start | bytes 614408 | tf_op jit(solution)/shard_map/ppermute | solution.py:298
  31.8 19.1 %collective-permute-start.27 = (bf16[1,2,160,640]{3,2,1,0:T(8,128)(2,1)S(1)}, bf16[1,2,160,640]{3,2,1,0:T(8,128)(2,1)S(1)}, u32[]{:S(2)}, u32[]{:S(2)}) collective-permute-start(bf16[1,2,160,640]{3,2,1,0:T(8,128)(2,1)S(1)} %get-tuple-element.53), channel_id=1, source_target_pairs={{0,16},{8,24},{16,32},{24,40},{32,48},{40,56},{48,0},{56,8},{64,80... | collective-permute-start | bytes 1228808 | tf_op jit(solution)/shard_map/ppermute | solution.py:288
  33.0 10.4 %collective-permute-start.29 = (bf16[160,640]{1,0:T(8,128)(2,1)S(1)}, bf16[160,640]{1,0:T(8,128)(2,1)S(1)}, u32[]{:S(2)}, u32[]{:S(2)}) collective-permute-start(bf16[160,640]{1,0:T(8,128)(2,1)S(1)} %get-tuple-element.75), channel_id=1, source_target_pairs={{0,48},{8,56},{16,0},{24,8},{32,16},{40,24},{48,32},{56,40},{64,11... | collective-permute-start | bytes 614408 | tf_op jit(solution)/shard_map/ppermute | solution.py:298
  37.8 10.0 %collective-permute-start.31 = (bf16[160,640]{1,0:T(8,128)(2,1)S(1)}, bf16[160,640]{1,0:T(8,128)(2,1)S(1)}, u32[]{:S(2)}, u32[]{:S(2)}) collective-permute-start(bf16[160,640]{1,0:T(8,128)(2,1)S(1)} %get-tuple-element.74), channel_id=1, source_target_pairs={{0,48},{8,56},{16,0},{24,8},{32,16},{40,24},{48,32},{56,40},{64,11... | collective-permute-start | bytes 614408 | tf_op jit(solution)/shard_map/ppermute | solution.py:298
  51.1 11.1 %collective-permute-start.32 = (bf16[320,640]{1,0:T(8,128)(2,1)S(1)}, bf16[320,640]{1,0:T(8,128)(2,1)}, u32[]{:S(2)}, u32[]{:S(2)}) collective-permute-start(bf16[320,640]{1,0:T(8,128)(2,1)S(1)} %pad_maximum_fusion.1), channel_id=1, source_target_pairs={{0,64},{8,72},{16,80},{24,88},{32,96},{40,104},{48,112},{56,120},{... | collective-permute-start | bytes 1228808 | tf_op jit(solution)/shard_map/ppermute | solution.py:303
  68.7 32.2 %collective-permute-start.33 = (bf16[320,640]{1,0:T(8,128)(2,1)}, bf16[320,640]{1,0:T(8,128)(2,1)}, u32[]{:S(2)}, u32[]{:S(2)}) collective-permute-start(bf16[320,640]{1,0:T(8,128)(2,1)} %get-tuple-element.58.a), channel_id=1, source_target_pairs={{0,64},{8,72},{16,80},{24,88},{32,96},{40,104},{48,112},{56,120},{... | collective-permute-start | bytes 1228808 | tf_op jit(solution)/shard_map/ppermute | solution.py:306
  71.2 6.9 %collective-permute-start = (f32[16,128]{1,0:T(8,128)S(1)}, f32[16,128]{1,0:T(8,128)S(1)}, u32[]{:S(2)}, u32[]{:S(2)}) collective-permute-start(f32[16,128]{1,0:T(8,128)S(1)} %maximum_maximum_fusion.refs_0_), channel_id=1, source_target_pairs={{0,7},{1,0},{2,1},{3,2},{4,3},{5,4},{6,5},{7,6},{8,15},{9,8},{10,9... | collective-permute-start | bytes 24584 | tf_op jit(solution)/shard_map/ppermute | solution.py:498
  75.1 7.0 %collective-permute-start.2 = (f32[16,128]{1,0:T(8,128)S(1)}, f32[16,128]{1,0:T(8,128)S(1)}, u32[]{:S(2)}, u32[]{:S(2)}) collective-permute-start(f32[16,128]{1,0:T(8,128)S(1)} %maximum_maximum_fusion.refs_0_), channel_id=1, source_target_pairs={{0,5},{1,6},{2,7},{3,0},{4,1},{5,2},{6,3},{7,4},{8,13},{9,14},{10,... | collective-permute-start | bytes 24584 | tf_op jit(solution)/shard_map/ppermute | solution.py:498
  90.3 25.0 %collective-permute-start.39 = (bf16[320,640]{1,0:T(8,128)(2,1)}, bf16[320,640]{1,0:T(8,128)(2,1)}, u32[]{:S(2)}, u32[]{:S(2)}) collective-permute-start(bf16[320,640]{1,0:T(8,128)(2,1)} %get-tuple-element.58.a), channel_id=1, source_target_pairs={{0,16},{8,24},{16,32},{24,40},{32,48},{40,56},{48,0},{56,8},{64,80... | collective-permute-start | bytes 1228808 | tf_op jit(solution)/shard_map/ppermute | solution.py:307
  96.1 28.5 %collective-permute-start.41 = (bf16[320,640]{1,0:T(8,128)(2,1)}, bf16[320,640]{1,0:T(8,128)(2,1)}, u32[]{:S(2)}, u32[]{:S(2)}) collective-permute-start(bf16[320,640]{1,0:T(8,128)(2,1)} %get-tuple-element.58.a), channel_id=1, source_target_pairs={{0,48},{8,56},{16,0},{24,8},{32,16},{40,24},{48,32},{56,40},{64,11... | collective-permute-start | bytes 1228808 | tf_op jit(solution)/shard_map/ppermute | solution.py:307
  100.9 25.5 %collective-permute-start.34 = (bf16[320,640]{1,0:T(8,128)(2,1)}, bf16[320,640]{1,0:T(8,128)(2,1)}, u32[]{:S(2)}, u32[]{:S(2)}) collective-permute-start(bf16[320,640]{1,0:T(8,128)(2,1)} %collective-permute-done.33.mine), channel_id=1, source_target_pairs={{0,16},{8,24},{16,32},{24,40},{32,48},{40,56},{48,0},{56,8},{64,80... | collective-permute-start | bytes 1228808 | tf_op jit(solution)/shard_map/ppermute | solution.py:308
  104.1 35.5 %collective-permute-start.36 = (bf16[320,640]{1,0:T(8,128)(2,1)}, bf16[320,640]{1,0:T(8,128)(2,1)}, u32[]{:S(2)}, u32[]{:S(2)}) collective-permute-start(bf16[320,640]{1,0:T(8,128)(2,1)} %collective-permute-done.33.mine), channel_id=1, source_target_pairs={{0,48},{8,56},{16,0},{24,8},{32,16},{40,24},{48,32},{56,40},{64,11... | collective-permute-start | bytes 1228808 | tf_op jit(solution)/shard_map/ppermute | solution.py:308
  116.2 22.8 %collective-permute-start.40 = (bf16[160,640]{1,0:T(8,128)(2,1)S(1)}, bf16[160,640]{1,0:T(8,128)(2,1)S(1)}, u32[]{:S(2)}, u32[]{:S(2)}) collective-permute-start(bf16[160,640]{1,0:T(8,128)(2,1)S(1)} %slice.100), channel_id=1, source_target_pairs={{0,16},{8,24},{16,32},{24,40},{32,48},{40,56},{48,0},{56,8},{64,80... | collective-permute-start | bytes 614408 | tf_op jit(solution)/shard_map/ppermute | solution.py:314
  121.9 8.2 %collective-permute-start.16 = (f32[192,128]{1,0:T(8,128)S(1)}, f32[192,128]{1,0:T(8,128)S(1)}, u32[]{:S(2)}, u32[]{:S(2)}) collective-permute-start(f32[192,128]{1,0:T(8,128)S(1)} %token_sums.1.refs_0_), channel_id=1, source_target_pairs={{0,5},{1,6},{2,7},{3,0},{4,1},{5,2},{6,3},{7,4},{8,13},{9,14},{10,... | collective-permute-start | bytes 294920 | tf_op jit(solution)/shard_map/ppermute | solution.py:498
  124.5 14.5 %collective-permute-start.17 = (f32[192,128]{1,0:T(8,128)S(1)}, f32[192,128]{1,0:T(8,128)S(1)}, u32[]{:S(2)}, u32[]{:S(2)}) collective-permute-start(f32[192,128]{1,0:T(8,128)S(1)} %token_sums.1.refs_0_), channel_id=1, source_target_pairs={{0,4},{1,5},{2,6},{3,7},{4,0},{5,1},{6,2},{7,3},{8,12},{9,13},{10,... | collective-permute-start | bytes 294920 | tf_op jit(solution)/shard_map/ppermute | solution.py:498
  126.4 15.4 %collective-permute-start.42 = (bf16[160,640]{1,0:T(8,128)(2,1)S(1)}, bf16[160,640]{1,0:T(8,128)(2,1)S(1)}, u32[]{:S(2)}, u32[]{:S(2)}) collective-permute-start(bf16[160,640]{1,0:T(8,128)(2,1)S(1)} %slice.101), channel_id=1, source_target_pairs={{0,48},{8,56},{16,0},{24,8},{32,16},{40,24},{48,32},{56,40},{64,11... | collective-permute-start | bytes 614408 | tf_op jit(solution)/shard_map/ppermute | solution.py:314
  130.1 34.0 %collective-permute-start.49 = (bf16[320,640]{1,0:T(8,128)(2,1)}, bf16[320,640]{1,0:T(8,128)(2,1)}, u32[]{:S(2)}, u32[]{:S(2)}) collective-permute-start(bf16[320,640]{1,0:T(8,128)(2,1)} %get-tuple-element.58.a), channel_id=1, source_target_pairs={{0,8},{8,0},{16,24},{24,16},{32,40},{40,32},{48,56},{56,48},{64,72... | collective-permute-start | bytes 1228808 | tf_op jit(solution)/shard_map/ppermute | solution.py:320
  139.0 25.0 %collective-permute-start.48 = (bf16[320,640]{1,0:T(8,128)(2,1)}, bf16[320,640]{1,0:T(8,128)(2,1)}, u32[]{:S(2)}, u32[]{:S(2)}) collective-permute-start(bf16[320,640]{1,0:T(8,128)(2,1)} %collective-permute-done.33.mine), channel_id=1, source_target_pairs={{0,8},{8,0},{16,24},{24,16},{32,40},{40,32},{48,56},{56,48},{64,72... | collective-permute-start | bytes 1228808 | tf_op jit(solution)/shard_map/ppermute | solution.py:320
  139.1 25.5 %collective-permute-start.47 = (bf16[320,640]{1,0:T(8,128)(2,1)}, bf16[320,640]{1,0:T(8,128)(2,1)}, u32[]{:S(2)}, u32[]{:S(2)}) collective-permute-start(bf16[320,640]{1,0:T(8,128)(2,1)} %collective-permute-done.39.mine), channel_id=1, source_target_pairs={{0,8},{8,0},{16,24},{24,16},{32,40},{40,32},{48,56},{56,48},{64,72... | collective-permute-start | bytes 1228808 | tf_op jit(solution)/shard_map/ppermute | solution.py:320
  139.6 7.9 %collective-permute-start.35 = (bf16[160,640]{1,0:T(8,128)(2,1)S(1)}, bf16[160,640]{1,0:T(8,128)(2,1)S(1)}, u32[]{:S(2)}, u32[]{:S(2)}) collective-permute-start(bf16[160,640]{1,0:T(8,128)(2,1)S(1)} %slice.98), channel_id=1, source_target_pairs={{0,16},{8,24},{16,32},{24,40},{32,48},{40,56},{48,0},{56,8},{64,80... | collective-permute-start | bytes 614408 | tf_op jit(solution)/shard_map/ppermute | solution.py:314
  141.8 12.8 %collective-permute-start.37 = (bf16[160,640]{1,0:T(8,128)(2,1)S(1)}, bf16[160,640]{1,0:T(8,128)(2,1)S(1)}, u32[]{:S(2)}, u32[]{:S(2)}) collective-permute-start(bf16[160,640]{1,0:T(8,128)(2,1)S(1)} %slice.99), channel_id=1, source_target_pairs={{0,48},{8,56},{16,0},{24,8},{32,16},{40,24},{48,32},{56,40},{64,11... | collective-permute-start | bytes 614408 | tf_op jit(solution)/shard_map/ppermute | solution.py:314
  154.6 6.7 %collective-permute-start.20 = (f32[192,128]{1,0:T(8,128)S(1)}, f32[192,128]{1,0:T(8,128)S(1)}, u32[]{:S(2)}, u32[]{:S(2)}) collective-permute-start(f32[192,128]{1,0:T(8,128)S(1)} %token_sums.1.refs_0_), channel_id=1, source_target_pairs={{0,1},{1,2},{2,3},{3,4},{4,5},{5,6},{6,7},{7,0},{8,9},{9,10},{10,1... | collective-permute-start | bytes 294920 | tf_op jit(solution)/shard_map/ppermute | solution.py:498
  157.7 26.5 %collective-permute-start.46 = (bf16[320,640]{1,0:T(8,128)(2,1)}, bf16[320,640]{1,0:T(8,128)(2,1)}, u32[]{:S(2)}, u32[]{:S(2)}) collective-permute-start(bf16[320,640]{1,0:T(8,128)(2,1)} %collective-permute-done.41.mine), channel_id=1, source_target_pairs={{0,8},{8,0},{16,24},{24,16},{32,40},{40,32},{48,56},{56,48},{64,72... | collective-permute-start | bytes 1228808 | tf_op jit(solution)/shard_map/ppermute | solution.py:320
  161.3 27.4 %collective-permute-start.45 = (bf16[320,640]{1,0:T(8,128)(2,1)}, bf16[320,640]{1,0:T(8,128)(2,1)}, u32[]{:S(2)}, u32[]{:S(2)}) collective-permute-start(bf16[320,640]{1,0:T(8,128)(2,1)} %collective-permute-done.34.mine), channel_id=1, source_target_pairs={{0,8},{8,0},{16,24},{24,16},{32,40},{40,32},{48,56},{56,48},{64,72... | collective-permute-start | bytes 1228808 | tf_op jit(solution)/shard_map/ppermute | solution.py:320
  164.1 29.3 %collective-permute-start.44 = (bf16[320,640]{1,0:T(8,128)(2,1)}, bf16[320,640]{1,0:T(8,128)(2,1)}, u32[]{:S(2)}, u32[]{:S(2)}) collective-permute-start(bf16[320,640]{1,0:T(8,128)(2,1)} %collective-permute-done.36.mine), channel_id=1, source_target_pairs={{0,8},{8,0},{16,24},{24,16},{32,40},{40,32},{48,56},{56,48},{64,72... | collective-permute-start | bytes 1228808 | tf_op jit(solution)/shard_map/ppermute | solution.py:320
  164.1 33.9 %collective-permute-start.43 = (bf16[320,640]{1,0:T(8,128)(2,1)}, bf16[320,640]{1,0:T(8,128)(2,1)}, u32[]{:S(2)}, u32[]{:S(2)}) collective-permute-start(bf16[320,640]{1,0:T(8,128)(2,1)} %constant_dynamic-update-slice_fusion.2.mine), channel_id=1, source_target_pairs={{0,8},{8,0},{16,24},{24,16},{32,40},{40,32},{48,56},{56,48},{64,72... | collective-permute-start | bytes 1228808 | tf_op jit(solution)/shard_map/ppermute | solution.py:320
  164.6 38.0 %collective-permute-start.38 = (bf16[320,640]{1,0:T(8,128)(2,1)}, bf16[320,640]{1,0:T(8,128)(2,1)}, u32[]{:S(2)}, u32[]{:S(2)}) collective-permute-start(bf16[320,640]{1,0:T(8,128)(2,1)} %constant_dynamic-update-slice_fusion.mine), channel_id=1, source_target_pairs={{0,8},{8,0},{16,24},{24,16},{32,40},{40,32},{48,56},{56,48},{64,72... | collective-permute-start | bytes 1228808 | tf_op jit(solution)/shard_map/ppermute | solution.py:320
  (29 other events, 461.5 us)

commit v2 on v0

v2 whole, which is shorter than its diff:
```python
import functools
import math

import jax
import jax.numpy as jnp
from jax import lax
from jax.experimental import pallas as pl
from jax.experimental.pallas import tpu as pltpu
from jax.sharding import PartitionSpec as P

FREQ_DIM = 256
PATCH_DIM = 64
QBLOCK = 128
SAMPLE_TOKENS = 512

epsilon = 1e-06
inner_rate = 0.5
outer_rate = 0.7
momentum_decay = 0.9

f32 = jnp.float32
bf16 = jnp.bfloat16

N_Y, N_XH, N_CORE, N_FSDP = 4, 2, 2, 8
COL = 320
PAIR = 640
ROWS = 640
ROUND = 1.5 * 2.0**23
NUDGE = 1.0 + 2.0**-21

limit = pltpu.CompilerParams(vmem_limit_bytes=56 * 2**20)
brief = pl.CostEstimate(flops=1, bytes_accessed=1, transcendentals=0)
unread = pl.BlockSpec(memory_space=pl.ANY)

NT = (((1,), (1,)), ((), ()))
TN = (((0,), (0,)), ((), ()))
NN = (((1,), (0,)), ((), ()))


def dot(a, b, dims):
    return lax.dot_general(a, b, dims, preferred_element_type=f32)


def split2(x):
    hi = x.astype(bf16)
    return hi, (x - hi.astype(f32)).astype(bf16)


def quantized(delta):
    peak = jnp.max(jnp.abs(delta), axis=0, keepdims=True)
    scale = (peak + epsilon).astype(bf16).astype(f32)
    ratio = (7.0 / scale) * NUDGE
    shifted = delta * ratio + ROUND
    code = jnp.clip(shifted, ROUND - 7.0, ROUND + 7.0) - ROUND
    return code * (scale / 7.0)


def quant_kernel(pos_ref, start_ref, current_ref, keep, send):
    first_core = pos_ref[0] == 0
    low_lane = lax.broadcasted_iota(jnp.int32, (64, 128), 1) < 64
    for chip in range(N_Y * N_XH):
        dy = lax.rem(chip % N_Y - pos_ref[1] + N_Y, N_Y)
        dx = lax.rem(chip // N_Y - pos_ref[2] + N_XH, N_XH)
        slot = dy * N_XH + dx

        def terms(tile):
            lanes = slice(chip * PAIR + tile * 128, chip * PAIR + (tile + 1) * 128)
            return quantized(start_ref[:, lanes].astype(f32) - current_ref[:, lanes].astype(f32))

        def put(lane, low, high):
            keep[slot, :, lane : lane + 128] = jnp.where(first_core, low, high).astype(bf16)
            send[slot, :, lane : lane + 128] = jnp.where(first_core, high, low).astype(bf16)

        for tile in range(2):
            low, high = terms(tile), terms(tile + 3)
            put(tile * 128, low[:64], high[:64])
            put(256 + tile * 128, low[64:], high[64:])
        both = terms(2)
        top, bottom = both[:64], both[64:]
        low = jnp.where(low_lane, top, pltpu.roll(bottom, 64, 1))
        high = jnp.where(low_lane, pltpu.roll(top, 64, 1), bottom)
        put(512, low, high)


def quantize(pos, frag_start, frag_current):
    chips = N_Y * N_XH
    whole = pl.BlockSpec((QBLOCK, frag_start.shape[1]), lambda i, pos: (i, 0))
    made = pl.BlockSpec((chips, QBLOCK // 2, PAIR), lambda i, pos: (0, i, 0))
    keep, sent = pl.pallas_call(
        quant_kernel,
        grid_spec=pltpu.PrefetchScalarGridSpec(
            num_scalar_prefetch=1,
            grid=(ROWS // QBLOCK,),
            in_specs=[whole, whole],
            out_specs=[made, made],
        ),
        out_shape=[jax.ShapeDtypeStruct((chips, ROWS // 2, PAIR), bf16)] * 2,
        compiler_params=limit,
        cost_estimate=brief,
        name="quantize",
    )(pos, frag_start, frag_current)
    return keep.reshape(N_Y, N_XH, ROWS // 2, PAIR), sent.reshape(N_Y, N_XH, ROWS // 2, PAIR)


def outer_kernel(pos_ref, own_ref, far_ref, anchor_ref, momentum_ref, unread_ref, new_anchor, new_momentum, params, native, fresh):
    low_lane = lax.broadcasted_iota(jnp.int32, (64, 128), 1) < 64
    first_core = pos_ref[0] == 0
    for block in range(ROWS // QBLOCK):
        message = slice(block * 64, block * 64 + 64)
        total = own_ref[message].astype(f32) + far_ref[message].astype(f32)
        rest = total[:, 512:640]
        for half, tail in ((0, rest), (1, pltpu.roll(rest, 64, 1))):
            rows = slice(block * 128 + half * 64, block * 128 + half * 64 + 64)
            main0 = total[:, half * 256 : half * 256 + 128]
            main1 = total[:, half * 256 + 128 : half * 256 + 256]
            turn0, turn1 = pltpu.roll(main0, 64, 1), pltpu.roll(main1, 64, 1)
            native[rows, 0:128] = jnp.where(first_core, main0, jnp.where(low_lane, tail, turn0))
            native[rows, 128:256] = jnp.where(first_core, main1, jnp.where(low_lane, turn0, turn1))
            native[rows, 256:384] = jnp.where(first_core, tail, turn1)
        rows = slice(block * 128, block * 128 + 128)
        average = native[rows, 0:COL] / float(N_Y * N_XH * N_CORE)
        momentum = momentum_decay * momentum_ref[rows] + average
        anchor = anchor_ref[rows] - outer_rate * (average + momentum_decay * momentum)
        new_momentum[rows] = momentum
        new_anchor[rows] = anchor
        fresh[rows, 0:COL] = anchor
        for half in range(2):
            rows = slice(block * 128 + half * 64, block * 128 + half * 64 + 64)
            tiles = [fresh[rows, t * 128 : t * 128 + 128] for t in range(3)]
            turn = [pltpu.roll(tile, 64, 1) for tile in tiles]
            for t in range(2):
                value = jnp.where(first_core, tiles[t], jnp.where(low_lane, turn[t], turn[t + 1]))
                at = half * 256 + t * 128
                params[message, at : at + 128] = value.astype(bf16)
            if half == 0:
                top = jnp.where(first_core, tiles[2], tiles[0])
            else:
                bottom = jnp.where(first_core, turn[2], turn[0])
        params[message, 512:640] = jnp.where(low_lane, top, bottom).astype(bf16)


def outer_update(pos, own, far, anchor, momentum, after):
    held = pl.BlockSpec(memory_space=pltpu.VMEM)
    return pl.pallas_call(
        outer_kernel,
        in_specs=[pl.BlockSpec(memory_space=pltpu.SMEM)] + [held] * 4 + [unread],
        out_specs=[held] * 3,
        scratch_shapes=[pltpu.VMEM((ROWS, 384), f32), pltpu.VMEM((ROWS, 384), f32)],
        out_shape=[
            jax.ShapeDtypeStruct((ROWS, COL), f32),
            jax.ShapeDtypeStruct((ROWS, COL), f32),
            jax.ShapeDtypeStruct((ROWS // 2, PAIR), bf16),
        ],
        compiler_params=limit,
        cost_estimate=brief,
        name="outer_update",
    )(pos, own, far, anchor, momentum, after)


def place_kernel(chips, after, pos_ref, *refs):
    out = refs[-1]
    count = sum(pieces for _, _, pieces in chips)
    mine, theirs = refs[:count], refs[count : 2 * count]
    first_core = pos_ref[0] == 0
    step = pl.program_id(0)
    early = step < pl.num_programs(0) // 2
    size = mine[0].shape[0]
    at = pl.multiple_of(lax.rem(step, 64 // size) * size, size)
    low_lane = lax.broadcasted_iota(jnp.int32, (size, 128), 1) < 64
    index = 0
    for dy, dx, pieces in chips:
        a, b = mine[index][...], theirs[index][...]
        if pieces == 2:
            a = jnp.where(early, a, mine[index + 1][...])
            b = jnp.where(early, b, theirs[index + 1][...])
        index += pieces
        low, high = jnp.where(first_core, a, b), jnp.where(first_core, b, a)
        chip = lax.rem(pos_ref[2] + dx, N_XH) * N_Y + lax.rem(pos_ref[1] + dy, N_Y)

        def put(half, lane, value):
            lanes = pl.ds(pl.multiple_of(chip * PAIR + lane, 128), value.shape[1])
            out[pl.ds(at + half * 64, size), lanes] = value

        for half in range(2):
            put(half, 0, low[:, half * 256 : half * 256 + 256])
            put(half, 384, high[:, half * 256 : half * 256 + 256])
        low_rest, high_rest = low[:, 512:640].astype(f32), high[:, 512:640].astype(f32)
        put(0, 256, jnp.where(low_lane, low_rest, pltpu.roll(high_rest, 64, 1)).astype(bf16))
        put(1, 256, jnp.where(low_lane, pltpu.roll(low_rest, 64, 1), high_rest).astype(bf16))


def place(pos, chips, mine, theirs, after):
    size = 32
    steps = ROWS // 2 // size

    def block(piece, pieces):
        if pieces == 1:
            return pl.BlockSpec((size, PAIR), lambda i, pos: (i, 0))
        if piece == 0:
            return pl.BlockSpec((size, PAIR), lambda i, pos: (jnp.minimum(i, steps // 2 - 1), 0))
        return pl.BlockSpec((size, PAIR), lambda i, pos: (jnp.maximum(i - steps // 2, 0), 0))

    blocks = [block(piece, pieces) for _, _, pieces in chips for piece in range(pieces)]
    return pl.pallas_call(
        functools.partial(place_kernel, chips, len(after)),
        grid_spec=pltpu.PrefetchScalarGridSpec(
            num_scalar_prefetch=1,
            grid=(steps,),
            in_specs=blocks * 2 + [unread] * len(after),
            out_specs=pl.BlockSpec((QBLOCK, N_Y * N_XH * PAIR), lambda i, pos: (i // (64 // size), 0)),
        ),
        out_shape=jax.ShapeDtypeStruct((ROWS, N_Y * N_XH * PAIR), bf16),
        compiler_params=limit,
        cost_estimate=brief,
        name="place",
    )(pos, *mine, *theirs, *after)


def halves_kernel(after, below, above, *refs):
    first, second = refs[after:]
    first[...] = below[...]
    second[...] = above[...]


def halves(below, above, after):
    rows, columns = below.shape
    shape = jax.ShapeDtypeStruct((rows // 2, columns), below.dtype)
    part = [pl.BlockSpec((rows // 2, columns), lambda i, j=j: (j, 0)) for j in range(2)]
    return pl.pallas_call(
        functools.partial(halves_kernel, len(after)),
        grid=(1,),
        in_specs=part + [unread] * len(after),
        out_specs=[part[0], part[0]],
        out_shape=[shape, shape],
        compiler_params=limit,
        cost_estimate=brief,
        name="halves",
    )(below, above, *after)


def join_kernel(after, *refs):
    parts, out = refs[: -1 - after], refs[-1]
    at = 0
    for part in parts:
        out[at : at + part.shape[0]] = part[...]
        at += part.shape[0]


def join(parts, after):
    count = sum(part.shape[0] for part in parts)
    return pl.pallas_call(
        functools.partial(join_kernel, len(after)),
        in_specs=[pl.BlockSpec(memory_space=pltpu.VMEM)] * len(parts) + [unread] * len(after),
        out_shape=jax.ShapeDtypeStruct((count,) + parts[0].shape[1:], f32),
        compiler_params=limit,
        cost_estimate=brief,
        name="join",
    )(*parts, *after)


def settle_kernel(a, b, a_out, b_out, token):
    del a, b, a_out, b_out
    token[...] = jnp.zeros_like(token)


def settle(a, b):
    return pl.pallas_call(
        settle_kernel,
        in_specs=[unread] * 2,
        out_specs=[unread] * 2 + [pl.BlockSpec(memory_space=pltpu.VMEM)],
        out_shape=[jax.ShapeDtypeStruct(x.shape, x.dtype) for x in (a, b)] + [jax.ShapeDtypeStruct((8, 128), f32)],
        input_output_aliases={0: 0, 1: 1},
        cost_estimate=brief,
        name="settle",
    )(a, b)


def gate_kernel(*refs):
    del refs


def gate(arrays, after):
    count = len(arrays)
    return pl.pallas_call(
        gate_kernel,
        in_specs=[unread] * (count + len(after)),
        out_specs=[unread] * count,
        out_shape=[jax.ShapeDtypeStruct(a.shape, a.dtype) for a in arrays],
        input_output_aliases={i: i for i in range(count)},
        cost_estimate=brief,
        name="gate",
    )(*arrays, *after)


def total(*refs):
    return sum(ref.astype(f32) for ref in refs)


def spot(dy, x, rows, columns, part=0):
    return pl.BlockSpec((1, 1, rows, columns), lambda i: (dy, x, part, 0))


def first_kernel(keep1, got1, keep2, got2, keep3, got3, up, down):
    half = up.shape[1]
    low, high = slice(0, half), slice(half, 2 * half)
    up[0] = total(keep2[0, 0, low], got2[0, 0, low]).astype(bf16)
    down[0] = total(keep2[0, 0, high], got2[0, 0, high]).astype(bf16)
    up[1] = total(keep1[0, 0], got1[0, 0]).astype(bf16)
    down[1] = total(keep3[0, 0], got3[0, 0]).astype(bf16)


def first_messages(keep, got, x, after):
    _, _, rows, columns = keep.shape
    half = rows // 2
    part = pl.BlockSpec((2, half, columns), lambda i: (0, 0, 0))
    shape = jax.ShapeDtypeStruct((2, half, columns), bf16)

    def kernel(*refs):
        first_kernel(*refs[:6], *refs[6 + len(after) :])

    return pl.pallas_call(
        kernel,
        grid=(1,),
        in_specs=[spot(1, x, half, columns, 1)] * 2
        + [spot(2, x, rows, columns)] * 2
        + [spot(3, x, half, columns, 0)] * 2
        + [unread] * len(after),
        out_specs=[part] * 2,
        out_shape=[shape] * 2,
        compiler_params=limit,
        cost_estimate=brief,
        name="first_messages",
    )(keep, got, keep, got, keep, got, *after)


def second_kernel(keep1, got1, keep3, got3, up, down, up_out, down_out):
    up_out[...] = total(keep1[0, 0], got1[0, 0], up[0]).astype(bf16)
    down_out[...] = total(keep3[0, 0], got3[0, 0], down[0]).astype(bf16)


def second_messages(keep, got, up, down, x):
    _, _, rows, columns = keep.shape
    half = rows // 2
    came = pl.BlockSpec((1, half, columns), lambda i: (0, 0, 0))
    part = pl.BlockSpec((half, columns), lambda i: (0, 0))
    shape = jax.ShapeDtypeStruct((half, columns), bf16)
    return pl.pallas_call(
        second_kernel,
        grid=(1,),
        in_specs=[spot(1, x, half, columns, 0)] * 2 + [spot(3, x, half, columns, 1)] * 2 + [came] * 2,
        out_specs=[part] * 2,
        out_shape=[shape] * 2,
        compiler_params=limit,
        cost_estimate=brief,
        name="second_messages",
    )(keep, got, keep, got, up, down)


def chip_kernel(keep, got, up, down, up2, down2, out):
    half = up.shape[1]
    low, high = slice(0, half), slice(half, 2 * half)
    out[low] = total(keep[0, 0, low], got[0, 0, low], down[0], up2[...]).astype(out.dtype)
    out[high] = total(keep[0, 0, high], got[0, 0, high], up[0], down2[...]).astype(out.dtype)


def chip_sum(keep, got, up, down, up2, down2, x, dtype):
    _, _, rows, columns = keep.shape
    came = pl.BlockSpec((1, rows // 2, columns), lambda i: (1, 0, 0))
    part = pl.BlockSpec((rows // 2, columns), lambda i: (0, 0))
    return pl.pallas_call(
        chip_kernel,
        grid=(1,),
        in_specs=[spot(0, x, rows, columns)] * 2 + [came] * 2 + [part] * 2,
        out_specs=pl.BlockSpec((rows, columns), lambda i: (0, 0)),
        out_shape=jax.ShapeDtypeStruct((rows, columns), dtype),
        compiler_params=limit,
        cost_estimate=brief,
        name="chip_sum",
    )(keep, got, up, down, up2, down2)


def per_device(
    latents,
    target,
    timesteps,
    patch_weight,
    head_weight,
    modulation,
    time_weight,
    anchor,
    momentum,
    frag_start,
    frag_current,
):
    frag_current = frag_current[0]
    params = (patch_weight[0], head_weight[0], modulation[0], time_weight[0])
    columns = params[0].shape[1]
    width = float(columns * N_FSDP)
    tokens = float(latents.shape[0] * N_FSDP)
    replica = lax.axis_index("replica")
    pos = jnp.stack([replica % 2, (replica // 2) % 4, replica // 8]).astype(jnp.int32)

    to_core = [(r, r ^ 1) for r in range(16)]
    to_x = [(r, r ^ 8) for r in range(16)]

    def to_y(step):
        return [
            (xh * 8 + y * 2 + c, xh * 8 + ((y + step) % N_Y) * 2 + c)
            for xh in range(N_XH)
            for y in range(N_Y)
            for c in range(N_CORE)
        ]

    send = functools.partial(lax.ppermute, axis_name="replica")
    to_sibling = functools.partial(send, perm=to_core)

    def across(value, bit):
        return lax.ppermute(value, "fsdp", [(i, i ^ bit) for i in range(N_FSDP)])

    h0 = step_head(timesteps, params[0])[None]
    h1 = across(h0, 1)
    keep, sent = quantize(pos, frag_start, frag_current)
    got = to_sibling(sent)
    h01 = join([h0, h1], [keep])
    h2 = across(h01, 2)
    up, down = [None, None], [None, None]

    def ring(x, messages):
        up[x], down[x] = send(messages[0], perm=to_y(1)), send(messages[1], perm=to_y(-1))

    message = first_messages(keep, got, 1, [])
    ring(1, message)
    h03 = join([h01, h2], [message[0]])
    h4 = across(h03, 4)
    near, away, pre, center, sines = weight_products(h03, h4, *params, [message[0]], width)
    away = across(away, 4)
    away2 = across(near[2:4] + away[2:4], 2)
    away1 = across(near[1:2] + away[1:2] + away2[1:2], 1)

    far = second_messages(keep, got, up[1], down[1], 1)
    far_up, far_down = send(far[0], perm=to_y(1)), send(far[1], perm=to_y(-1))
    ring(0, first_messages(keep, got, 0, [far[0]]))
    far = send(chip_sum(keep, got, up[1], down[1], far_up, far_down, 1, bf16), perm=to_x)
    own = second_messages(keep, got, up[0], down[0], 0)
    own_up, own_down = send(own[0], perm=to_y(1)), send(own[1], perm=to_y(-1))
    q0 = token_sums(near[0:1] + away[0:1] + away2[0:1], away1, latents.T, target.T, [anchor, momentum], width, tokens)
    q1 = across(q0, 1)
    own = chip_sum(keep, got, up[0], down[0], own_up, own_down, 0, f32)
    new_anchor, new_momentum, n0 = outer_update(pos, own, far, anchor, momentum, q0)

    n1 = send(n0, perm=to_x)
    up0, down0 = send(n0, perm=to_y(1)), send(n0, perm=to_y(-1))
    q01 = join([q0, q1], [])
    q2 = across(q01, 2)
    anchor_t, momentum_t, settled = settle(new_anchor.T, new_momentum.T)
    q4 = across(join([q01, q2], []), 4)
    first0 = halves(up0, down0, [])
    on0 = send(first0[0], perm=to_y(1)), send(first0[1], perm=to_y(-1))
    up1, down1 = send(n1, perm=to_y(1)), send(n1, perm=to_y(-1))
    inner = finish(q0, q1, q2, q4, pre, center, sines, params, [])
    first1 = halves(up1, down1, [])
    on1 = send(first1[0], perm=to_y(1)), send(first1[1], perm=to_y(-1))
    mine = [n0, up0, down0, n1, up1, down1, *on0]
    mine = gate(mine, [first1[0], inner[2], settled])
    mine = [*mine, *on1]
    theirs = [to_sibling(part) for part in mine]
    chips = ((0, 0, 1), (3, 0, 1), (1, 0, 1), (0, 1, 1), (3, 1, 1), (1, 1, 1), (2, 0, 2), (2, 1, 2))
    new_params = place(pos, chips, mine, theirs, [inner[2], settled])
    return tuple(a[None] for a in inner) + (anchor_t.T, momentum_t.T, new_params)


def column(row):
    eye = lax.broadcasted_iota(jnp.int32, (64, 128), 0) == lax.broadcasted_iota(jnp.int32, (64, 128), 1)
    return jnp.sum(jnp.where(eye, row, 0.0), axis=1, keepdims=True)


def gains(pre, mod_ref):
    embed = pre * jax.nn.sigmoid(pre)
    mod = mod_ref[...].astype(bf16).astype(f32)
    return 1.0 + mod[1:2] + embed, mod[0:1] + embed


def weights_kernel(width, after, near_heads, away_heads, patch_ref, head_ref, mod_ref, time_ref, *refs):
    near, away, pre_ref, center_ref, sines_ref, high, low = refs[after:]
    count = N_FSDP
    total = jnp.zeros((1, 128), f32)
    for k in range(count):
        head = (near_heads if k < count // 2 else away_heads)[k % (count // 2)]
        total = total + head[8:9]
        sines_ref[4 * k : 4 * k + 4, 0:128] = head[0:4]
        sines_ref[4 * k : 4 * k + 4, 128:256] = head[4:8]
    pre = dot(sines_ref[...].astype(bf16), time_ref[...].astype(bf16), NN)
    pre_ref[...] = pre
    gain, shift = gains(pre, mod_ref)
    center = patch_ref[...].astype(bf16).astype(f32) - column(total / width)
    center_ref[...] = center
    samples = 4 * count
    for s in range(samples):
        k, i = s // 4, s % 4
        at = (i // 2) * (samples // 2 * 64) + (2 * k + i % 2) * 64
        hi, lo = split2(center * gain[s : s + 1])
        high[at : at + 64, :] = hi
        low[at : at + 64, :] = lo
    head = head_ref[...].astype(bf16)
    blank = jnp.zeros_like(head)
    left = jnp.concatenate([head, blank], axis=0)
    right = jnp.concatenate([blank, head], axis=0)
    part = samples // 2 * 64
    packed = dot(high[0:part], left, NT) + dot(low[0:part], left, NT)
    packed = packed + dot(high[part:], right, NT) + dot(low[part:], right, NT)
    chi, clo = split2(center)
    chi_left = jnp.concatenate([chi, blank], axis=0)
    clo_left = jnp.concatenate([clo, blank], axis=0)
    gram = dot(chi, chi_left, NT) + dot(clo, chi_left, NT) + dot(chi, clo_left, NT)
    for k in range(count):
        out = near if k < count // 2 else away
        slot = k % (count // 2)
        rows = jnp.concatenate([shift[4 * k : 4 * k + 4], gain[4 * k : 4 * k + 4]], axis=0)
        hi, lo = split2(rows)
        extra = dot(hi, right, NT) + dot(lo, right, NT)
        out[slot, 0:128, :] = packed[128 * k : 128 * k + 128]
        out[slot, 128:136, :] = gram[0:8] + extra
        out[slot, 136:192, :] = gram[8:64]


def row(column):
    eye = lax.broadcasted_iota(jnp.int32, (64, 128), 0) == lax.broadcasted_iota(jnp.int32, (64, 128), 1)
    return jnp.sum(jnp.where(eye, column, 0.0), axis=0, keepdims=True)


def tokens_kernel(width, tokens, after, own_ref, away_ref, latent_ref, target_ref, *refs):
    out, wide = refs[after:]
    total = own_ref[0] + away_ref[0]
    turned = pltpu.roll(total, 64, 1)
    gram = total[128:192, 0:64] / width
    g0 = gram.astype(bf16)
    g1, g2 = split2(gram - g0.astype(f32))
    gain_means = turned[132:136, :] / width
    wide[...] = jnp.zeros_like(wide)
    curve = jnp.zeros((64, 64), f32)
    sums = []
    for s in range(4):
        at = slice(s * SAMPLE_TOKENS, (s + 1) * SAMPLE_TOKENS)
        latent = latent_ref[:, at]
        latent_f = latent.astype(f32)
        mix = (total if s < 2 else turned)[(s % 2) * 64 : (s % 2) * 64 + 64, 0:64]
        mix_hi, mix_lo = split2(mix)
        spread = dot(g0, latent, NN) + dot(g1, latent, NN) + dot(g2, latent, NN)
        variance = jnp.sum(spread * latent_f, axis=0, keepdims=True)
        inv_std = lax.rsqrt(jnp.maximum(variance, 0.0) + epsilon)
        varied = inv_std * (dot(mix_hi, latent, TN) + dot(mix_lo, latent, TN))
        output = varied + column(turned[128 + s : 129 + s, :])
        grad_out = (2.0 * (output - target_ref[:, at].astype(f32)) / tokens).astype(bf16)
        grad_f = grad_out.astype(f32)
        along = jnp.sum(grad_f * varied, axis=0, keepdims=True) / width
        cross = dot((grad_f * inv_std).astype(bf16), latent, NT)
        curve = curve + dot((latent_f * (along * inv_std * inv_std)).astype(bf16), latent, NT)
        sums.append(row(jnp.sum(grad_f, axis=1, keepdims=True)))
        if s < 2:
            out[0, s * 64 : s * 64 + 64, 0:64] = cross
        else:
            wide[(s - 2) * 64 : (s - 2) * 64 + 64, 0:64] = cross
    for s in range(4):
        wide[128 + s : 129 + s, :] = sums[s]
    wide[132:136, 0:64] = gain_means[:, 0:64]
    packed = pltpu.roll(wide[...], 64, 1)
    low_lane = lax.broadcasted_iota(jnp.int32, (128, 128), 1) < 64
    out[0, 0:128, :] = jnp.where(low_lane, out[0, 0:128, :], packed[0:128])
    wide[128:192, 0:64] = curve
    out[0, 128:192, :] = jnp.where(low_lane[0:64], wide[128:192, :], packed[128:192])


def finish_kernel(
    after,
    parts0,
    parts1,
    parts2,
    parts4,
    pre_ref,
    center_ref,
    sines_ref,
    patch_ref,
    head_ref,
    mod_ref,
    time_ref,
    *refs,
):
    patch_new, head_new, mod_new, time_new, sums, slope_rows = refs[after:]
    count = N_FSDP
    parts = [ref[i] for ref in (parts0, parts1, parts2, parts4) for i in range(ref.shape[0])]
    pre = pre_ref[...]
    gain, shift = gains(pre, mod_ref)
    head = head_ref[...].astype(bf16)
    head_f = head.astype(f32)
    center = center_ref[...]
    chi, clo = split2(center)
    curve = parts[0][128:192, 0:64]
    for k in range(1, count):
        curve = curve + parts[k][128:192, 0:64]
    curve_hi, curve_lo = split2(curve)
    grad_patch = -(dot(curve_hi, chi, NN) + dot(curve_lo, chi, NN) + dot(curve_hi, clo, NN))
    grad_head = jnp.zeros_like(center)
    grad_scale = jnp.zeros_like(gain[0:1])
    for k in range(count):
        plain = parts[k]
        turned = pltpu.roll(plain, 64, 1)
        sums[4 * k : 4 * k + 4, :] = turned[128:132]
        crosses, fine = split2(jnp.concatenate([plain[0:128, 0:64], turned[0:128, 0:64]], axis=0))
        mixed = dot(crosses, chi, NN) + dot(fine, chi, NN) + dot(crosses, clo, NN)
        pulls = []
        for i in range(4):
            s = 4 * k + i
            one = mixed[i * 64 : i * 64 + 64]
            grad_head = grad_head + one * gain[s : s + 1]
            slope = jnp.sum(head_f * one, axis=0, keepdims=True)
            slope_rows[s : s + 1, :] = slope
            grad_scale = grad_scale + slope
            pulls.append((head_f * gain[s : s + 1] - column(turned[132 + i : 133 + i])).astype(bf16))
        grad_patch = grad_patch + dot(crosses, jnp.concatenate(pulls, axis=0), TN)
    sum_hi, sum_lo = split2(sums[:, 0:64])
    shift_hi, shift_lo = split2(shift)
    grad_head = grad_head + dot(sum_hi, shift_hi, TN) + dot(sum_lo, shift_hi, TN) + dot(sum_hi, shift_lo, TN)
    mixed_sums = dot(sum_hi, head, NN) + dot(sum_lo, head, NN)
    grad_shift = jnp.sum(mixed_sums, axis=0, keepdims=True)
    grad_embed = mixed_sums + slope_rows[...]
    sigmoid = jax.nn.sigmoid(pre)
    grad_pre = (grad_embed * (sigmoid * (1.0 + pre * (1.0 - sigmoid)))).astype(bf16)
    grad_time = dot(sines_ref[...].astype(bf16), grad_pre, TN)
    patch_new[...] = patch_ref[...] - inner_rate * grad_patch
    head_new[...] = head_ref[...] - inner_rate * grad_head
    mod_new[0:1, :] = mod_ref[0:1, :] - inner_rate * grad_shift
    mod_new[1:2, :] = mod_ref[1:2, :] - inner_rate * grad_scale
    time_new[...] = time_ref[...] - inner_rate * grad_time


def sinusoid(time_steps):
    index = jnp.arange(FREQ_DIM // 2, dtype=f32)
    frequency = jnp.exp(-math.log(10000.0) * index / (FREQ_DIM // 2))
    angles = time_steps.astype(f32)[:, None] * frequency[None, :]
    return jnp.cos(angles), jnp.sin(angles)


def step_head(timesteps, patch):
    cos, sin = sinusoid(timesteps)
    row_sums = jnp.sum(patch.astype(bf16).astype(f32), axis=1)
    return jnp.concatenate(
        [cos, sin, jnp.pad(row_sums, (0, 128 - PATCH_DIM))[None], jnp.zeros((7, 128), f32)], axis=0
    )


def weight_products(near, away, patch, head, mod, time, after, width):
    columns = patch.shape[1]
    samples = 4 * N_FSDP
    share = jax.ShapeDtypeStruct((N_FSDP // 2, 192, 128), f32)
    return pl.pallas_call(
        functools.partial(weights_kernel, width, len(after)),
        in_specs=[pl.BlockSpec(memory_space=pltpu.VMEM)] * 6 + [unread] * len(after),
        out_shape=[
            share,
            share,
            jax.ShapeDtypeStruct((samples, columns), f32),
            jax.ShapeDtypeStruct((PATCH_DIM, columns), f32),
            jax.ShapeDtypeStruct((samples, FREQ_DIM), f32),
        ],
        scratch_shapes=[pltpu.VMEM((samples * PATCH_DIM, columns), bf16)] * 2,
        compiler_params=limit,
        cost_estimate=brief,
        name="weight_products",
    )(near, away, patch, head, mod, time, *after)


def token_sums(own, away, latents, target, after, width, tokens):
    return pl.pallas_call(
        functools.partial(tokens_kernel, width, tokens, len(after)),
        in_specs=[pl.BlockSpec(memory_space=pltpu.VMEM)] * 4 + [unread] * len(after),
        out_shape=jax.ShapeDtypeStruct((1, 192, 128), f32),
        scratch_shapes=[pltpu.VMEM((192, 128), f32)],
        compiler_params=limit,
        cost_estimate=brief,
        name="token_sums",
    )(own, away, latents, target, *after)


def finish(q0, q1, q2, q4, pre, center, sines, params, after):
    samples, columns = pre.shape
    return pl.pallas_call(
        functools.partial(finish_kernel, len(after)),
        in_specs=[pl.BlockSpec(memory_space=pltpu.VMEM)] * 11 + [unread] * len(after),
        out_shape=[jax.ShapeDtypeStruct(a.shape, f32) for a in params],
        scratch_shapes=[pltpu.VMEM((samples, 128), f32), pltpu.VMEM((samples, columns), f32)],
        compiler_params=limit,
        cost_estimate=brief,
        name="finish",
    )(q0, q1, q2, q4, pre, center, sines, *params, *after)


def solution(mesh):
    in_specs = (
        P(("replica", "fsdp"), None),
        P(("replica", "fsdp"), None),
        P(("replica", "fsdp")),
        P("replica", None, "fsdp"),
        P("replica", None, "fsdp"),
        P("replica", None, "fsdp"),
        P("replica", None, "fsdp"),
        P("fsdp", "replica"),
        P("fsdp", "replica"),
        P("fsdp", None),
        P("replica", "fsdp", None),
    )
    out_specs = (
        P("replica", None, "fsdp"),
        P("replica", None, "fsdp"),
        P("replica", None, "fsdp"),
        P("replica", None, "fsdp"),
        P("fsdp", "replica"),
        P("fsdp", "replica"),
        P("fsdp", None),
    )
    return jax.shard_map(
        per_device, mesh=mesh, in_specs=in_specs, out_specs=out_specs, check_vma=False
    )
```

time: 521 us -> 156 us (0.30)
  waiting for transfers between devices: 224 us -> 17.7 us
  matrix products: 78.1 us -> 0 us
  blocking collectives: 75.7 us -> 0 us
  other arithmetic: 77.2 us -> 1.62 us
  Pallas kernels: 0 us -> 63.5 us
  starting transfers between devices: 0.3 us -> 46.9 us
  local copies, waits for them, and re-layouts: 47.5 us -> 24.1 us
  between operations: 15.8 us -> 1.06 us
    unnamed x12 -> x0, waiting for transfers between devices: 158 us -> none
    dot_general x22 -> x0, matrix products: 78.1 us -> none  [the longest x4 20.6 us: visit_block(): lax.dot_general(latent_blk, grad_hidden, (((0,), (0,)), ((), ())), prefer...]
    all_gather x3 -> x0, blocking collectives: 75.7 us -> none  [the longest x1 26.9 us: per_device(): lax.all_gather(head_local, 'fsdp', axis=1, tiled=True)]
    all_gather x2 -> x0, waiting for transfers between devices: 65.9 us -> none  [the longest x1 65.9 us: per_device(): lax.all_gather(new_anchor.astype(jnp.bfloat16), 'replica', axis=1, tiled=...]
    pallas_call x0 -> x20, Pallas kernels: none -> 63.5 us  [the longest x1 11.7 us: quantize(): pl.pallas_call(quant_kernel, grid_spec=pltpu.PrefetchScalarGridSpec(num_s...]
    ppermute x0 -> x38, starting transfers between devices: none -> 46.9 us  [the longest x10 14.6 us: per_device(): theirs = [to_sibling(part) for part in mine]]
    convert_element_type x15 -> x1, other arithmetic: 44.5 us -> 0.01 us  [sinusoid(): angles = time_steps.astype(f32)[:, None] * frequency[None, :]]
    unnamed x40 -> x88, local copies, waits for them, and re-layouts: 38.3 us -> 19.2 us
  transfers between devices with their start and end apart: 7 -> 38, of which waited for: 5 -> 13; matrix products, arithmetic and copies ran while one was open for 37% -> 5% of each run, Pallas kernels for 0% -> 24%
where the time goes in v2:
time: 156 us; the launch traced here: 155 us
  Pallas kernels  63.5 us (41%)
  starting transfers between devices  46.9 us (30%)
  local copies, waits for them, and re-layouts  24.1 us (15%)
  waiting for transfers between devices  17.7 us (11%)
  other arithmetic  1.62 us (1%)
    unnamed x88, local copies, waits for them, and re-layouts  19.2 us
    ppermute x10, starting transfers between devices, per_device(): theirs = [to_sibling(part) for part in mine]  14.6 us
    pallas_call x1, Pallas kernels, quantize(): pl.pallas_call(quant_kernel, grid_spec=pltpu.PrefetchScalarGridSpec(num_s...  11.7 us
    pallas_call x1, Pallas kernels, place(): pl.pallas_call(functools.partial(place_kernel, chips, len(after)), grid_s...  10 us
    ppermute x9, starting transfers between devices, across(): return lax.ppermute(value, 'fsdp', [(i, i ^ bit) for i in range(N_FSDP)])  9.37 us
    ppermute x9, waiting for transfers between devices, across(): return lax.ppermute(value, 'fsdp', [(i, i ^ bit) for i in range(N_FSDP)])  6.95 us
    pallas_call x4, Pallas kernels, join(): pl.pallas_call(functools.partial(join_kernel, len(after)), in_specs=[pl.B...  6.09 us
    ppermute x2, waiting for transfers between devices, ring(): send(messages[0], perm=to_y(1))  5.93 us
  transfers between devices with their start and end apart: 38, of which 13 were waited for; matrix products, arithmetic and copies ran while one was open for 5% of the time, Pallas kernels for 24%

profile of v2, /device:TPU:1, one launch (start us, length us, event | category | flops | bytes accessed | tf_op | source)
XLA Modules:
  0.0 154.8 jit_solution(8076671905839277151)
XLA Ops:
  1.3 11.7 %quantize.1 = (bf16[8,320,640]{2,1,0:T(8,128)(2,1)}, bf16[8,320,640]{2,1,0:T(8,128)(2,1)}) custom-call(s32[3]{0:T(128)} %pad_add_fusion.pos_ref, bf16[640,5120]{1,0:T(8,128)(2,1)} %start_ref.1, bf16[640,5120]{1,0:T(8,128)(2,1)} %bitcast.38), custom_call_target="tpu_custom_call" | custom-call | flops 1 | bytes 1 | tf_op jit(solution)/shard_map/quantize/pallas_call | solution.py:89
  14.8 1.8 %collective-permute-start = (f32[1,16,128]{2,1,0:T(8,128)S(1)}, f32[1,16,128]{2,1,0:T(8,128)S(1)}, u32[]{:S(2)}, u32[]{:S(2)}) collective-permute-start(f32[1,16,128]{2,1,0:T(8,128)S(1)} %maximum_bitcast_fusion.refs_0_), channel_id=1, source_target_pairs={{0,1},{1,0},{2,3},{3,2},{4,5},{5,4},{6,7},{7,6},{8,9},{9,8},{10,11... | collective-permute-start | bytes 24584 | tf_op jit(solution)/shard_map/ppermute | solution.py:418
  19.5 3.4 %collective-permute-start.1 = (f32[2,16,128]{2,1,0:T(8,128)}, f32[2,16,128]{2,1,0:T(8,128)S(1)}, u32[]{:S(2)}, u32[]{:S(2)}) collective-permute-start(f32[2,16,128]{2,1,0:T(8,128)} %join.4.refs_0_), channel_id=1, source_target_pairs={{0,2},{1,3},{2,0},{3,1},{4,6},{5,7},{6,4},{7,5},{8,10},{9,11},{10,... | collective-permute-start | bytes 49160 | tf_op jit(solution)/shard_map/ppermute | solution.py:418
  23.0 1.7 %copy-done = bf16[4,2,320,640]{3,2,1,0:T(8,128)(2,1)} copy-done((bf16[4,2,320,640]{3,2,1,0:T(8,128)(2,1)}, bf16[4,2,320,640]{3,2,1,0:T(8,128)(2,1)S(1)}, u32[]{:S(2)}) %copy-start) | copy-done | bytes 3276824
  24.7 2.4 %first_messages.2 = (bf16[2,160,640]{2,1,0:T(8,128)(2,1)}, bf16[2,160,640]{2,1,0:T(8,128)(2,1)}) custom-call(bf16[4,2,320,640]{3,2,1,0:T(8,128)(2,1)} %bitcast.26, bf16[4,2,320,640]{3,2,1,0:T(8,128)(2,1)} %copy-done, bf16[4,2,320,640]{3,2,1,0:T(8,128)(2,1)} %bitcast.27, bf16[4,2,320,640]{3,2,1,0:T(8,128)(2,1)} %copy-done, bf16[4,2,320,640]{3,2,1,0:T(8,128)(2,1)} %bitcast.28, ...), custom_call_target="tpu_custom_call" | custom-call | flops 1 | bytes 1 | tf_op jit(solution)/shard_map/first_messages/pallas_call | solution.py:321
  30.3 2.7 %collective-permute-start.11 = (bf16[2,160,640]{2,1,0:T(8,128)(2,1)}, bf16[2,160,640]{2,1,0:T(8,128)(2,1)S(1)}, u32[]{:S(2)}, u32[]{:S(2)}) collective-permute-start(bf16[2,160,640]{2,1,0:T(8,128)(2,1)} %get-tuple-element.56), channel_id=1, source_target_pairs={{0,48},{8,56},{16,0},{24,8},{32,16},{40,24},{48,32},{56,40},{64,11... | collective-permute-start | bytes 1228808 | tf_op jit(solution)/shard_map/ppermute | solution.py:429
  33.6 4.8 %weight_products.1 = (f32[4,192,128]{2,1,0:T(8,128)}, f32[4,192,128]{2,1,0:T(8,128)}, f32[32,640]{1,0:T(8,128)}, f32[64,640]{1,0:T(8,128)}, f32[32,256]{1,0:T(8,128)}) custom-call(f32[4,16,128]{2,1,0:T(8,128)} %join.5.near_heads, f32[4,16,128]{2,1,0:T(8,128)} %copy-done.39, f32[64,640]{1,0:T(8,128)} %bitcast.45, f32[64,640]{1,0:T(8,128)} %bitcast.47, ...), custom_call_target="tpu_custom_call" | custom-call | flops 1 | bytes 1 | tf_op jit(solution)/shard_map/weight_products/pallas_call | solution.py:655
  40.4 3.0 %collective-permute-done.10.up = bf16[2,160,640]{2,1,0:T(8,128)(2,1)S(1)} collective-permute-done((bf16[2,160,640]{2,1,0:T(8,128)(2,1)}, bf16[2,160,640]{2,1,0:T(8,128)(2,1)S(1)}, u32[]{:S(2)}, u32[]{:S(2)}) %collective-permute-start.10) | collective-permute-done | bytes 409632 | tf_op jit(solution)/shard_map/ppermute | solution.py:429
  44.1 2.2 %second_messages.2 = (bf16[160,640]{1,0:T(8,128)(2,1)}, bf16[160,640]{1,0:T(8,128)(2,1)}) custom-call(bf16[4,2,320,640]{3,2,1,0:T(8,128)(2,1)} %bitcast.29, bf16[4,2,320,640]{3,2,1,0:T(8,128)(2,1)} %copy-done, bf16[4,2,320,640]{3,2,1,0:T(8,128)(2,1)} %bitcast.30, bf16[4,2,320,640]{3,2,1,0:T(8,128)(2,1)} %copy-done, bf16[2,160,640]{2,1,0:T(8,128)(2,1)} %copy-done.9, ...), custom_call_target="tpu_custom_call" | custom-call | flops 1 | bytes 1 | tf_op jit(solution)/shard_map/second_messages/pallas_call | solution.py:347
  47.8 2.5 %first_messages.3 = (bf16[2,160,640]{2,1,0:T(8,128)(2,1)}, bf16[2,160,640]{2,1,0:T(8,128)(2,1)}) custom-call(bf16[4,2,320,640]{3,2,1,0:T(8,128)(2,1)} %bitcast.31, bf16[4,2,320,640]{3,2,1,0:T(8,128)(2,1)} %copy-done, bf16[4,2,320,640]{3,2,1,0:T(8,128)(2,1)} %bitcast.32, bf16[4,2,320,640]{3,2,1,0:T(8,128)(2,1)} %copy-done, bf16[4,2,320,640]{3,2,1,0:T(8,128)(2,1)} %bitcast.33, ...), custom_call_target="tpu_custom_call" | custom-call | flops 1 | bytes 1 | tf_op jit(solution)/shard_map/first_messages/pallas_call | solution.py:321
  50.3 2.6 %collective-permute-start.13 = (bf16[2,160,640]{2,1,0:T(8,128)(2,1)}, bf16[2,160,640]{2,1,0:T(8,128)(2,1)S(1)}, u32[]{:S(2)}, u32[]{:S(2)}) collective-permute-start(bf16[2,160,640]{2,1,0:T(8,128)(2,1)} %get-tuple-element.59), channel_id=1, source_target_pairs={{0,48},{8,56},{16,0},{24,8},{32,16},{40,24},{48,32},{56,40},{64,11... | collective-permute-start | bytes 1228808 | tf_op jit(solution)/shard_map/ppermute | solution.py:429
  55.1 2.3 %chip_sum.3 = bf16[320,640]{1,0:T(8,128)(2,1)} custom-call(bf16[4,2,320,640]{3,2,1,0:T(8,128)(2,1)} %bitcast.34, bf16[4,2,320,640]{3,2,1,0:T(8,128)(2,1)} %copy-done, bf16[2,160,640]{2,1,0:T(8,128)(2,1)} %copy-done.9, bf16[2,160,640]{2,1,0:T(8,128)(2,1)} %copy-done.8, bf16[160,640]{1,0:T(8,128)(2,1)} %copy-done.36, bf16[160,640]{1,0:T(8,128)(2,1)} %copy-done.35), custom_call_target="tpu_custom_call" | custom-call | flops 1 | bytes 1 | tf_op jit(solution)/shard_map/chip_sum/pallas_call | solution.py:370
  57.4 2.5 %collective-permute-start.18 = (bf16[320,640]{1,0:T(8,128)(2,1)}, bf16[320,640]{1,0:T(8,128)(2,1)S(1)}, u32[]{:S(2)}, u32[]{:S(2)}) collective-permute-start(bf16[320,640]{1,0:T(8,128)(2,1)} %chip_sum.3), channel_id=1, source_target_pairs={{0,64},{8,72},{16,80},{24,88},{32,96},{40,104},{48,112},{56,120},{... | collective-permute-start | bytes 1228808 | tf_op jit(solution)/shard_map/ppermute | solution.py:443
  59.9 2.9 %collective-permute-done.12.up = bf16[2,160,640]{2,1,0:T(8,128)(2,1)S(1)} collective-permute-done((bf16[2,160,640]{2,1,0:T(8,128)(2,1)}, bf16[2,160,640]{2,1,0:T(8,128)(2,1)S(1)}, u32[]{:S(2)}, u32[]{:S(2)}) %collective-permute-start.12) | collective-permute-done | bytes 409632 | tf_op jit(solution)/shard_map/ppermute | solution.py:429
  64.3 2.2 %second_messages.3 = (bf16[160,640]{1,0:T(8,128)(2,1)}, bf16[160,640]{1,0:T(8,128)(2,1)}) custom-call(bf16[4,2,320,640]{3,2,1,0:T(8,128)(2,1)} %bitcast.35, bf16[4,2,320,640]{3,2,1,0:T(8,128)(2,1)} %copy-done, bf16[4,2,320,640]{3,2,1,0:T(8,128)(2,1)} %bitcast.36, bf16[4,2,320,640]{3,2,1,0:T(8,128)(2,1)} %copy-done, bf16[2,160,640]{2,1,0:T(8,128)(2,1)} %copy-done.6, ...), custom_call_target="tpu_custom_call" | custom-call | flops 1 | bytes 1 | tf_op jit(solution)/shard_map/second_messages/pallas_call | solution.py:347
  66.5 2.7 %collective-permute-start.15 = (bf16[160,640]{1,0:T(8,128)(2,1)}, bf16[160,640]{1,0:T(8,128)(2,1)S(1)}, u32[]{:S(2)}, u32[]{:S(2)}) collective-permute-start(bf16[160,640]{1,0:T(8,128)(2,1)} %get-tuple-element.61), channel_id=1, source_target_pairs={{0,48},{8,56},{16,0},{24,8},{32,16},{40,24},{48,32},{56,40},{64,11... | collective-permute-start | bytes 614408 | tf_op jit(solution)/shard_map/ppermute | solution.py:445
  74.3 3.0 %token_sums.1.refs_0_.parts0.unread_ref = f32[1,192,128]{2,1,0:T(8,128)} custom-call(f32[1,192,128]{2,1,0:T(8,128)} %get-tuple-element.82.own_ref, f32[1,192,128]{2,1,0:T(8,128)} %copy-done.37, bf16[64,2048]{1,0:T(8,128)(2,1)} %bitcast.49, bf16[64,2048]{1,0:T(8,128)(2,1)} %bitcast.50, f32[640,320]{1,0:T(8,128)} %copy.28.refs_0_.anchor_ref, ...), custom_call_target="tpu_custom_call" | custom-call | flops 1 | bytes 1 | tf_op jit(solution)/shard_map/token_sums/pallas_call | solution.py:673
  78.7 2.5 %chip_sum.2.own_ref = f32[320,640]{1,0:T(8,128)} custom-call(bf16[4,2,320,640]{3,2,1,0:T(8,128)(2,1)} %bitcast.37, bf16[4,2,320,640]{3,2,1,0:T(8,128)(2,1)} %copy-done, bf16[2,160,640]{2,1,0:T(8,128)(2,1)} %copy-done.6, bf16[2,160,640]{2,1,0:T(8,128)(2,1)} %copy-done.7, bf16[160,640]{1,0:T(8,128)(2,1)} %copy-done.33, bf16[160,640]{1,0:T(8,128)(2,1)} %copy-done.34), custom_call_target="tpu_custom_call" | custom-call | flops 1 | bytes 1 | tf_op jit(solution)/shard_map/chip_sum/pallas_call | solution.py:370
  81.9 4.0 %outer_update.1 = (f32[640,320]{1,0:T(8,128)}, f32[640,320]{1,0:T(8,128)}, bf16[320,640]{1,0:T(8,128)(2,1)}) custom-call(s32[3]{0:T(128)} %pad_add_fusion.pos_ref, f32[320,640]{1,0:T(8,128)} %chip_sum.2.own_ref, bf16[320,640]{1,0:T(8,128)(2,1)} %copy-done.17, f32[640,320]{1,0:T(8,128)} %copy.28.refs_0_.anchor_ref, f32[640,320]{1,0:T(8,128)} %copy.29.refs_1_.momentum_ref, ...), custom_call_target="tpu_custom_call" | custom-call | flops 1 | bytes 1 | tf_op jit(solution)/shard_map/outer_update/pallas_call | solution.py:144
  85.9 2.5 %collective-permute-start.21 = (bf16[320,640]{1,0:T(8,128)(2,1)}, bf16[320,640]{1,0:T(8,128)(2,1)S(1)}, u32[]{:S(2)}, u32[]{:S(2)}) collective-permute-start(bf16[320,640]{1,0:T(8,128)(2,1)} %get-tuple-element.67.refs_0_), channel_id=1, source_target_pairs={{0,64},{8,72},{16,80},{24,88},{32,96},{40,104},{48,112},{56,120},{... | collective-permute-start | bytes 1228808 | tf_op jit(solution)/shard_map/ppermute | solution.py:451
  92.5 1.6 %join.6.refs_0_ = f32[2,192,128]{2,1,0:T(8,128)} custom-call(f32[1,192,128]{2,1,0:T(8,128)} %token_sums.1.refs_0_.parts0.unread_ref, f32[1,192,128]{2,1,0:T(8,128)} %copy-done.24), custom_call_target="tpu_custom_call" | custom-call | flops 1 | bytes 1 | tf_op jit(solution)/shard_map/join/pallas_call | solution.py:251
  96.2 4.2 %collective-permute-done.8.refs_1_.parts2 = f32[2,192,128]{2,1,0:T(8,128)S(1)} collective-permute-done((f32[2,192,128]{2,1,0:T(8,128)}, f32[2,192,128]{2,1,0:T(8,128)S(1)}, u32[]{:S(2)}, u32[]{:S(2)}) %collective-permute-start.8) | collective-permute-done | bytes 196640 | tf_op jit(solution)/shard_map/ppermute | solution.py:418
  101.0 1.8 %join.7 = f32[4,192,128]{2,1,0:T(8,128)} custom-call(f32[2,192,128]{2,1,0:T(8,128)} %join.6.refs_0_, f32[2,192,128]{2,1,0:T(8,128)} %copy-done.16), custom_call_target="tpu_custom_call" | custom-call | flops 1 | bytes 1 | tf_op jit(solution)/shard_map/join/pallas_call | solution.py:251
  104.4 1.8 %halves.2 = (bf16[160,640]{1,0:T(8,128)(2,1)}, bf16[160,640]{1,0:T(8,128)(2,1)}) custom-call(bf16[320,640]{1,0:T(8,128)(2,1)} %copy-done.2, bf16[320,640]{1,0:T(8,128)(2,1)} %copy-done.1), custom_call_target="tpu_custom_call" | custom-call | flops 1 | bytes 1 | tf_op jit(solution)/shard_map/halves/pallas_call | solution.py:229
  106.2 2.7 %collective-permute-start.25 = (bf16[160,640]{1,0:T(8,128)(2,1)}, bf16[160,640]{1,0:T(8,128)(2,1)S(1)}, u32[]{:S(2)}, u32[]{:S(2)}) collective-permute-start(bf16[160,640]{1,0:T(8,128)(2,1)} %get-tuple-element.69), channel_id=1, source_target_pairs={{0,48},{8,56},{16,0},{24,8},{32,16},{40,24},{48,32},{56,40},{64,11... | collective-permute-start | bytes 614408 | tf_op jit(solution)/shard_map/ppermute | solution.py:458
  108.8 2.4 %copy.32 = f32[640,320]{0,1:T(8,128)} copy(f32[640,320]{1,0:T(8,128)} %get-tuple-element.63) | data formatting | bytes 1638400 | tf_op jit(solution)/shard_map/outer_update/pallas_call | solution.py:144
  111.2 2.4 %copy.33 = f32[640,320]{0,1:T(8,128)} copy(f32[640,320]{1,0:T(8,128)} %get-tuple-element.64) | data formatting | bytes 1638400 | tf_op jit(solution)/shard_map/outer_update/pallas_call | solution.py:144
  115.0 5.4 %finish.1 = (f32[64,640]{1,0:T(8,128)}, f32[64,640]{1,0:T(8,128)}, f32[2,640]{1,0:T(2,128)}, f32[256,640]{1,0:T(8,128)}) custom-call(f32[1,192,128]{2,1,0:T(8,128)} %token_sums.1.refs_0_.parts0.unread_ref, f32[1,192,128]{2,1,0:T(8,128)} %copy-done.24, f32[2,192,128]{2,1,0:T(8,128)} %copy-done.16, f32[4,192,128]{2,1,0:T(8,128)} %copy-done.25, ...), custom_call_target="tpu_custom_call" | custom-call | flops 1 | bytes 1 | tf_op jit(solution)/shard_map/finish/pallas_call | solution.py:686
  121.9 1.8 %halves.3 = (bf16[160,640]{1,0:T(8,128)(2,1)}, bf16[160,640]{1,0:T(8,128)(2,1)}) custom-call(bf16[320,640]{1,0:T(8,128)(2,1)} %copy-done.4, bf16[320,640]{1,0:T(8,128)(2,1)} %copy-done.3), custom_call_target="tpu_custom_call" | custom-call | flops 1 | bytes 1 | tf_op jit(solution)/shard_map/halves/pallas_call | solution.py:229
  126.0 9.0 %collective-permute-start.28 = (bf16[320,640]{1,0:T(8,128)(2,1)}, bf16[320,640]{1,0:T(8,128)(2,1)S(1)}, u32[]{:S(2)}, u32[]{:S(2)}) collective-permute-start(bf16[320,640]{1,0:T(8,128)(2,1)} %get-tuple-element.72.refs_0_), channel_id=1, source_target_pairs={{0,8},{8,0},{16,24},{24,16},{32,40},{40,32},{48,56},{56,48},{64,72... | collective-permute-start | bytes 1228808 | tf_op jit(solution)/shard_map/ppermute | solution.py:466
  135.5 2.7 %collective-permute-start.37 = (bf16[160,640]{1,0:T(8,128)(2,1)S(1)}, bf16[160,640]{1,0:T(8,128)(2,1)S(1)}, u32[]{:S(2)}, u32[]{:S(2)}) collective-permute-start(bf16[160,640]{1,0:T(8,128)(2,1)S(1)} %collective-permute-done.27.refs_9_), channel_id=1, source_target_pairs={{0,8},{8,0},{16,24},{24,16},{32,40},{40,32},{48,56},{56,48},{64,72... | collective-permute-start | bytes 614408 | tf_op jit(solution)/shard_map/ppermute | solution.py:466
  144.7 10.0 %place.1 = bf16[640,5120]{1,0:T(8,128)(2,1)} custom-call(s32[3]{0:T(128)} %pad_add_fusion.pos_ref, bf16[320,640]{1,0:T(8,128)(2,1)} %get-tuple-element.72.refs_0_, bf16[320,640]{1,0:T(8,128)(2,1)} %get-tuple-element.73.refs_1_, bf16[320,640]{1,0:T(8,128)(2,1)} %get-tuple-element.74.refs_2_, bf16[320,640]{1,0:T(8,128)(2,1)} %get-tuple-element.75.refs_3_, ...), custom_call_target="tpu_custom_call" | custom-call | flops 1 | bytes 1 | tf_op jit(solution)/shard_map/place/pallas_call | solution.py:204
  (165 shorter events, 44.4 us)
Async XLA Ops:
  13.0 10.0 %collective-permute-start.2 = (bf16[4,2,320,640]{3,2,1,0:T(8,128)(2,1)}, bf16[4,2,320,640]{3,2,1,0:T(8,128)(2,1)S(1)}, u32[]{:S(2)}, u32[]{:S(2)}) collective-permute-start(bf16[4,2,320,640]{3,2,1,0:T(8,128)(2,1)} %bitcast.54), channel_id=1, source_target_pairs={{0,8},{8,0},{16,24},{24,16},{32,40},{40,32},{48,56},{56,48},{64,72... | collective-permute-start | bytes 9830408 | tf_op jit(solution)/shard_map/ppermute | solution.py:423
  19.5 7.6 %collective-permute-start.1 = (f32[2,16,128]{2,1,0:T(8,128)}, f32[2,16,128]{2,1,0:T(8,128)S(1)}, u32[]{:S(2)}, u32[]{:S(2)}) collective-permute-start(f32[2,16,128]{2,1,0:T(8,128)} %join.4.refs_0_), channel_id=1, source_target_pairs={{0,2},{1,3},{2,0},{3,1},{4,6},{5,7},{6,4},{7,5},{8,10},{9,11},{10,... | collective-permute-start | bytes 49160 | tf_op jit(solution)/shard_map/ppermute | solution.py:418
  29.1 4.0 %collective-permute-start.3 = (f32[4,16,128]{2,1,0:T(8,128)}, f32[4,16,128]{2,1,0:T(8,128)S(1)}, u32[]{:S(2)}, u32[]{:S(2)}) collective-permute-start(f32[4,16,128]{2,1,0:T(8,128)} %join.5.near_heads), channel_id=1, source_target_pairs={{0,4},{1,5},{2,6},{3,7},{4,0},{5,1},{6,2},{7,3},{8,12},{9,13},{10,... | collective-permute-start | bytes 98312 | tf_op jit(solution)/shard_map/ppermute | solution.py:418
  30.3 10.1 %collective-permute-start.11 = (bf16[2,160,640]{2,1,0:T(8,128)(2,1)}, bf16[2,160,640]{2,1,0:T(8,128)(2,1)S(1)}, u32[]{:S(2)}, u32[]{:S(2)}) collective-permute-start(bf16[2,160,640]{2,1,0:T(8,128)(2,1)} %get-tuple-element.56), channel_id=1, source_target_pairs={{0,48},{8,56},{16,0},{24,8},{32,16},{40,24},{48,32},{56,40},{64,11... | collective-permute-start | bytes 1228808 | tf_op jit(solution)/shard_map/ppermute | solution.py:429
  33.0 10.4 %collective-permute-start.10 = (bf16[2,160,640]{2,1,0:T(8,128)(2,1)}, bf16[2,160,640]{2,1,0:T(8,128)(2,1)S(1)}, u32[]{:S(2)}, u32[]{:S(2)}) collective-permute-start(bf16[2,160,640]{2,1,0:T(8,128)(2,1)} %get-tuple-element.46.refs_2_.refs_0_), channel_id=1, source_target_pairs={{0,16},{8,24},{16,32},{24,40},{32,48},{40,56},{48,0},{56,8},{64,80... | collective-permute-start | bytes 1228808 | tf_op jit(solution)/shard_map/ppermute | solution.py:429
  38.5 14.5 %collective-permute-start.4 = (f32[4,192,128]{2,1,0:T(8,128)}, f32[4,192,128]{2,1,0:T(8,128)S(1)}, u32[]{:S(2)}, u32[]{:S(2)}) collective-permute-start(f32[4,192,128]{2,1,0:T(8,128)} %get-tuple-element.48), channel_id=1, source_target_pairs={{0,4},{1,5},{2,6},{3,7},{4,0},{5,1},{6,2},{7,3},{8,12},{9,13},{10,... | collective-permute-start | bytes 1179656 | tf_op jit(solution)/shard_map/ppermute | solution.py:418
  46.4 7.3 %collective-permute-start.17 = (bf16[160,640]{1,0:T(8,128)(2,1)}, bf16[160,640]{1,0:T(8,128)(2,1)S(1)}, u32[]{:S(2)}, u32[]{:S(2)}) collective-permute-start(bf16[160,640]{1,0:T(8,128)(2,1)} %get-tuple-element.62), channel_id=1, source_target_pairs={{0,48},{8,56},{16,0},{24,8},{32,16},{40,24},{48,32},{56,40},{64,11... | collective-permute-start | bytes 614408 | tf_op jit(solution)/shard_map/ppermute | solution.py:441
  47.4 6.3 %collective-permute-start.16 = (bf16[160,640]{1,0:T(8,128)(2,1)}, bf16[160,640]{1,0:T(8,128)(2,1)S(1)}, u32[]{:S(2)}, u32[]{:S(2)}) collective-permute-start(bf16[160,640]{1,0:T(8,128)(2,1)} %get-tuple-element.57.refs_6_), channel_id=1, source_target_pairs={{0,16},{8,24},{16,32},{24,40},{32,48},{40,56},{48,0},{56,8},{64,80... | collective-permute-start | bytes 614408 | tf_op jit(solution)/shard_map/ppermute | solution.py:441
  50.3 12.5 %collective-permute-start.12 = (bf16[2,160,640]{2,1,0:T(8,128)(2,1)}, bf16[2,160,640]{2,1,0:T(8,128)(2,1)S(1)}, u32[]{:S(2)}, u32[]{:S(2)}) collective-permute-start(bf16[2,160,640]{2,1,0:T(8,128)(2,1)} %get-tuple-element.58), channel_id=1, source_target_pairs={{0,16},{8,24},{16,32},{24,40},{32,48},{40,56},{48,0},{56,8},{64,80... | collective-permute-start | bytes 1228808 | tf_op jit(solution)/shard_map/ppermute | solution.py:429
  50.3 12.4 %collective-permute-start.13 = (bf16[2,160,640]{2,1,0:T(8,128)(2,1)}, bf16[2,160,640]{2,1,0:T(8,128)(2,1)S(1)}, u32[]{:S(2)}, u32[]{:S(2)}) collective-permute-start(bf16[2,160,640]{2,1,0:T(8,128)(2,1)} %get-tuple-element.59), channel_id=1, source_target_pairs={{0,48},{8,56},{16,0},{24,8},{32,16},{40,24},{48,32},{56,40},{64,11... | collective-permute-start | bytes 1228808 | tf_op jit(solution)/shard_map/ppermute | solution.py:429
  53.0 16.2 %collective-permute-start.5 = (f32[2,192,128]{2,1,0:T(8,128)S(1)}, f32[2,192,128]{2,1,0:T(8,128)S(1)}, u32[]{:S(2)}, u32[]{:S(2)}) collective-permute-start(f32[2,192,128]{2,1,0:T(8,128)S(1)} %slice_add_fusion), channel_id=1, source_target_pairs={{0,2},{1,3},{2,0},{3,1},{4,6},{5,7},{6,4},{7,5},{8,10},{9,11},{10,... | collective-permute-start | bytes 589832 | tf_op jit(solution)/shard_map/ppermute | solution.py:418
  57.4 23.7 %collective-permute-start.18 = (bf16[320,640]{1,0:T(8,128)(2,1)}, bf16[320,640]{1,0:T(8,128)(2,1)S(1)}, u32[]{:S(2)}, u32[]{:S(2)}) collective-permute-start(bf16[320,640]{1,0:T(8,128)(2,1)} %chip_sum.3), channel_id=1, source_target_pairs={{0,64},{8,72},{16,80},{24,88},{32,96},{40,104},{48,112},{56,120},{... | collective-permute-start | bytes 1228808 | tf_op jit(solution)/shard_map/ppermute | solution.py:443
  66.5 10.8 %collective-permute-start.14 = (bf16[160,640]{1,0:T(8,128)(2,1)}, bf16[160,640]{1,0:T(8,128)(2,1)S(1)}, u32[]{:S(2)}, u32[]{:S(2)}) collective-permute-start(bf16[160,640]{1,0:T(8,128)(2,1)} %get-tuple-element.60), channel_id=1, source_target_pairs={{0,16},{8,24},{16,32},{24,40},{32,48},{40,56},{48,0},{56,8},{64,80... | collective-permute-start | bytes 614408 | tf_op jit(solution)/shard_map/ppermute | solution.py:445
  66.5 10.8 %collective-permute-start.15 = (bf16[160,640]{1,0:T(8,128)(2,1)}, bf16[160,640]{1,0:T(8,128)(2,1)S(1)}, u32[]{:S(2)}, u32[]{:S(2)}) collective-permute-start(bf16[160,640]{1,0:T(8,128)(2,1)} %get-tuple-element.61), channel_id=1, source_target_pairs={{0,48},{8,56},{16,0},{24,8},{32,16},{40,24},{48,32},{56,40},{64,11... | collective-permute-start | bytes 614408 | tf_op jit(solution)/shard_map/ppermute | solution.py:445
  69.9 3.8 %collective-permute-start.6 = (f32[1,192,128]{2,1,0:T(8,128)S(1)}, f32[1,192,128]{2,1,0:T(8,128)S(1)}, u32[]{:S(2)}, u32[]{:S(2)}) collective-permute-start(f32[1,192,128]{2,1,0:T(8,128)S(1)} %get-tuple-element.81), channel_id=1, source_target_pairs={{0,1},{1,0},{2,3},{3,2},{4,5},{5,4},{6,7},{7,6},{8,9},{9,8},{10,11... | collective-permute-start | bytes 294920 | tf_op jit(solution)/shard_map/ppermute | solution.py:418
  85.9 8.7 %collective-permute-start.21 = (bf16[320,640]{1,0:T(8,128)(2,1)}, bf16[320,640]{1,0:T(8,128)(2,1)S(1)}, u32[]{:S(2)}, u32[]{:S(2)}) collective-permute-start(bf16[320,640]{1,0:T(8,128)(2,1)} %get-tuple-element.67.refs_0_), channel_id=1, source_target_pairs={{0,64},{8,72},{16,80},{24,88},{32,96},{40,104},{48,112},{56,120},{... | collective-permute-start | bytes 1228808 | tf_op jit(solution)/shard_map/ppermute | solution.py:451
  88.4 3.5 %collective-permute-start.7 = (f32[1,192,128]{2,1,0:T(8,128)S(1)}, f32[1,192,128]{2,1,0:T(8,128)S(1)}, u32[]{:S(2)}, u32[]{:S(2)}) collective-permute-start(f32[1,192,128]{2,1,0:T(8,128)S(1)} %copy-done.10), channel_id=1, source_target_pairs={{0,1},{1,0},{2,3},{3,2},{4,5},{5,4},{6,7},{7,6},{8,9},{9,8},{10,11... | collective-permute-start | bytes 294920 | tf_op jit(solution)/shard_map/ppermute | solution.py:418
  89.1 13.7 %collective-permute-start.20 = (bf16[320,640]{1,0:T(8,128)(2,1)}, bf16[320,640]{1,0:T(8,128)(2,1)S(1)}, u32[]{:S(2)}, u32[]{:S(2)}) collective-permute-start(bf16[320,640]{1,0:T(8,128)(2,1)} %get-tuple-element.67.refs_0_), channel_id=1, source_target_pairs={{0,48},{8,56},{16,0},{24,8},{32,16},{40,24},{48,32},{56,40},{64,11... | collective-permute-start | bytes 1228808 | tf_op jit(solution)/shard_map/ppermute | solution.py:452
  89.1 13.7 %collective-permute-start.19 = (bf16[320,640]{1,0:T(8,128)(2,1)}, bf16[320,640]{1,0:T(8,128)(2,1)S(1)}, u32[]{:S(2)}, u32[]{:S(2)}) collective-permute-start(bf16[320,640]{1,0:T(8,128)(2,1)} %get-tuple-element.67.refs_0_), channel_id=1, source_target_pairs={{0,16},{8,24},{16,32},{24,40},{32,48},{40,56},{48,0},{56,8},{64,80... | collective-permute-start | bytes 1228808 | tf_op jit(solution)/shard_map/ppermute | solution.py:452
  94.1 6.2 %collective-permute-start.8 = (f32[2,192,128]{2,1,0:T(8,128)}, f32[2,192,128]{2,1,0:T(8,128)S(1)}, u32[]{:S(2)}, u32[]{:S(2)}) collective-permute-start(f32[2,192,128]{2,1,0:T(8,128)} %join.6.refs_0_), channel_id=1, source_target_pairs={{0,2},{1,3},{2,0},{3,1},{4,6},{5,7},{6,4},{7,5},{8,10},{9,11},{10,... | collective-permute-start | bytes 589832 | tf_op jit(solution)/shard_map/ppermute | solution.py:418
  94.7 25.8 %collective-permute-start.23 = (bf16[320,640]{1,0:T(8,128)(2,1)S(1)}, bf16[320,640]{1,0:T(8,128)(2,1)S(1)}, u32[]{:S(2)}, u32[]{:S(2)}) collective-permute-start(bf16[320,640]{1,0:T(8,128)(2,1)S(1)} %collective-permute-done.21.refs_3_), channel_id=1, source_target_pairs={{0,48},{8,56},{16,0},{24,8},{32,16},{40,24},{48,32},{56,40},{64,11... | collective-permute-start | bytes 1228808 | tf_op jit(solution)/shard_map/ppermute | solution.py:459
  95.1 25.4 %collective-permute-start.22 = (bf16[320,640]{1,0:T(8,128)(2,1)S(1)}, bf16[320,640]{1,0:T(8,128)(2,1)S(1)}, u32[]{:S(2)}, u32[]{:S(2)}) collective-permute-start(bf16[320,640]{1,0:T(8,128)(2,1)S(1)} %collective-permute-done.21.refs_3_), channel_id=1, source_target_pairs={{0,16},{8,24},{16,32},{24,40},{32,48},{40,56},{48,0},{56,8},{64,80... | collective-permute-start | bytes 1228808 | tf_op jit(solution)/shard_map/ppermute | solution.py:459
  102.8 11.4 %collective-permute-start.9 = (f32[4,192,128]{2,1,0:T(8,128)}, f32[4,192,128]{2,1,0:T(8,128)S(1)}, u32[]{:S(2)}, u32[]{:S(2)}) collective-permute-start(f32[4,192,128]{2,1,0:T(8,128)} %join.7), channel_id=1, source_target_pairs={{0,4},{1,5},{2,6},{3,7},{4,0},{5,1},{6,2},{7,3},{8,12},{9,13},{10,... | collective-permute-start | bytes 1179656 | tf_op jit(solution)/shard_map/ppermute | solution.py:418
  106.2 19.1 %collective-permute-start.24 = (bf16[160,640]{1,0:T(8,128)(2,1)}, bf16[160,640]{1,0:T(8,128)(2,1)S(1)}, u32[]{:S(2)}, u32[]{:S(2)}) collective-permute-start(bf16[160,640]{1,0:T(8,128)(2,1)} %get-tuple-element.68), channel_id=1, source_target_pairs={{0,16},{8,24},{16,32},{24,40},{32,48},{40,56},{48,0},{56,8},{64,80... | collective-permute-start | bytes 614408 | tf_op jit(solution)/shard_map/ppermute | solution.py:458
  106.2 19.1 %collective-permute-start.25 = (bf16[160,640]{1,0:T(8,128)(2,1)}, bf16[160,640]{1,0:T(8,128)(2,1)S(1)}, u32[]{:S(2)}, u32[]{:S(2)}) collective-permute-start(bf16[160,640]{1,0:T(8,128)(2,1)} %get-tuple-element.69), channel_id=1, source_target_pairs={{0,48},{8,56},{16,0},{24,8},{32,16},{40,24},{48,32},{56,40},{64,11... | collective-permute-start | bytes 614408 | tf_op jit(solution)/shard_map/ppermute | solution.py:458
  123.7 11.8 %collective-permute-start.27 = (bf16[160,640]{1,0:T(8,128)(2,1)}, bf16[160,640]{1,0:T(8,128)(2,1)S(1)}, u32[]{:S(2)}, u32[]{:S(2)}) collective-permute-start(bf16[160,640]{1,0:T(8,128)(2,1)} %get-tuple-element.80), channel_id=1, source_target_pairs={{0,48},{8,56},{16,0},{24,8},{32,16},{40,24},{48,32},{56,40},{64,11... | collective-permute-start | bytes 614408 | tf_op jit(solution)/shard_map/ppermute | solution.py:462
  123.7 14.4 %collective-permute-start.26 = (bf16[160,640]{1,0:T(8,128)(2,1)}, bf16[160,640]{1,0:T(8,128)(2,1)S(1)}, u32[]{:S(2)}, u32[]{:S(2)}) collective-permute-start(bf16[160,640]{1,0:T(8,128)(2,1)} %get-tuple-element.70.refs_8_), channel_id=1, source_target_pairs={{0,16},{8,24},{16,32},{24,40},{32,48},{40,56},{48,0},{56,8},{64,80... | collective-permute-start | bytes 614408 | tf_op jit(solution)/shard_map/ppermute | solution.py:462
  126.0 14.9 %collective-permute-start.28 = (bf16[320,640]{1,0:T(8,128)(2,1)}, bf16[320,640]{1,0:T(8,128)(2,1)S(1)}, u32[]{:S(2)}, u32[]{:S(2)}) collective-permute-start(bf16[320,640]{1,0:T(8,128)(2,1)} %get-tuple-element.72.refs_0_), channel_id=1, source_target_pairs={{0,8},{8,0},{16,24},{24,16},{32,40},{40,32},{48,56},{56,48},{64,72... | collective-permute-start | bytes 1228808 | tf_op jit(solution)/shard_map/ppermute | solution.py:466
  135.0 4.4 %collective-permute-start.34 = (bf16[160,640]{1,0:T(8,128)(2,1)}, bf16[160,640]{1,0:T(8,128)(2,1)S(1)}, u32[]{:S(2)}, u32[]{:S(2)}) collective-permute-start(bf16[160,640]{1,0:T(8,128)(2,1)} %get-tuple-element.78.refs_6_), channel_id=1, source_target_pairs={{0,8},{8,0},{16,24},{24,16},{32,40},{40,32},{48,56},{56,48},{64,72... | collective-permute-start | bytes 614408 | tf_op jit(solution)/shard_map/ppermute | solution.py:466
  135.0 4.5 %collective-permute-start.35 = (bf16[160,640]{1,0:T(8,128)(2,1)}, bf16[160,640]{1,0:T(8,128)(2,1)S(1)}, u32[]{:S(2)}, u32[]{:S(2)}) collective-permute-start(bf16[160,640]{1,0:T(8,128)(2,1)} %get-tuple-element.79.refs_7_), channel_id=1, source_target_pairs={{0,8},{8,0},{16,24},{24,16},{32,40},{40,32},{48,56},{56,48},{64,72... | collective-permute-start | bytes 614408 | tf_op jit(solution)/shard_map/ppermute | solution.py:466
  135.5 4.4 %collective-permute-start.37 = (bf16[160,640]{1,0:T(8,128)(2,1)S(1)}, bf16[160,640]{1,0:T(8,128)(2,1)S(1)}, u32[]{:S(2)}, u32[]{:S(2)}) collective-permute-start(bf16[160,640]{1,0:T(8,128)(2,1)S(1)} %collective-permute-done.27.refs_9_), channel_id=1, source_target_pairs={{0,8},{8,0},{16,24},{24,16},{32,40},{40,32},{48,56},{56,48},{64,72... | collective-permute-start | bytes 614408 | tf_op jit(solution)/shard_map/ppermute | solution.py:466
  140.9 2.8 %collective-permute-start.33 = (bf16[320,640]{1,0:T(8,128)(2,1)}, bf16[320,640]{1,0:T(8,128)(2,1)S(1)}, u32[]{:S(2)}, u32[]{:S(2)}) collective-permute-start(bf16[320,640]{1,0:T(8,128)(2,1)} %get-tuple-element.77.refs_5_), channel_id=1, source_target_pairs={{0,8},{8,0},{16,24},{24,16},{32,40},{40,32},{48,56},{56,48},{64,72... | collective-permute-start | bytes 1228808 | tf_op jit(solution)/shard_map/ppermute | solution.py:466
  (49 other events, 177.5 us)

commit v3 on v2

--- a/solution.py
+++ b/solution.py
@@ -157,29 +157,27 @@
     )(pos, own, far, anchor, momentum, after)
 
 
-def place_kernel(chips, after, pos_ref, *refs):
+def place_kernel(chips, pos_ref, *refs):
     out = refs[-1]
-    count = sum(pieces for _, _, pieces in chips)
+    count = sum(2 if cut else 1 for _, _, cut in chips)
     mine, theirs = refs[:count], refs[count : 2 * count]
     first_core = pos_ref[0] == 0
-    step = pl.program_id(0)
-    early = step < pl.num_programs(0) // 2
-    size = mine[0].shape[0]
-    at = pl.multiple_of(lax.rem(step, 64 // size) * size, size)
-    low_lane = lax.broadcasted_iota(jnp.int32, (size, 128), 1) < 64
+    low_lane = lax.broadcasted_iota(jnp.int32, (64, 128), 1) < 64
     index = 0
-    for dy, dx, pieces in chips:
+    for dy, dx, cut in chips:
         a, b = mine[index][...], theirs[index][...]
-        if pieces == 2:
-            a = jnp.where(early, a, mine[index + 1][...])
-            b = jnp.where(early, b, theirs[index + 1][...])
-        index += pieces
+        index += 1
+        if cut:
+            early = pl.program_id(0) < cut
+            a = jnp.where(early, a, mine[index][...])
+            b = jnp.where(early, b, theirs[index][...])
+            index += 1
         low, high = jnp.where(first_core, a, b), jnp.where(first_core, b, a)
         chip = lax.rem(pos_ref[2] + dx, N_XH) * N_Y + lax.rem(pos_ref[1] + dy, N_Y)
 
         def put(half, lane, value):
             lanes = pl.ds(pl.multiple_of(chip * PAIR + lane, 128), value.shape[1])
-            out[pl.ds(at + half * 64, size), lanes] = value
+            out[half * 64 : half * 64 + 64, lanes] = value
 
         for half in range(2):
             put(half, 0, low[:, half * 256 : half * 256 + 256])
@@ -190,24 +188,22 @@
 
 
 def place(pos, chips, mine, theirs, after):
-    size = 32
-    steps = ROWS // 2 // size
-
-    def block(piece, pieces):
-        if pieces == 1:
-            return pl.BlockSpec((size, PAIR), lambda i, pos: (i, 0))
-        if piece == 0:
-            return pl.BlockSpec((size, PAIR), lambda i, pos: (jnp.minimum(i, steps // 2 - 1), 0))
-        return pl.BlockSpec((size, PAIR), lambda i, pos: (jnp.maximum(i - steps // 2, 0), 0))
-
-    blocks = [block(piece, pieces) for _, _, pieces in chips for piece in range(pieces)]
-    return pl.pallas_call(
-        functools.partial(place_kernel, chips, len(after)),
+    def blocks(cut):
+        if not cut:
+            return [pl.BlockSpec((64, PAIR), lambda i, pos: (i, 0))]
+        return [
+            pl.BlockSpec((64, PAIR), lambda i, pos: (jnp.minimum(i, cut - 1), 0)),
+            pl.BlockSpec((64, PAIR), lambda i, pos: (jnp.maximum(i - cut, 0), 0)),
+        ]
+
+    specs = [spec for _, _, cut in chips for spec in blocks(cut)]
+    return pl.pallas_call(
+        functools.partial(place_kernel, chips),
         grid_spec=pltpu.PrefetchScalarGridSpec(
             num_scalar_prefetch=1,
-            grid=(steps,),
-            in_specs=blocks * 2 + [unread] * len(after),
-            out_specs=pl.BlockSpec((QBLOCK, N_Y * N_XH * PAIR), lambda i, pos: (i // (64 // size), 0)),
+            grid=(ROWS // QBLOCK,),
+            in_specs=specs * 2 + [unread] * len(after),
+            out_specs=pl.BlockSpec((QBLOCK, N_Y * N_XH * PAIR), lambda i, pos: (i, 0)),
         ),
         out_shape=jax.ShapeDtypeStruct((ROWS, N_Y * N_XH * PAIR), bf16),
         compiler_params=limit,
@@ -216,26 +212,21 @@
     )(pos, *mine, *theirs, *after)
 
 
-def halves_kernel(after, below, above, *refs):
-    first, second = refs[after:]
-    first[...] = below[...]
-    second[...] = above[...]
-
-
-def halves(below, above, after):
+def parts_kernel(below, above, first, second):
+    cut = first.shape[0]
+    first[...] = below[0:cut]
+    second[...] = above[cut:]
+
+
+def parts(below, above, cut):
     rows, columns = below.shape
-    shape = jax.ShapeDtypeStruct((rows // 2, columns), below.dtype)
-    part = [pl.BlockSpec((rows // 2, columns), lambda i, j=j: (j, 0)) for j in range(2)]
-    return pl.pallas_call(
-        functools.partial(halves_kernel, len(after)),
-        grid=(1,),
-        in_specs=part + [unread] * len(after),
-        out_specs=[part[0], part[0]],
-        out_shape=[shape, shape],
-        compiler_params=limit,
-        cost_estimate=brief,
-        name="halves",
-    )(below, above, *after)
+    return pl.pallas_call(
+        parts_kernel,
+        out_shape=[jax.ShapeDtypeStruct((n, columns), below.dtype) for n in (cut * 64, rows - cut * 64)],
+        compiler_params=limit,
+        cost_estimate=brief,
+        name="parts",
+    )(below, above)
 
 
 def join_kernel(after, *refs):
@@ -258,21 +249,21 @@
     )(*parts, *after)
 
 
-def settle_kernel(a, b, a_out, b_out, token):
-    del a, b, a_out, b_out
+def settle_kernel(a, b, unread_ref, a_out, b_out, token):
+    del a, b, unread_ref, a_out, b_out
     token[...] = jnp.zeros_like(token)
 
 
-def settle(a, b):
+def settle(a, b, after):
     return pl.pallas_call(
         settle_kernel,
-        in_specs=[unread] * 2,
+        in_specs=[unread] * 3,
         out_specs=[unread] * 2 + [pl.BlockSpec(memory_space=pltpu.VMEM)],
         out_shape=[jax.ShapeDtypeStruct(x.shape, x.dtype) for x in (a, b)] + [jax.ShapeDtypeStruct((8, 128), f32)],
         input_output_aliases={0: 0, 1: 1},
         cost_estimate=brief,
         name="settle",
-    )(a, b)
+    )(a, b, after)
 
 
 def gate_kernel(*refs):
@@ -452,19 +443,20 @@
     up0, down0 = send(n0, perm=to_y(1)), send(n0, perm=to_y(-1))
     q01 = join([q0, q1], [])
     q2 = across(q01, 2)
-    anchor_t, momentum_t, settled = settle(new_anchor.T, new_momentum.T)
     q4 = across(join([q01, q2], []), 4)
-    first0 = halves(up0, down0, [])
+    first0 = parts(up0, down0, 2)
     on0 = send(first0[0], perm=to_y(1)), send(first0[1], perm=to_y(-1))
+    (n1,) = gate([n1], [q01])
     up1, down1 = send(n1, perm=to_y(1)), send(n1, perm=to_y(-1))
-    inner = finish(q0, q1, q2, q4, pre, center, sines, params, [])
-    first1 = halves(up1, down1, [])
+    first1 = parts(up1, down1, 3)
     on1 = send(first1[0], perm=to_y(1)), send(first1[1], perm=to_y(-1))
+    inner = finish(q0, q1, q2, q4, pre, center, sines, params, [first1[0]])
+    anchor_t, momentum_t, settled = settle(new_anchor.T, new_momentum.T, first1[0])
     mine = [n0, up0, down0, n1, up1, down1, *on0]
-    mine = gate(mine, [first1[0], inner[2], settled])
+    mine = gate(mine, [*on1, inner[2], settled])
     mine = [*mine, *on1]
     theirs = [to_sibling(part) for part in mine]
-    chips = ((0, 0, 1), (3, 0, 1), (1, 0, 1), (0, 1, 1), (3, 1, 1), (1, 1, 1), (2, 0, 2), (2, 1, 2))
+    chips = ((0, 0, 0), (3, 0, 0), (1, 0, 0), (0, 1, 0), (3, 1, 0), (1, 1, 0), (2, 0, 2), (2, 1, 3))
     new_params = place(pos, chips, mine, theirs, [inner[2], settled])
     return tuple(a[None] for a in inner) + (anchor_t.T, momentum_t.T, new_params)
 

time: 156 us -> 155 us (level)
  starting transfers between devices: 46.9 us -> 43.6 us
  waiting for transfers between devices: 17.7 us -> 20.8 us
    ppermute x10, starting transfers between devices: 14.6 us -> 11.1 us  [per_device(): theirs = [to_sibling(part) for part in mine]]
  transfers between devices with their start and end apart: 38 -> 38, of which waited for: 13 -> 14; matrix products, arithmetic and copies ran while one was open for 5% -> 6% of each run, Pallas kernels for 24% -> 24%
where the time goes in v3:
time: 155 us; the launch traced here: 154 us
  Pallas kernels  62.3 us (40%)
  starting transfers between devices  43.6 us (28%)
  local copies, waits for them, and re-layouts  25 us (16%)
  waiting for transfers between devices  20.8 us (13%)
  other arithmetic  1.6 us (1%)
    unnamed x88, local copies, waits for them, and re-layouts  20.1 us
    pallas_call x1, Pallas kernels, quantize(): pl.pallas_call(quant_kernel, grid_spec=pltpu.PrefetchScalarGridSpec(num_s...  11.7 us
    ppermute x10, starting transfers between devices, per_device(): theirs = [to_sibling(part) for part in mine]  11.1 us
    ppermute x9, starting transfers between devices, across(): return lax.ppermute(value, 'fsdp', [(i, i ^ bit) for i in range(N_FSDP)])  9.54 us
    pallas_call x1, Pallas kernels, place(): pl.pallas_call(functools.partial(place_kernel, chips), grid_spec=pltpu.Pr...  8.57 us
    ppermute x9, waiting for transfers between devices, across(): return lax.ppermute(value, 'fsdp', [(i, i ^ bit) for i in range(N_FSDP)])  8.44 us
    pallas_call x4, Pallas kernels, join(): pl.pallas_call(functools.partial(join_kernel, len(after)), in_specs=[pl.B...  6.09 us
    ppermute x2, waiting for transfers between devices, ring(): send(messages[0], perm=to_y(1))  6 us
  transfers between devices with their start and end apart: 38, of which 14 were waited for; matrix products, arithmetic and copies ran while one was open for 6% of the time, Pallas kernels for 24%

profile of v3, /device:TPU:1, one launch (start us, length us, event | category | flops | bytes accessed | tf_op | source)
XLA Modules:
  0.0 154.3 jit_solution(2981018316324806229)
XLA Ops:
  1.3 11.7 %quantize.1 = (bf16[8,320,640]{2,1,0:T(8,128)(2,1)}, bf16[8,320,640]{2,1,0:T(8,128)(2,1)}) custom-call(s32[3]{0:T(128)} %pad_add_fusion.pos_ref, bf16[640,5120]{1,0:T(8,128)(2,1)} %start_ref.1, bf16[640,5120]{1,0:T(8,128)(2,1)} %bitcast.38), custom_call_target="tpu_custom_call" | custom-call | flops 1 | bytes 1 | tf_op jit(solution)/shard_map/quantize/pallas_call | solution.py:89
  14.8 1.8 %collective-permute-start = (f32[1,16,128]{2,1,0:T(8,128)S(1)}, f32[1,16,128]{2,1,0:T(8,128)S(1)}, u32[]{:S(2)}, u32[]{:S(2)}) collective-permute-start(f32[1,16,128]{2,1,0:T(8,128)S(1)} %maximum_bitcast_fusion.refs_0_), channel_id=1, source_target_pairs={{0,1},{1,0},{2,3},{3,2},{4,5},{5,4},{6,7},{7,6},{8,9},{9,8},{10,11... | collective-permute-start | bytes 24584 | tf_op jit(solution)/shard_map/ppermute | solution.py:409
  19.5 3.4 %collective-permute-start.1 = (f32[2,16,128]{2,1,0:T(8,128)}, f32[2,16,128]{2,1,0:T(8,128)S(1)}, u32[]{:S(2)}, u32[]{:S(2)}) collective-permute-start(f32[2,16,128]{2,1,0:T(8,128)} %join.4.refs_0_), channel_id=1, source_target_pairs={{0,2},{1,3},{2,0},{3,1},{4,6},{5,7},{6,4},{7,5},{8,10},{9,11},{10,... | collective-permute-start | bytes 49160 | tf_op jit(solution)/shard_map/ppermute | solution.py:409
  23.0 1.7 %copy-done = bf16[4,2,320,640]{3,2,1,0:T(8,128)(2,1)} copy-done((bf16[4,2,320,640]{3,2,1,0:T(8,128)(2,1)}, bf16[4,2,320,640]{3,2,1,0:T(8,128)(2,1)S(1)}, u32[]{:S(2)}) %copy-start) | copy-done | bytes 3276824
  24.6 2.4 %first_messages.2 = (bf16[2,160,640]{2,1,0:T(8,128)(2,1)}, bf16[2,160,640]{2,1,0:T(8,128)(2,1)}) custom-call(bf16[4,2,320,640]{3,2,1,0:T(8,128)(2,1)} %bitcast.26, bf16[4,2,320,640]{3,2,1,0:T(8,128)(2,1)} %copy-done, bf16[4,2,320,640]{3,2,1,0:T(8,128)(2,1)} %bitcast.27, bf16[4,2,320,640]{3,2,1,0:T(8,128)(2,1)} %copy-done, bf16[4,2,320,640]{3,2,1,0:T(8,128)(2,1)} %bitcast.28, ...), custom_call_target="tpu_custom_call" | custom-call | flops 1 | bytes 1 | tf_op jit(solution)/shard_map/first_messages/pallas_call | solution.py:312
  30.3 2.7 %collective-permute-start.11 = (bf16[2,160,640]{2,1,0:T(8,128)(2,1)}, bf16[2,160,640]{2,1,0:T(8,128)(2,1)S(1)}, u32[]{:S(2)}, u32[]{:S(2)}) collective-permute-start(bf16[2,160,640]{2,1,0:T(8,128)(2,1)} %get-tuple-element.52), channel_id=1, source_target_pairs={{0,48},{8,56},{16,0},{24,8},{32,16},{40,24},{48,32},{56,40},{64,11... | collective-permute-start | bytes 1228808 | tf_op jit(solution)/shard_map/ppermute | solution.py:420
  33.6 4.9 %weight_products.1 = (f32[4,192,128]{2,1,0:T(8,128)}, f32[4,192,128]{2,1,0:T(8,128)}, f32[32,640]{1,0:T(8,128)}, f32[64,640]{1,0:T(8,128)}, f32[32,256]{1,0:T(8,128)}) custom-call(f32[4,16,128]{2,1,0:T(8,128)} %join.5.near_heads, f32[4,16,128]{2,1,0:T(8,128)} %copy-done.39, f32[64,640]{1,0:T(8,128)} %bitcast.45, f32[64,640]{1,0:T(8,128)} %bitcast.47, ...), custom_call_target="tpu_custom_call" | custom-call | flops 1 | bytes 1 | tf_op jit(solution)/shard_map/weight_products/pallas_call | solution.py:647
  38.7 1.6 %collective-permute-done.11.down = bf16[2,160,640]{2,1,0:T(8,128)(2,1)S(1)} collective-permute-done((bf16[2,160,640]{2,1,0:T(8,128)(2,1)}, bf16[2,160,640]{2,1,0:T(8,128)(2,1)S(1)}, u32[]{:S(2)}, u32[]{:S(2)}) %collective-permute-start.11) | collective-permute-done | bytes 409632 | tf_op jit(solution)/shard_map/ppermute | solution.py:420
  40.3 3.0 %collective-permute-done.10.up = bf16[2,160,640]{2,1,0:T(8,128)(2,1)S(1)} collective-permute-done((bf16[2,160,640]{2,1,0:T(8,128)(2,1)}, bf16[2,160,640]{2,1,0:T(8,128)(2,1)S(1)}, u32[]{:S(2)}, u32[]{:S(2)}) %collective-permute-start.10) | collective-permute-done | bytes 409632 | tf_op jit(solution)/shard_map/ppermute | solution.py:420
  44.1 2.2 %second_messages.2 = (bf16[160,640]{1,0:T(8,128)(2,1)}, bf16[160,640]{1,0:T(8,128)(2,1)}) custom-call(bf16[4,2,320,640]{3,2,1,0:T(8,128)(2,1)} %bitcast.29, bf16[4,2,320,640]{3,2,1,0:T(8,128)(2,1)} %copy-done, bf16[4,2,320,640]{3,2,1,0:T(8,128)(2,1)} %bitcast.30, bf16[4,2,320,640]{3,2,1,0:T(8,128)(2,1)} %copy-done, bf16[2,160,640]{2,1,0:T(8,128)(2,1)} %copy-done.9, ...), custom_call_target="tpu_custom_call" | custom-call | flops 1 | bytes 1 | tf_op jit(solution)/shard_map/second_messages/pallas_call | solution.py:338
  47.8 2.5 %first_messages.3 = (bf16[2,160,640]{2,1,0:T(8,128)(2,1)}, bf16[2,160,640]{2,1,0:T(8,128)(2,1)}) custom-call(bf16[4,2,320,640]{3,2,1,0:T(8,128)(2,1)} %bitcast.31, bf16[4,2,320,640]{3,2,1,0:T(8,128)(2,1)} %copy-done, bf16[4,2,320,640]{3,2,1,0:T(8,128)(2,1)} %bitcast.32, bf16[4,2,320,640]{3,2,1,0:T(8,128)(2,1)} %copy-done, bf16[4,2,320,640]{3,2,1,0:T(8,128)(2,1)} %bitcast.33, ...), custom_call_target="tpu_custom_call" | custom-call | flops 1 | bytes 1 | tf_op jit(solution)/shard_map/first_messages/pallas_call | solution.py:312
  50.3 2.6 %collective-permute-start.13 = (bf16[2,160,640]{2,1,0:T(8,128)(2,1)}, bf16[2,160,640]{2,1,0:T(8,128)(2,1)S(1)}, u32[]{:S(2)}, u32[]{:S(2)}) collective-permute-start(bf16[2,160,640]{2,1,0:T(8,128)(2,1)} %get-tuple-element.55), channel_id=1, source_target_pairs={{0,48},{8,56},{16,0},{24,8},{32,16},{40,24},{48,32},{56,40},{64,11... | collective-permute-start | bytes 1228808 | tf_op jit(solution)/shard_map/ppermute | solution.py:420
  54.9 2.4 %chip_sum.3 = bf16[320,640]{1,0:T(8,128)(2,1)} custom-call(bf16[4,2,320,640]{3,2,1,0:T(8,128)(2,1)} %bitcast.34, bf16[4,2,320,640]{3,2,1,0:T(8,128)(2,1)} %copy-done, bf16[2,160,640]{2,1,0:T(8,128)(2,1)} %copy-done.9, bf16[2,160,640]{2,1,0:T(8,128)(2,1)} %copy-done.8, bf16[160,640]{1,0:T(8,128)(2,1)} %copy-done.34, bf16[160,640]{1,0:T(8,128)(2,1)} %copy-done.33), custom_call_target="tpu_custom_call" | custom-call | flops 1 | bytes 1 | tf_op jit(solution)/shard_map/chip_sum/pallas_call | solution.py:361
  57.3 2.5 %collective-permute-start.18 = (bf16[320,640]{1,0:T(8,128)(2,1)}, bf16[320,640]{1,0:T(8,128)(2,1)S(1)}, u32[]{:S(2)}, u32[]{:S(2)}) collective-permute-start(bf16[320,640]{1,0:T(8,128)(2,1)} %chip_sum.3), channel_id=1, source_target_pairs={{0,64},{8,72},{16,80},{24,88},{32,96},{40,104},{48,112},{56,120},{... | collective-permute-start | bytes 1228808 | tf_op jit(solution)/shard_map/ppermute | solution.py:434
  59.7 3.0 %collective-permute-done.12.up = bf16[2,160,640]{2,1,0:T(8,128)(2,1)S(1)} collective-permute-done((bf16[2,160,640]{2,1,0:T(8,128)(2,1)}, bf16[2,160,640]{2,1,0:T(8,128)(2,1)S(1)}, u32[]{:S(2)}, u32[]{:S(2)}) %collective-permute-start.12) | collective-permute-done | bytes 409632 | tf_op jit(solution)/shard_map/ppermute | solution.py:420
  64.2 2.2 %second_messages.3 = (bf16[160,640]{1,0:T(8,128)(2,1)}, bf16[160,640]{1,0:T(8,128)(2,1)}) custom-call(bf16[4,2,320,640]{3,2,1,0:T(8,128)(2,1)} %bitcast.35, bf16[4,2,320,640]{3,2,1,0:T(8,128)(2,1)} %copy-done, bf16[4,2,320,640]{3,2,1,0:T(8,128)(2,1)} %bitcast.36, bf16[4,2,320,640]{3,2,1,0:T(8,128)(2,1)} %copy-done, bf16[2,160,640]{2,1,0:T(8,128)(2,1)} %copy-done.6, ...), custom_call_target="tpu_custom_call" | custom-call | flops 1 | bytes 1 | tf_op jit(solution)/shard_map/second_messages/pallas_call | solution.py:338
  66.4 2.7 %collective-permute-start.15 = (bf16[160,640]{1,0:T(8,128)(2,1)}, bf16[160,640]{1,0:T(8,128)(2,1)S(1)}, u32[]{:S(2)}, u32[]{:S(2)}) collective-permute-start(bf16[160,640]{1,0:T(8,128)(2,1)} %get-tuple-element.57), channel_id=1, source_target_pairs={{0,48},{8,56},{16,0},{24,8},{32,16},{40,24},{48,32},{56,40},{64,11... | collective-permute-start | bytes 614408 | tf_op jit(solution)/shard_map/ppermute | solution.py:436
  74.2 3.0 %token_sums.1.refs_0_.unread_ref.parts0 = f32[1,192,128]{2,1,0:T(8,128)} custom-call(f32[1,192,128]{2,1,0:T(8,128)} %get-tuple-element.82.own_ref, f32[1,192,128]{2,1,0:T(8,128)} %copy-done.37, bf16[64,2048]{1,0:T(8,128)(2,1)} %bitcast.49, bf16[64,2048]{1,0:T(8,128)(2,1)} %bitcast.50, f32[640,320]{1,0:T(8,128)} %copy.29.refs_0_.anchor_ref, ...), custom_call_target="tpu_custom_call" | custom-call | flops 1 | bytes 1 | tf_op jit(solution)/shard_map/token_sums/pallas_call | solution.py:665
  78.6 2.5 %chip_sum.2.own_ref = f32[320,640]{1,0:T(8,128)} custom-call(bf16[4,2,320,640]{3,2,1,0:T(8,128)(2,1)} %bitcast.37, bf16[4,2,320,640]{3,2,1,0:T(8,128)(2,1)} %copy-done, bf16[2,160,640]{2,1,0:T(8,128)(2,1)} %copy-done.6, bf16[2,160,640]{2,1,0:T(8,128)(2,1)} %copy-done.7, bf16[160,640]{1,0:T(8,128)(2,1)} %copy-done.31, bf16[160,640]{1,0:T(8,128)(2,1)} %copy-done.32), custom_call_target="tpu_custom_call" | custom-call | flops 1 | bytes 1 | tf_op jit(solution)/shard_map/chip_sum/pallas_call | solution.py:361
  81.8 4.0 %outer_update.1 = (f32[640,320]{1,0:T(8,128)}, f32[640,320]{1,0:T(8,128)}, bf16[320,640]{1,0:T(8,128)(2,1)}) custom-call(s32[3]{0:T(128)} %pad_add_fusion.pos_ref, f32[320,640]{1,0:T(8,128)} %chip_sum.2.own_ref, bf16[320,640]{1,0:T(8,128)(2,1)} %copy-done.19, f32[640,320]{1,0:T(8,128)} %copy.29.refs_0_.anchor_ref, f32[640,320]{1,0:T(8,128)} %copy.30.refs_1_.momentum_ref, ...), custom_call_target="tpu_custom_call" | custom-call | flops 1 | bytes 1 | tf_op jit(solution)/shard_map/outer_update/pallas_call | solution.py:144
  85.9 2.5 %collective-permute-start.19 = (bf16[320,640]{1,0:T(8,128)(2,1)}, bf16[320,640]{1,0:T(8,128)(2,1)S(1)}, u32[]{:S(2)}, u32[]{:S(2)}) collective-permute-start(bf16[320,640]{1,0:T(8,128)(2,1)} %get-tuple-element.59.refs_0_), channel_id=1, source_target_pairs={{0,64},{8,72},{16,80},{24,88},{32,96},{40,104},{48,112},{56,120},{... | collective-permute-start | bytes 1228808 | tf_op jit(solution)/shard_map/ppermute | solution.py:442
  92.4 1.6 %join.6.refs_0_.refs_1_ = f32[2,192,128]{2,1,0:T(8,128)} custom-call(f32[1,192,128]{2,1,0:T(8,128)} %token_sums.1.refs_0_.unread_ref.parts0, f32[1,192,128]{2,1,0:T(8,128)} %copy-done.26), custom_call_target="tpu_custom_call" | custom-call | flops 1 | bytes 1 | tf_op jit(solution)/shard_map/join/pallas_call | solution.py:242
  97.1 5.7 %collective-permute-done.8.refs_1_.parts2 = f32[2,192,128]{2,1,0:T(8,128)S(1)} collective-permute-done((f32[2,192,128]{2,1,0:T(8,128)}, f32[2,192,128]{2,1,0:T(8,128)S(1)}, u32[]{:S(2)}, u32[]{:S(2)}) %collective-permute-start.8) | collective-permute-done | bytes 196640 | tf_op jit(solution)/shard_map/ppermute | solution.py:409
  103.5 1.8 %join.7 = f32[4,192,128]{2,1,0:T(8,128)} custom-call(f32[2,192,128]{2,1,0:T(8,128)} %join.6.refs_0_.refs_1_, f32[2,192,128]{2,1,0:T(8,128)} %copy-done.16), custom_call_target="tpu_custom_call" | custom-call | flops 1 | bytes 1 | tf_op jit(solution)/shard_map/join/pallas_call | solution.py:242
  107.1 1.9 %parts.3 = (bf16[128,640]{1,0:T(8,128)(2,1)}, bf16[192,640]{1,0:T(8,128)(2,1)}) custom-call(bf16[320,640]{1,0:T(8,128)(2,1)} %copy-done.2, bf16[320,640]{1,0:T(8,128)(2,1)} %copy-done.1), custom_call_target="tpu_custom_call" | custom-call | flops 1 | bytes 1 | tf_op jit(solution)/shard_map/parts/pallas_call | solution.py:223
  111.8 1.9 %parts.2 = (bf16[192,640]{1,0:T(8,128)(2,1)}, bf16[128,640]{1,0:T(8,128)(2,1)}) custom-call(bf16[320,640]{1,0:T(8,128)(2,1)} %copy-done.4, bf16[320,640]{1,0:T(8,128)(2,1)} %copy-done.3), custom_call_target="tpu_custom_call" | custom-call | flops 1 | bytes 1 | tf_op jit(solution)/shard_map/parts/pallas_call | solution.py:223
  114.0 2.6 %collective-permute-start.27 = (bf16[128,640]{1,0:T(8,128)(2,1)}, bf16[128,640]{1,0:T(8,128)(2,1)S(1)}, u32[]{:S(2)}, u32[]{:S(2)}) collective-permute-start(bf16[128,640]{1,0:T(8,128)(2,1)} %get-tuple-element.71), channel_id=1, source_target_pairs={{0,48},{8,56},{16,0},{24,8},{32,16},{40,24},{48,32},{56,40},{64,11... | collective-permute-start | bytes 491528 | tf_op jit(solution)/shard_map/ppermute | solution.py:452
  116.6 2.4 %copy.33 = f32[640,320]{0,1:T(8,128)} copy(f32[640,320]{1,0:T(8,128)} %get-tuple-element.65) | data formatting | bytes 1638400 | tf_op jit(solution)/shard_map/outer_update/pallas_call | solution.py:144
  119.0 2.4 %copy.34 = f32[640,320]{0,1:T(8,128)} copy(f32[640,320]{1,0:T(8,128)} %get-tuple-element.66) | data formatting | bytes 1638400 | tf_op jit(solution)/shard_map/outer_update/pallas_call | solution.py:144
  122.8 5.4 %finish.1 = (f32[64,640]{1,0:T(8,128)}, f32[64,640]{1,0:T(8,128)}, f32[2,640]{1,0:T(2,128)}, f32[256,640]{1,0:T(8,128)}) custom-call(f32[1,192,128]{2,1,0:T(8,128)} %token_sums.1.refs_0_.unread_ref.parts0, f32[1,192,128]{2,1,0:T(8,128)} %copy-done.26, f32[2,192,128]{2,1,0:T(8,128)} %copy-done.16, f32[4,192,128]{2,1,0:T(8,128)} %copy-done.28, ...), custom_call_target="tpu_custom_call" | custom-call | flops 1 | bytes 1 | tf_op jit(solution)/shard_map/finish/pallas_call | solution.py:678
  129.1 8.7 %collective-permute-start.28 = (bf16[320,640]{1,0:T(8,128)(2,1)}, bf16[320,640]{1,0:T(8,128)(2,1)S(1)}, u32[]{:S(2)}, u32[]{:S(2)}) collective-permute-start(bf16[320,640]{1,0:T(8,128)(2,1)} %get-tuple-element.73.refs_0_), channel_id=1, source_target_pairs={{0,8},{8,0},{16,24},{24,16},{32,40},{40,32},{48,56},{56,48},{64,72... | collective-permute-start | bytes 1228808 | tf_op jit(solution)/shard_map/ppermute | solution.py:458
  145.6 8.6 %place.1 = bf16[640,5120]{1,0:T(8,128)(2,1)} custom-call(s32[3]{0:T(128)} %pad_add_fusion.pos_ref, bf16[320,640]{1,0:T(8,128)(2,1)} %get-tuple-element.73.refs_0_, bf16[320,640]{1,0:T(8,128)(2,1)} %get-tuple-element.74.refs_1_, bf16[320,640]{1,0:T(8,128)(2,1)} %get-tuple-element.75.refs_2_, bf16[320,640]{1,0:T(8,128)(2,1)} %get-tuple-element.76.refs_3_, ...), custom_call_target="tpu_custom_call" | custom-call | flops 1 | bytes 1 | tf_op jit(solution)/shard_map/place/pallas_call | solution.py:200
  (166 shorter events, 44.9 us)
Async XLA Ops:
  13.0 10.0 %collective-permute-start.2 = (bf16[4,2,320,640]{3,2,1,0:T(8,128)(2,1)}, bf16[4,2,320,640]{3,2,1,0:T(8,128)(2,1)S(1)}, u32[]{:S(2)}, u32[]{:S(2)}) collective-permute-start(bf16[4,2,320,640]{3,2,1,0:T(8,128)(2,1)} %bitcast.54), channel_id=1, source_target_pairs={{0,8},{8,0},{16,24},{24,16},{32,40},{40,32},{48,56},{56,48},{64,72... | collective-permute-start | bytes 9830408 | tf_op jit(solution)/shard_map/ppermute | solution.py:414
  19.5 7.5 %collective-permute-start.1 = (f32[2,16,128]{2,1,0:T(8,128)}, f32[2,16,128]{2,1,0:T(8,128)S(1)}, u32[]{:S(2)}, u32[]{:S(2)}) collective-permute-start(f32[2,16,128]{2,1,0:T(8,128)} %join.4.refs_0_), channel_id=1, source_target_pairs={{0,2},{1,3},{2,0},{3,1},{4,6},{5,7},{6,4},{7,5},{8,10},{9,11},{10,... | collective-permute-start | bytes 49160 | tf_op jit(solution)/shard_map/ppermute | solution.py:409
  29.0 4.0 %collective-permute-start.3 = (f32[4,16,128]{2,1,0:T(8,128)}, f32[4,16,128]{2,1,0:T(8,128)S(1)}, u32[]{:S(2)}, u32[]{:S(2)}) collective-permute-start(f32[4,16,128]{2,1,0:T(8,128)} %join.5.near_heads), channel_id=1, source_target_pairs={{0,4},{1,5},{2,6},{3,7},{4,0},{5,1},{6,2},{7,3},{8,12},{9,13},{10,... | collective-permute-start | bytes 98312 | tf_op jit(solution)/shard_map/ppermute | solution.py:409
  30.3 10.1 %collective-permute-start.11 = (bf16[2,160,640]{2,1,0:T(8,128)(2,1)}, bf16[2,160,640]{2,1,0:T(8,128)(2,1)S(1)}, u32[]{:S(2)}, u32[]{:S(2)}) collective-permute-start(bf16[2,160,640]{2,1,0:T(8,128)(2,1)} %get-tuple-element.52), channel_id=1, source_target_pairs={{0,48},{8,56},{16,0},{24,8},{32,16},{40,24},{48,32},{56,40},{64,11... | collective-permute-start | bytes 1228808 | tf_op jit(solution)/shard_map/ppermute | solution.py:420
  33.0 10.4 %collective-permute-start.10 = (bf16[2,160,640]{2,1,0:T(8,128)(2,1)}, bf16[2,160,640]{2,1,0:T(8,128)(2,1)S(1)}, u32[]{:S(2)}, u32[]{:S(2)}) collective-permute-start(bf16[2,160,640]{2,1,0:T(8,128)(2,1)} %get-tuple-element.46.refs_2_.refs_0_), channel_id=1, source_target_pairs={{0,16},{8,24},{16,32},{24,40},{32,48},{40,56},{48,0},{56,8},{64,80... | collective-permute-start | bytes 1228808 | tf_op jit(solution)/shard_map/ppermute | solution.py:420
  38.5 14.4 %collective-permute-start.4 = (f32[4,192,128]{2,1,0:T(8,128)}, f32[4,192,128]{2,1,0:T(8,128)S(1)}, u32[]{:S(2)}, u32[]{:S(2)}) collective-permute-start(f32[4,192,128]{2,1,0:T(8,128)} %get-tuple-element.48), channel_id=1, source_target_pairs={{0,4},{1,5},{2,6},{3,7},{4,0},{5,1},{6,2},{7,3},{8,12},{9,13},{10,... | collective-permute-start | bytes 1179656 | tf_op jit(solution)/shard_map/ppermute | solution.py:409
  46.3 7.3 %collective-permute-start.17 = (bf16[160,640]{1,0:T(8,128)(2,1)}, bf16[160,640]{1,0:T(8,128)(2,1)S(1)}, u32[]{:S(2)}, u32[]{:S(2)}) collective-permute-start(bf16[160,640]{1,0:T(8,128)(2,1)} %get-tuple-element.58), channel_id=1, source_target_pairs={{0,48},{8,56},{16,0},{24,8},{32,16},{40,24},{48,32},{56,40},{64,11... | collective-permute-start | bytes 614408 | tf_op jit(solution)/shard_map/ppermute | solution.py:432
  47.3 6.3 %collective-permute-start.16 = (bf16[160,640]{1,0:T(8,128)(2,1)}, bf16[160,640]{1,0:T(8,128)(2,1)S(1)}, u32[]{:S(2)}, u32[]{:S(2)}) collective-permute-start(bf16[160,640]{1,0:T(8,128)(2,1)} %get-tuple-element.53.refs_6_), channel_id=1, source_target_pairs={{0,16},{8,24},{16,32},{24,40},{32,48},{40,56},{48,0},{56,8},{64,80... | collective-permute-start | bytes 614408 | tf_op jit(solution)/shard_map/ppermute | solution.py:432
  50.2 12.5 %collective-permute-start.12 = (bf16[2,160,640]{2,1,0:T(8,128)(2,1)}, bf16[2,160,640]{2,1,0:T(8,128)(2,1)S(1)}, u32[]{:S(2)}, u32[]{:S(2)}) collective-permute-start(bf16[2,160,640]{2,1,0:T(8,128)(2,1)} %get-tuple-element.54), channel_id=1, source_target_pairs={{0,16},{8,24},{16,32},{24,40},{32,48},{40,56},{48,0},{56,8},{64,80... | collective-permute-start | bytes 1228808 | tf_op jit(solution)/shard_map/ppermute | solution.py:420
  50.3 12.4 %collective-permute-start.13 = (bf16[2,160,640]{2,1,0:T(8,128)(2,1)}, bf16[2,160,640]{2,1,0:T(8,128)(2,1)S(1)}, u32[]{:S(2)}, u32[]{:S(2)}) collective-permute-start(bf16[2,160,640]{2,1,0:T(8,128)(2,1)} %get-tuple-element.55), channel_id=1, source_target_pairs={{0,48},{8,56},{16,0},{24,8},{32,16},{40,24},{48,32},{56,40},{64,11... | collective-permute-start | bytes 1228808 | tf_op jit(solution)/shard_map/ppermute | solution.py:420
  52.9 16.2 %collective-permute-start.5 = (f32[2,192,128]{2,1,0:T(8,128)S(1)}, f32[2,192,128]{2,1,0:T(8,128)S(1)}, u32[]{:S(2)}, u32[]{:S(2)}) collective-permute-start(f32[2,192,128]{2,1,0:T(8,128)S(1)} %slice_add_fusion), channel_id=1, source_target_pairs={{0,2},{1,3},{2,0},{3,1},{4,6},{5,7},{6,4},{7,5},{8,10},{9,11},{10,... | collective-permute-start | bytes 589832 | tf_op jit(solution)/shard_map/ppermute | solution.py:409
  57.3 23.8 %collective-permute-start.18 = (bf16[320,640]{1,0:T(8,128)(2,1)}, bf16[320,640]{1,0:T(8,128)(2,1)S(1)}, u32[]{:S(2)}, u32[]{:S(2)}) collective-permute-start(bf16[320,640]{1,0:T(8,128)(2,1)} %chip_sum.3), channel_id=1, source_target_pairs={{0,64},{8,72},{16,80},{24,88},{32,96},{40,104},{48,112},{56,120},{... | collective-permute-start | bytes 1228808 | tf_op jit(solution)/shard_map/ppermute | solution.py:434
  66.4 10.8 %collective-permute-start.14 = (bf16[160,640]{1,0:T(8,128)(2,1)}, bf16[160,640]{1,0:T(8,128)(2,1)S(1)}, u32[]{:S(2)}, u32[]{:S(2)}) collective-permute-start(bf16[160,640]{1,0:T(8,128)(2,1)} %get-tuple-element.56), channel_id=1, source_target_pairs={{0,16},{8,24},{16,32},{24,40},{32,48},{40,56},{48,0},{56,8},{64,80... | collective-permute-start | bytes 614408 | tf_op jit(solution)/shard_map/ppermute | solution.py:436
  66.4 10.8 %collective-permute-start.15 = (bf16[160,640]{1,0:T(8,128)(2,1)}, bf16[160,640]{1,0:T(8,128)(2,1)S(1)}, u32[]{:S(2)}, u32[]{:S(2)}) collective-permute-start(bf16[160,640]{1,0:T(8,128)(2,1)} %get-tuple-element.57), channel_id=1, source_target_pairs={{0,48},{8,56},{16,0},{24,8},{32,16},{40,24},{48,32},{56,40},{64,11... | collective-permute-start | bytes 614408 | tf_op jit(solution)/shard_map/ppermute | solution.py:436
  69.8 3.8 %collective-permute-start.6 = (f32[1,192,128]{2,1,0:T(8,128)S(1)}, f32[1,192,128]{2,1,0:T(8,128)S(1)}, u32[]{:S(2)}, u32[]{:S(2)}) collective-permute-start(f32[1,192,128]{2,1,0:T(8,128)S(1)} %get-tuple-element.81), channel_id=1, source_target_pairs={{0,1},{1,0},{2,3},{3,2},{4,5},{5,4},{6,7},{7,6},{8,9},{9,8},{10,11... | collective-permute-start | bytes 294920 | tf_op jit(solution)/shard_map/ppermute | solution.py:409
  85.9 8.5 %collective-permute-start.19 = (bf16[320,640]{1,0:T(8,128)(2,1)}, bf16[320,640]{1,0:T(8,128)(2,1)S(1)}, u32[]{:S(2)}, u32[]{:S(2)}) collective-permute-start(bf16[320,640]{1,0:T(8,128)(2,1)} %get-tuple-element.59.refs_0_), channel_id=1, source_target_pairs={{0,64},{8,72},{16,80},{24,88},{32,96},{40,104},{48,112},{56,120},{... | collective-permute-start | bytes 1228808 | tf_op jit(solution)/shard_map/ppermute | solution.py:442
  88.3 3.5 %collective-permute-start.7 = (f32[1,192,128]{2,1,0:T(8,128)S(1)}, f32[1,192,128]{2,1,0:T(8,128)S(1)}, u32[]{:S(2)}, u32[]{:S(2)}) collective-permute-start(f32[1,192,128]{2,1,0:T(8,128)S(1)} %copy-done.10), channel_id=1, source_target_pairs={{0,1},{1,0},{2,3},{3,2},{4,5},{5,4},{6,7},{7,6},{8,9},{9,8},{10,11... | collective-permute-start | bytes 294920 | tf_op jit(solution)/shard_map/ppermute | solution.py:409
  89.1 16.5 %collective-permute-start.23 = (bf16[320,640]{1,0:T(8,128)(2,1)}, bf16[320,640]{1,0:T(8,128)(2,1)S(1)}, u32[]{:S(2)}, u32[]{:S(2)}) collective-permute-start(bf16[320,640]{1,0:T(8,128)(2,1)} %get-tuple-element.59.refs_0_), channel_id=1, source_target_pairs={{0,48},{8,56},{16,0},{24,8},{32,16},{40,24},{48,32},{56,40},{64,11... | collective-permute-start | bytes 1228808 | tf_op jit(solution)/shard_map/ppermute | solution.py:443
  89.1 16.5 %collective-permute-start.22 = (bf16[320,640]{1,0:T(8,128)(2,1)}, bf16[320,640]{1,0:T(8,128)(2,1)S(1)}, u32[]{:S(2)}, u32[]{:S(2)}) collective-permute-start(bf16[320,640]{1,0:T(8,128)(2,1)} %get-tuple-element.59.refs_0_), channel_id=1, source_target_pairs={{0,16},{8,24},{16,32},{24,40},{32,48},{40,56},{48,0},{56,8},{64,80... | collective-permute-start | bytes 1228808 | tf_op jit(solution)/shard_map/ppermute | solution.py:443
  95.2 15.1 %collective-permute-start.21 = (bf16[320,640]{1,0:T(8,128)(2,1)}, bf16[320,640]{1,0:T(8,128)(2,1)S(1)}, u32[]{:S(2)}, u32[]{:S(2)}) collective-permute-start(bf16[320,640]{1,0:T(8,128)(2,1)} %gate.2.refs_3_), channel_id=1, source_target_pairs={{0,48},{8,56},{16,0},{24,8},{32,16},{40,24},{48,32},{56,40},{64,11... | collective-permute-start | bytes 1228808 | tf_op jit(solution)/shard_map/ppermute | solution.py:450
  95.2 15.1 %collective-permute-start.20 = (bf16[320,640]{1,0:T(8,128)(2,1)}, bf16[320,640]{1,0:T(8,128)(2,1)S(1)}, u32[]{:S(2)}, u32[]{:S(2)}) collective-permute-start(bf16[320,640]{1,0:T(8,128)(2,1)} %gate.2.refs_3_), channel_id=1, source_target_pairs={{0,16},{8,24},{16,32},{24,40},{32,48},{40,56},{48,0},{56,8},{64,80... | collective-permute-start | bytes 1228808 | tf_op jit(solution)/shard_map/ppermute | solution.py:450
  96.6 6.2 %collective-permute-start.8 = (f32[2,192,128]{2,1,0:T(8,128)}, f32[2,192,128]{2,1,0:T(8,128)S(1)}, u32[]{:S(2)}, u32[]{:S(2)}) collective-permute-start(f32[2,192,128]{2,1,0:T(8,128)} %join.6.refs_0_.refs_1_), channel_id=1, source_target_pairs={{0,2},{1,3},{2,0},{3,1},{4,6},{5,7},{6,4},{7,5},{8,10},{9,11},{10,... | collective-permute-start | bytes 589832 | tf_op jit(solution)/shard_map/ppermute | solution.py:409
  105.3 16.7 %collective-permute-start.9 = (f32[4,192,128]{2,1,0:T(8,128)}, f32[4,192,128]{2,1,0:T(8,128)S(1)}, u32[]{:S(2)}, u32[]{:S(2)}) collective-permute-start(f32[4,192,128]{2,1,0:T(8,128)} %join.7), channel_id=1, source_target_pairs={{0,4},{1,5},{2,6},{3,7},{4,0},{5,1},{6,2},{7,3},{8,12},{9,13},{10,... | collective-permute-start | bytes 1179656 | tf_op jit(solution)/shard_map/ppermute | solution.py:409
  109.0 19.2 %collective-permute-start.25 = (bf16[192,640]{1,0:T(8,128)(2,1)}, bf16[192,640]{1,0:T(8,128)(2,1)S(1)}, u32[]{:S(2)}, u32[]{:S(2)}) collective-permute-start(bf16[192,640]{1,0:T(8,128)(2,1)} %get-tuple-element.70), channel_id=1, source_target_pairs={{0,48},{8,56},{16,0},{24,8},{32,16},{40,24},{48,32},{56,40},{64,11... | collective-permute-start | bytes 737288 | tf_op jit(solution)/shard_map/ppermute | solution.py:448
  113.7 14.6 %collective-permute-start.26 = (bf16[192,640]{1,0:T(8,128)(2,1)}, bf16[192,640]{1,0:T(8,128)(2,1)S(1)}, u32[]{:S(2)}, u32[]{:S(2)}) collective-permute-start(bf16[192,640]{1,0:T(8,128)(2,1)} %get-tuple-element.60.refs_0_.unread_ref), channel_id=1, source_target_pairs={{0,16},{8,24},{16,32},{24,40},{32,48},{40,56},{48,0},{56,8},{64,80... | collective-permute-start | bytes 737288 | tf_op jit(solution)/shard_map/ppermute | solution.py:452
  113.9 14.3 %collective-permute-start.24 = (bf16[128,640]{1,0:T(8,128)(2,1)}, bf16[128,640]{1,0:T(8,128)(2,1)S(1)}, u32[]{:S(2)}, u32[]{:S(2)}) collective-permute-start(bf16[128,640]{1,0:T(8,128)(2,1)} %get-tuple-element.69), channel_id=1, source_target_pairs={{0,16},{8,24},{16,32},{24,40},{32,48},{40,56},{48,0},{56,8},{64,80... | collective-permute-start | bytes 491528 | tf_op jit(solution)/shard_map/ppermute | solution.py:448
  114.0 14.3 %collective-permute-start.27 = (bf16[128,640]{1,0:T(8,128)(2,1)}, bf16[128,640]{1,0:T(8,128)(2,1)S(1)}, u32[]{:S(2)}, u32[]{:S(2)}) collective-permute-start(bf16[128,640]{1,0:T(8,128)(2,1)} %get-tuple-element.71), channel_id=1, source_target_pairs={{0,48},{8,56},{16,0},{24,8},{32,16},{40,24},{48,32},{56,40},{64,11... | collective-permute-start | bytes 491528 | tf_op jit(solution)/shard_map/ppermute | solution.py:452
  129.1 12.4 %collective-permute-start.28 = (bf16[320,640]{1,0:T(8,128)(2,1)}, bf16[320,640]{1,0:T(8,128)(2,1)S(1)}, u32[]{:S(2)}, u32[]{:S(2)}) collective-permute-start(bf16[320,640]{1,0:T(8,128)(2,1)} %get-tuple-element.73.refs_0_), channel_id=1, source_target_pairs={{0,8},{8,0},{16,24},{24,16},{32,40},{40,32},{48,56},{56,48},{64,72... | collective-permute-start | bytes 1228808 | tf_op jit(solution)/shard_map/ppermute | solution.py:458
  137.8 3.1 %collective-permute-start.36 = (bf16[192,640]{1,0:T(8,128)(2,1)}, bf16[192,640]{1,0:T(8,128)(2,1)S(1)}, u32[]{:S(2)}, u32[]{:S(2)}) collective-permute-start(bf16[192,640]{1,0:T(8,128)(2,1)} %copy-done.12), channel_id=1, source_target_pairs={{0,8},{8,0},{16,24},{24,16},{32,40},{40,32},{48,56},{56,48},{64,72... | collective-permute-start | bytes 737288 | tf_op jit(solution)/shard_map/ppermute | solution.py:458
  137.8 3.4 %collective-permute-start.35 = (bf16[192,640]{1,0:T(8,128)(2,1)}, bf16[192,640]{1,0:T(8,128)(2,1)S(1)}, u32[]{:S(2)}, u32[]{:S(2)}) collective-permute-start(bf16[192,640]{1,0:T(8,128)(2,1)} %get-tuple-element.80.refs_7_), channel_id=1, source_target_pairs={{0,8},{8,0},{16,24},{24,16},{32,40},{40,32},{48,56},{56,48},{64,72... | collective-permute-start | bytes 737288 | tf_op jit(solution)/shard_map/ppermute | solution.py:458
  141.2 2.8 %collective-permute-start.32 = (bf16[320,640]{1,0:T(8,128)(2,1)}, bf16[320,640]{1,0:T(8,128)(2,1)S(1)}, u32[]{:S(2)}, u32[]{:S(2)}) collective-permute-start(bf16[320,640]{1,0:T(8,128)(2,1)} %get-tuple-element.77.refs_4_), channel_id=1, source_target_pairs={{0,8},{8,0},{16,24},{24,16},{32,40},{40,32},{48,56},{56,48},{64,72... | collective-permute-start | bytes 1228808 | tf_op jit(solution)/shard_map/ppermute | solution.py:458
  141.5 3.2 %collective-permute-start.33 = (bf16[320,640]{1,0:T(8,128)(2,1)}, bf16[320,640]{1,0:T(8,128)(2,1)S(1)}, u32[]{:S(2)}, u32[]{:S(2)}) collective-permute-start(bf16[320,640]{1,0:T(8,128)(2,1)} %get-tuple-element.78.refs_5_), channel_id=1, source_target_pairs={{0,8},{8,0},{16,24},{24,16},{32,40},{40,32},{48,56},{56,48},{64,72... | collective-permute-start | bytes 1228808 | tf_op jit(solution)/shard_map/ppermute | solution.py:458
  (49 other events, 134.8 us)

commit v4 on v3

--- a/solution.py
+++ b/solution.py
@@ -324,12 +324,13 @@
     )(keep, got, keep, got, keep, got, *after)
 
 
-def second_kernel(keep1, got1, keep3, got3, up, down, up_out, down_out):
+def second_kernel(keep1, got1, keep3, got3, up, down, *refs):
+    up_out, down_out = refs[-2:]
     up_out[...] = total(keep1[0, 0], got1[0, 0], up[0]).astype(bf16)
     down_out[...] = total(keep3[0, 0], got3[0, 0], down[0]).astype(bf16)
 
 
-def second_messages(keep, got, up, down, x):
+def second_messages(keep, got, up, down, x, after):
     _, _, rows, columns = keep.shape
     half = rows // 2
     came = pl.BlockSpec((1, half, columns), lambda i: (0, 0, 0))
@@ -338,13 +339,13 @@
     return pl.pallas_call(
         second_kernel,
         grid=(1,),
-        in_specs=[spot(1, x, half, columns, 0)] * 2 + [spot(3, x, half, columns, 1)] * 2 + [came] * 2,
+        in_specs=[spot(1, x, half, columns, 0)] * 2 + [spot(3, x, half, columns, 1)] * 2 + [came] * 2 + [unread] * len(after),
         out_specs=[part] * 2,
         out_shape=[shape] * 2,
         compiler_params=limit,
         cost_estimate=brief,
         name="second_messages",
-    )(keep, got, keep, got, up, down)
+    )(keep, got, keep, got, up, down, *after)
 
 
 def chip_kernel(keep, got, up, down, up2, down2, out):
@@ -428,13 +429,13 @@
     away2 = across(near[2:4] + away[2:4], 2)
     away1 = across(near[1:2] + away[1:2] + away2[1:2], 1)
 
-    far = second_messages(keep, got, up[1], down[1], 1)
+    far = second_messages(keep, got, up[1], down[1], 1, [])
     far_up, far_down = send(far[0], perm=to_y(1)), send(far[1], perm=to_y(-1))
     ring(0, first_messages(keep, got, 0, [far[0]]))
     far = send(chip_sum(keep, got, up[1], down[1], far_up, far_down, 1, bf16), perm=to_x)
-    own = second_messages(keep, got, up[0], down[0], 0)
+    own = second_messages(keep, got, up[0], down[0], 0, [anchor, momentum])
     own_up, own_down = send(own[0], perm=to_y(1)), send(own[1], perm=to_y(-1))
-    q0 = token_sums(near[0:1] + away[0:1] + away2[0:1], away1, latents.T, target.T, [anchor, momentum], width, tokens)
+    q0 = token_sums(near[0:1] + away[0:1] + away2[0:1], away1, latents.T, target.T, [], width, tokens)
     q1 = across(q0, 1)
     own = chip_sum(keep, got, up[0], down[0], own_up, own_down, 0, f32)
     new_anchor, new_momentum, n0 = outer_update(pos, own, far, anchor, momentum, q0)
@@ -443,7 +444,8 @@
     up0, down0 = send(n0, perm=to_y(1)), send(n0, perm=to_y(-1))
     q01 = join([q0, q1], [])
     q2 = across(q01, 2)
-    q4 = across(join([q01, q2], []), 4)
+    anchor_t, momentum_t, settled = settle(new_anchor.T, new_momentum.T, q01)
+    q4 = across(join([q01, q2], [settled]), 4)
     first0 = parts(up0, down0, 2)
     on0 = send(first0[0], perm=to_y(1)), send(first0[1], perm=to_y(-1))
     (n1,) = gate([n1], [q01])
@@ -451,7 +453,6 @@
     first1 = parts(up1, down1, 3)
     on1 = send(first1[0], perm=to_y(1)), send(first1[1], perm=to_y(-1))
     inner = finish(q0, q1, q2, q4, pre, center, sines, params, [first1[0]])
-    anchor_t, momentum_t, settled = settle(new_anchor.T, new_momentum.T, first1[0])
     mine = [n0, up0, down0, n1, up1, down1, *on0]
     mine = gate(mine, [*on1, inner[2], settled])
     mine = [*mine, *on1]

time: 155 us -> 152 us (0.981)
  waiting for transfers between devices: 20.8 us -> 14.5 us
  starting transfers between devices: 43.6 us -> 46 us
    ppermute x9, waiting for transfers between devices: 8.44 us -> 5.03 us  [across(): return lax.ppermute(value, 'fsdp', [(i, i ^ bit) for i in range(N_FSDP)])]
    ppermute x2, waiting for transfers between devices: 6 us -> 3.03 us  [ring(): send(messages[0], perm=to_y(1))]
    ppermute x9, starting transfers between devices: 9.54 us -> 11.1 us  [across(): return lax.ppermute(value, 'fsdp', [(i, i ^ bit) for i in range(N_FSDP)])]
    unnamed x88 -> x92, local copies, waits for them, and re-layouts: 20.1 us -> 20.2 us
  transfers between devices with their start and end apart: 38 -> 38, of which waited for: 14 -> 12; matrix products, arithmetic and copies ran while one was open for 6% -> 6% of each run, Pallas kernels for 24% -> 24%
where the time goes in v4:
time: 152 us; the launch traced here: 151 us
  Pallas kernels  62.2 us (41%)
  starting transfers between devices  46 us (30%)
  local copies, waits for them, and re-layouts  25.1 us (17%)
  waiting for transfers between devices  14.5 us (10%)
  other arithmetic  2.37 us (2%)
    unnamed x92, local copies, waits for them, and re-layouts  20.2 us
    ppermute x10, starting transfers between devices, per_device(): theirs = [to_sibling(part) for part in mine]  12.1 us
    pallas_call x1, Pallas kernels, quantize(): pl.pallas_call(quant_kernel, grid_spec=pltpu.PrefetchScalarGridSpec(num_s...  11.7 us
    ppermute x9, starting transfers between devices, across(): return lax.ppermute(value, 'fsdp', [(i, i ^ bit) for i in range(N_FSDP)])  11.1 us
    pallas_call x1, Pallas kernels, place(): pl.pallas_call(functools.partial(place_kernel, chips), grid_spec=pltpu.Pr...  8.57 us
    pallas_call x4, Pallas kernels, join(): pl.pallas_call(functools.partial(join_kernel, len(after)), in_specs=[pl.B...  6.1 us
    pallas_call x1, Pallas kernels, finish(): pl.pallas_call(functools.partial(finish_kernel, len(after)), in_specs=[pl...  5.44 us
    ppermute x2, starting transfers between devices, ring(): send(messages[1], perm=to_y(-1))  5.37 us
  transfers between devices with their start and end apart: 38, of which 12 were waited for; matrix products, arithmetic and copies ran while one was open for 6% of the time, Pallas kernels for 24%

profile of v4, /device:TPU:1, one launch (start us, length us, event | category | flops | bytes accessed | tf_op | source)
XLA Modules:
  0.0 151.3 jit_solution(59784396972946449)
XLA Ops:
  1.3 11.7 %quantize.1 = (bf16[8,320,640]{2,1,0:T(8,128)(2,1)}, bf16[8,320,640]{2,1,0:T(8,128)(2,1)}) custom-call(s32[3]{0:T(128)} %pad_add_fusion.pos_ref, bf16[640,5120]{1,0:T(8,128)(2,1)} %start_ref.1, bf16[640,5120]{1,0:T(8,128)(2,1)} %bitcast.38), custom_call_target="tpu_custom_call" | custom-call | flops 1 | bytes 1 | tf_op jit(solution)/shard_map/quantize/pallas_call | solution.py:89
  14.8 1.8 %collective-permute-start = (f32[1,16,128]{2,1,0:T(8,128)S(1)}, f32[1,16,128]{2,1,0:T(8,128)S(1)}, u32[]{:S(2)}, u32[]{:S(2)}) collective-permute-start(f32[1,16,128]{2,1,0:T(8,128)S(1)} %maximum_bitcast_fusion.refs_0_), channel_id=1, source_target_pairs={{0,1},{1,0},{2,3},{3,2},{4,5},{5,4},{6,7},{7,6},{8,9},{9,8},{10,11... | collective-permute-start | bytes 24584 | tf_op jit(solution)/shard_map/ppermute | solution.py:410
  19.6 3.4 %collective-permute-start.1 = (f32[2,16,128]{2,1,0:T(8,128)}, f32[2,16,128]{2,1,0:T(8,128)S(1)}, u32[]{:S(2)}, u32[]{:S(2)}) collective-permute-start(f32[2,16,128]{2,1,0:T(8,128)} %join.4.refs_0_), channel_id=1, source_target_pairs={{0,2},{1,3},{2,0},{3,1},{4,6},{5,7},{6,4},{7,5},{8,10},{9,11},{10,... | collective-permute-start | bytes 49160 | tf_op jit(solution)/shard_map/ppermute | solution.py:410
  23.0 1.7 %copy-done = bf16[4,2,320,640]{3,2,1,0:T(8,128)(2,1)} copy-done((bf16[4,2,320,640]{3,2,1,0:T(8,128)(2,1)}, bf16[4,2,320,640]{3,2,1,0:T(8,128)(2,1)S(1)}, u32[]{:S(2)}) %copy-start) | copy-done | bytes 3276824
  24.7 2.4 %first_messages.2 = (bf16[2,160,640]{2,1,0:T(8,128)(2,1)}, bf16[2,160,640]{2,1,0:T(8,128)(2,1)}) custom-call(bf16[4,2,320,640]{3,2,1,0:T(8,128)(2,1)} %bitcast.26, bf16[4,2,320,640]{3,2,1,0:T(8,128)(2,1)} %copy-done, bf16[4,2,320,640]{3,2,1,0:T(8,128)(2,1)} %bitcast.27, bf16[4,2,320,640]{3,2,1,0:T(8,128)(2,1)} %copy-done, bf16[4,2,320,640]{3,2,1,0:T(8,128)(2,1)} %bitcast.28, ...), custom_call_target="tpu_custom_call" | custom-call | flops 1 | bytes 1 | tf_op jit(solution)/shard_map/first_messages/pallas_call | solution.py:312
  30.3 2.7 %collective-permute-start.10 = (bf16[2,160,640]{2,1,0:T(8,128)(2,1)}, bf16[2,160,640]{2,1,0:T(8,128)(2,1)S(1)}, u32[]{:S(2)}, u32[]{:S(2)}) collective-permute-start(bf16[2,160,640]{2,1,0:T(8,128)(2,1)} %get-tuple-element.49), channel_id=1, source_target_pairs={{0,48},{8,56},{16,0},{24,8},{32,16},{40,24},{48,32},{56,40},{64,11... | collective-permute-start | bytes 1228808 | tf_op jit(solution)/shard_map/ppermute | solution.py:421
  33.6 4.9 %weight_products.1 = (f32[4,192,128]{2,1,0:T(8,128)}, f32[4,192,128]{2,1,0:T(8,128)}, f32[32,640]{1,0:T(8,128)}, f32[64,640]{1,0:T(8,128)}, f32[32,256]{1,0:T(8,128)}) custom-call(f32[4,16,128]{2,1,0:T(8,128)} %join.5.near_heads, f32[4,16,128]{2,1,0:T(8,128)} %copy-done.41, f32[64,640]{1,0:T(8,128)} %bitcast.45, f32[64,640]{1,0:T(8,128)} %bitcast.47, ...), custom_call_target="tpu_custom_call" | custom-call | flops 1 | bytes 1 | tf_op jit(solution)/shard_map/weight_products/pallas_call | solution.py:648
  38.8 1.6 %collective-permute-done.10.down = bf16[2,160,640]{2,1,0:T(8,128)(2,1)S(1)} collective-permute-done((bf16[2,160,640]{2,1,0:T(8,128)(2,1)}, bf16[2,160,640]{2,1,0:T(8,128)(2,1)S(1)}, u32[]{:S(2)}, u32[]{:S(2)}) %collective-permute-start.10) | collective-permute-done | bytes 409632 | tf_op jit(solution)/shard_map/ppermute | solution.py:421
  40.4 3.0 %collective-permute-done.9.up = bf16[2,160,640]{2,1,0:T(8,128)(2,1)S(1)} collective-permute-done((bf16[2,160,640]{2,1,0:T(8,128)(2,1)}, bf16[2,160,640]{2,1,0:T(8,128)(2,1)S(1)}, u32[]{:S(2)}, u32[]{:S(2)}) %collective-permute-start.9) | collective-permute-done | bytes 409632 | tf_op jit(solution)/shard_map/ppermute | solution.py:421
  44.1 2.2 %second_messages.2 = (bf16[160,640]{1,0:T(8,128)(2,1)}, bf16[160,640]{1,0:T(8,128)(2,1)}) custom-call(bf16[4,2,320,640]{3,2,1,0:T(8,128)(2,1)} %bitcast.29, bf16[4,2,320,640]{3,2,1,0:T(8,128)(2,1)} %copy-done, bf16[4,2,320,640]{3,2,1,0:T(8,128)(2,1)} %bitcast.30, bf16[4,2,320,640]{3,2,1,0:T(8,128)(2,1)} %copy-done, bf16[2,160,640]{2,1,0:T(8,128)(2,1)} %copy-done.9, ...), custom_call_target="tpu_custom_call" | custom-call | flops 1 | bytes 1 | tf_op jit(solution)/shard_map/second_messages/pallas_call | solution.py:339
  47.8 2.4 %first_messages.3 = (bf16[2,160,640]{2,1,0:T(8,128)(2,1)}, bf16[2,160,640]{2,1,0:T(8,128)(2,1)}) custom-call(bf16[4,2,320,640]{3,2,1,0:T(8,128)(2,1)} %bitcast.31, bf16[4,2,320,640]{3,2,1,0:T(8,128)(2,1)} %copy-done, bf16[4,2,320,640]{3,2,1,0:T(8,128)(2,1)} %bitcast.32, bf16[4,2,320,640]{3,2,1,0:T(8,128)(2,1)} %copy-done, bf16[4,2,320,640]{3,2,1,0:T(8,128)(2,1)} %bitcast.33, ...), custom_call_target="tpu_custom_call" | custom-call | flops 1 | bytes 1 | tf_op jit(solution)/shard_map/first_messages/pallas_call | solution.py:312
  50.3 2.6 %collective-permute-start.12 = (bf16[2,160,640]{2,1,0:T(8,128)(2,1)}, bf16[2,160,640]{2,1,0:T(8,128)(2,1)S(1)}, u32[]{:S(2)}, u32[]{:S(2)}) collective-permute-start(bf16[2,160,640]{2,1,0:T(8,128)(2,1)} %get-tuple-element.52), channel_id=1, source_target_pairs={{0,48},{8,56},{16,0},{24,8},{32,16},{40,24},{48,32},{56,40},{64,11... | collective-permute-start | bytes 1228808 | tf_op jit(solution)/shard_map/ppermute | solution.py:421
  55.7 2.4 %chip_sum.3 = bf16[320,640]{1,0:T(8,128)(2,1)} custom-call(bf16[4,2,320,640]{3,2,1,0:T(8,128)(2,1)} %bitcast.34, bf16[4,2,320,640]{3,2,1,0:T(8,128)(2,1)} %copy-done, bf16[2,160,640]{2,1,0:T(8,128)(2,1)} %copy-done.9, bf16[2,160,640]{2,1,0:T(8,128)(2,1)} %copy-done.8, bf16[160,640]{1,0:T(8,128)(2,1)} %copy-done.36, bf16[160,640]{1,0:T(8,128)(2,1)} %copy-done.34), custom_call_target="tpu_custom_call" | custom-call | flops 1 | bytes 1 | tf_op jit(solution)/shard_map/chip_sum/pallas_call | solution.py:362
  58.0 2.5 %collective-permute-start.17 = (bf16[320,640]{1,0:T(8,128)(2,1)}, bf16[320,640]{1,0:T(8,128)(2,1)S(1)}, u32[]{:S(2)}, u32[]{:S(2)}) collective-permute-start(bf16[320,640]{1,0:T(8,128)(2,1)} %chip_sum.3), channel_id=1, source_target_pairs={{0,64},{8,72},{16,80},{24,88},{32,96},{40,104},{48,112},{56,120},{... | collective-permute-start | bytes 1228808 | tf_op jit(solution)/shard_map/ppermute | solution.py:435
  64.6 2.2 %second_messages.3 = (bf16[160,640]{1,0:T(8,128)(2,1)}, bf16[160,640]{1,0:T(8,128)(2,1)}) custom-call(bf16[4,2,320,640]{3,2,1,0:T(8,128)(2,1)} %bitcast.35, bf16[4,2,320,640]{3,2,1,0:T(8,128)(2,1)} %copy-done, bf16[4,2,320,640]{3,2,1,0:T(8,128)(2,1)} %bitcast.36, bf16[4,2,320,640]{3,2,1,0:T(8,128)(2,1)} %copy-done, bf16[2,160,640]{2,1,0:T(8,128)(2,1)} %copy-done.6, ...), custom_call_target="tpu_custom_call" | custom-call | flops 1 | bytes 1 | tf_op jit(solution)/shard_map/second_messages/pallas_call | solution.py:339
  66.9 2.7 %collective-permute-start.14 = (bf16[160,640]{1,0:T(8,128)(2,1)}, bf16[160,640]{1,0:T(8,128)(2,1)S(1)}, u32[]{:S(2)}, u32[]{:S(2)}) collective-permute-start(bf16[160,640]{1,0:T(8,128)(2,1)} %get-tuple-element.54), channel_id=1, source_target_pairs={{0,48},{8,56},{16,0},{24,8},{32,16},{40,24},{48,32},{56,40},{64,11... | collective-permute-start | bytes 614408 | tf_op jit(solution)/shard_map/ppermute | solution.py:437
  70.9 2.7 %collective-permute-done.6.away_ref = f32[1,192,128]{2,1,0:T(8,128)S(1)} collective-permute-done((f32[1,192,128]{2,1,0:T(8,128)S(1)}, f32[1,192,128]{2,1,0:T(8,128)S(1)}, u32[]{:S(2)}, u32[]{:S(2)}) %collective-permute-start.6) | collective-permute-done | bytes 98336 | tf_op jit(solution)/shard_map/ppermute | solution.py:410
  74.3 3.0 %token_sums.1.refs_0_.unread_ref.parts0 = f32[1,192,128]{2,1,0:T(8,128)} custom-call(f32[1,192,128]{2,1,0:T(8,128)} %get-tuple-element.82.own_ref, f32[1,192,128]{2,1,0:T(8,128)} %copy-done.39, bf16[64,2048]{1,0:T(8,128)(2,1)} %bitcast.49, bf16[64,2048]{1,0:T(8,128)(2,1)} %bitcast.50), custom_call_target="tpu_custom_call" | custom-call | flops 1 | bytes 1 | tf_op jit(solution)/shard_map/token_sums/pallas_call | solution.py:666
  78.7 2.5 %chip_sum.2.own_ref = f32[320,640]{1,0:T(8,128)} custom-call(bf16[4,2,320,640]{3,2,1,0:T(8,128)(2,1)} %bitcast.37, bf16[4,2,320,640]{3,2,1,0:T(8,128)(2,1)} %copy-done, bf16[2,160,640]{2,1,0:T(8,128)(2,1)} %copy-done.6, bf16[2,160,640]{2,1,0:T(8,128)(2,1)} %copy-done.7, bf16[160,640]{1,0:T(8,128)(2,1)} %copy-done.33, bf16[160,640]{1,0:T(8,128)(2,1)} %copy-done.35), custom_call_target="tpu_custom_call" | custom-call | flops 1 | bytes 1 | tf_op jit(solution)/shard_map/chip_sum/pallas_call | solution.py:362
  81.9 4.0 %outer_update.1 = (f32[640,320]{1,0:T(8,128)}, f32[640,320]{1,0:T(8,128)}, bf16[320,640]{1,0:T(8,128)(2,1)}) custom-call(s32[3]{0:T(128)} %pad_add_fusion.pos_ref, f32[320,640]{1,0:T(8,128)} %chip_sum.2.own_ref, bf16[320,640]{1,0:T(8,128)(2,1)} %copy-done.19, f32[640,320]{1,0:T(8,128)} %copy.29.refs_0_.anchor_ref, f32[640,320]{1,0:T(8,128)} %copy.30.refs_1_.momentum_ref, ...), custom_call_target="tpu_custom_call" | custom-call | flops 1 | bytes 1 | tf_op jit(solution)/shard_map/outer_update/pallas_call | solution.py:144
  86.0 2.3 %collective-permute-start.19 = (bf16[320,640]{1,0:T(8,128)(2,1)}, bf16[320,640]{1,0:T(8,128)(2,1)S(1)}, u32[]{:S(2)}, u32[]{:S(2)}) collective-permute-start(bf16[320,640]{1,0:T(8,128)(2,1)} %get-tuple-element.62.refs_0_), channel_id=1, source_target_pairs={{0,64},{8,72},{16,80},{24,88},{32,96},{40,104},{48,112},{56,120},{... | collective-permute-start | bytes 1228808 | tf_op jit(solution)/shard_map/ppermute | solution.py:443
  92.4 1.6 %join.6.unread_ref.refs_0_.refs_1_ = f32[2,192,128]{2,1,0:T(8,128)} custom-call(f32[1,192,128]{2,1,0:T(8,128)} %token_sums.1.refs_0_.unread_ref.parts0, f32[1,192,128]{2,1,0:T(8,128)} %copy-done.26), custom_call_target="tpu_custom_call" | custom-call | flops 1 | bytes 1 | tf_op jit(solution)/shard_map/join/pallas_call | solution.py:242
  96.7 2.4 %collective-permute-start.8 = (f32[2,192,128]{2,1,0:T(8,128)}, f32[2,192,128]{2,1,0:T(8,128)S(1)}, u32[]{:S(2)}, u32[]{:S(2)}) collective-permute-start(f32[2,192,128]{2,1,0:T(8,128)} %join.6.unread_ref.refs_0_.refs_1_), channel_id=1, source_target_pairs={{0,2},{1,3},{2,0},{3,1},{4,6},{5,7},{6,4},{7,5},{8,10},{9,11},{10,... | collective-permute-start | bytes 589832 | tf_op jit(solution)/shard_map/ppermute | solution.py:410
  99.1 2.4 %copy.33 = f32[640,320]{0,1:T(8,128)} copy(f32[640,320]{1,0:T(8,128)} %get-tuple-element.56) | data formatting | bytes 1638400 | tf_op jit(solution)/shard_map/outer_update/pallas_call | solution.py:144
  101.5 2.4 %copy.34 = f32[640,320]{0,1:T(8,128)} copy(f32[640,320]{1,0:T(8,128)} %get-tuple-element.57) | data formatting | bytes 1638400 | tf_op jit(solution)/shard_map/outer_update/pallas_call | solution.py:144
  105.2 1.8 %join.7 = f32[4,192,128]{2,1,0:T(8,128)} custom-call(f32[2,192,128]{2,1,0:T(8,128)} %join.6.unread_ref.refs_0_.refs_1_, f32[2,192,128]{2,1,0:T(8,128)} %copy-done.16, f32[8,128]{1,0:T(8,128)} %get-tuple-element.58.refs_2_.refs_11_.refs_21_), custom_call_target="tpu_custom_call" | custom-call | flops 1 | bytes 1 | tf_op jit(solution)/shard_map/join/pallas_call | solution.py:242
  108.6 1.9 %parts.3 = (bf16[128,640]{1,0:T(8,128)(2,1)}, bf16[192,640]{1,0:T(8,128)(2,1)}) custom-call(bf16[320,640]{1,0:T(8,128)(2,1)} %copy-done.2, bf16[320,640]{1,0:T(8,128)(2,1)} %copy-done.1), custom_call_target="tpu_custom_call" | custom-call | flops 1 | bytes 1 | tf_op jit(solution)/shard_map/parts/pallas_call | solution.py:223
  113.2 1.9 %parts.2 = (bf16[192,640]{1,0:T(8,128)(2,1)}, bf16[128,640]{1,0:T(8,128)(2,1)}) custom-call(bf16[320,640]{1,0:T(8,128)(2,1)} %copy-done.4, bf16[320,640]{1,0:T(8,128)(2,1)} %copy-done.3), custom_call_target="tpu_custom_call" | custom-call | flops 1 | bytes 1 | tf_op jit(solution)/shard_map/parts/pallas_call | solution.py:223
  115.4 2.6 %collective-permute-start.27 = (bf16[128,640]{1,0:T(8,128)(2,1)}, bf16[128,640]{1,0:T(8,128)(2,1)S(1)}, u32[]{:S(2)}, u32[]{:S(2)}) collective-permute-start(bf16[128,640]{1,0:T(8,128)(2,1)} %get-tuple-element.72), channel_id=1, source_target_pairs={{0,48},{8,56},{16,0},{24,8},{32,16},{40,24},{48,32},{56,40},{64,11... | collective-permute-start | bytes 491528 | tf_op jit(solution)/shard_map/ppermute | solution.py:454
  118.8 5.4 %finish.1 = (f32[64,640]{1,0:T(8,128)}, f32[64,640]{1,0:T(8,128)}, f32[2,640]{1,0:T(2,128)}, f32[256,640]{1,0:T(8,128)}) custom-call(f32[1,192,128]{2,1,0:T(8,128)} %token_sums.1.refs_0_.unread_ref.parts0, f32[1,192,128]{2,1,0:T(8,128)} %copy-done.26, f32[2,192,128]{2,1,0:T(8,128)} %copy-done.16, f32[4,192,128]{2,1,0:T(8,128)} %copy-done.30, ...), custom_call_target="tpu_custom_call" | custom-call | flops 1 | bytes 1 | tf_op jit(solution)/shard_map/finish/pallas_call | solution.py:679
  125.1 9.6 %collective-permute-start.28 = (bf16[320,640]{1,0:T(8,128)(2,1)}, bf16[320,640]{1,0:T(8,128)(2,1)S(1)}, u32[]{:S(2)}, u32[]{:S(2)}) collective-permute-start(bf16[320,640]{1,0:T(8,128)(2,1)} %get-tuple-element.73.refs_0_), channel_id=1, source_target_pairs={{0,8},{8,0},{16,24},{24,16},{32,40},{40,32},{48,56},{56,48},{64,72... | collective-permute-start | bytes 1228808 | tf_op jit(solution)/shard_map/ppermute | solution.py:459
  142.6 8.6 %place.1 = bf16[640,5120]{1,0:T(8,128)(2,1)} custom-call(s32[3]{0:T(128)} %pad_add_fusion.pos_ref, bf16[320,640]{1,0:T(8,128)(2,1)} %get-tuple-element.73.refs_0_, bf16[320,640]{1,0:T(8,128)(2,1)} %get-tuple-element.74.refs_1_, bf16[320,640]{1,0:T(8,128)(2,1)} %get-tuple-element.75.refs_2_, bf16[320,640]{1,0:T(8,128)(2,1)} %get-tuple-element.76.refs_3_, ...), custom_call_target="tpu_custom_call" | custom-call | flops 1 | bytes 1 | tf_op jit(solution)/shard_map/place/pallas_call | solution.py:200
  (170 shorter events, 44.7 us)
Async XLA Ops:
  13.0 10.0 %collective-permute-start.2 = (bf16[4,2,320,640]{3,2,1,0:T(8,128)(2,1)}, bf16[4,2,320,640]{3,2,1,0:T(8,128)(2,1)S(1)}, u32[]{:S(2)}, u32[]{:S(2)}) collective-permute-start(bf16[4,2,320,640]{3,2,1,0:T(8,128)(2,1)} %bitcast.54), channel_id=1, source_target_pairs={{0,8},{8,0},{16,24},{24,16},{32,40},{40,32},{48,56},{56,48},{64,72... | collective-permute-start | bytes 9830408 | tf_op jit(solution)/shard_map/ppermute | solution.py:415
  19.6 7.6 %collective-permute-start.1 = (f32[2,16,128]{2,1,0:T(8,128)}, f32[2,16,128]{2,1,0:T(8,128)S(1)}, u32[]{:S(2)}, u32[]{:S(2)}) collective-permute-start(f32[2,16,128]{2,1,0:T(8,128)} %join.4.refs_0_), channel_id=1, source_target_pairs={{0,2},{1,3},{2,0},{3,1},{4,6},{5,7},{6,4},{7,5},{8,10},{9,11},{10,... | collective-permute-start | bytes 49160 | tf_op jit(solution)/shard_map/ppermute | solution.py:410
  29.1 4.0 %collective-permute-start.3 = (f32[4,16,128]{2,1,0:T(8,128)}, f32[4,16,128]{2,1,0:T(8,128)S(1)}, u32[]{:S(2)}, u32[]{:S(2)}) collective-permute-start(f32[4,16,128]{2,1,0:T(8,128)} %join.5.near_heads), channel_id=1, source_target_pairs={{0,4},{1,5},{2,6},{3,7},{4,0},{5,1},{6,2},{7,3},{8,12},{9,13},{10,... | collective-permute-start | bytes 98312 | tf_op jit(solution)/shard_map/ppermute | solution.py:410
  30.3 10.1 %collective-permute-start.10 = (bf16[2,160,640]{2,1,0:T(8,128)(2,1)}, bf16[2,160,640]{2,1,0:T(8,128)(2,1)S(1)}, u32[]{:S(2)}, u32[]{:S(2)}) collective-permute-start(bf16[2,160,640]{2,1,0:T(8,128)(2,1)} %get-tuple-element.49), channel_id=1, source_target_pairs={{0,48},{8,56},{16,0},{24,8},{32,16},{40,24},{48,32},{56,40},{64,11... | collective-permute-start | bytes 1228808 | tf_op jit(solution)/shard_map/ppermute | solution.py:421
  33.0 10.4 %collective-permute-start.9 = (bf16[2,160,640]{2,1,0:T(8,128)(2,1)}, bf16[2,160,640]{2,1,0:T(8,128)(2,1)S(1)}, u32[]{:S(2)}, u32[]{:S(2)}) collective-permute-start(bf16[2,160,640]{2,1,0:T(8,128)(2,1)} %get-tuple-element.46.refs_2_.refs_0_), channel_id=1, source_target_pairs={{0,16},{8,24},{16,32},{24,40},{32,48},{40,56},{48,0},{56,8},{64,80... | collective-permute-start | bytes 1228808 | tf_op jit(solution)/shard_map/ppermute | solution.py:421
  38.5 14.4 %collective-permute-start.4 = (f32[4,192,128]{2,1,0:T(8,128)}, f32[4,192,128]{2,1,0:T(8,128)S(1)}, u32[]{:S(2)}, u32[]{:S(2)}) collective-permute-start(f32[4,192,128]{2,1,0:T(8,128)} %get-tuple-element.48), channel_id=1, source_target_pairs={{0,4},{1,5},{2,6},{3,7},{4,0},{5,1},{6,2},{7,3},{8,12},{9,13},{10,... | collective-permute-start | bytes 1179656 | tf_op jit(solution)/shard_map/ppermute | solution.py:410
  46.3 7.9 %collective-permute-start.16 = (bf16[160,640]{1,0:T(8,128)(2,1)}, bf16[160,640]{1,0:T(8,128)(2,1)S(1)}, u32[]{:S(2)}, u32[]{:S(2)}) collective-permute-start(bf16[160,640]{1,0:T(8,128)(2,1)} %get-tuple-element.55), channel_id=1, source_target_pairs={{0,48},{8,56},{16,0},{24,8},{32,16},{40,24},{48,32},{56,40},{64,11... | collective-permute-start | bytes 614408 | tf_op jit(solution)/shard_map/ppermute | solution.py:433
  47.4 6.9 %collective-permute-start.15 = (bf16[160,640]{1,0:T(8,128)(2,1)}, bf16[160,640]{1,0:T(8,128)(2,1)S(1)}, u32[]{:S(2)}, u32[]{:S(2)}) collective-permute-start(bf16[160,640]{1,0:T(8,128)(2,1)} %get-tuple-element.50.refs_6_), channel_id=1, source_target_pairs={{0,16},{8,24},{16,32},{24,40},{32,48},{40,56},{48,0},{56,8},{64,80... | collective-permute-start | bytes 614408 | tf_op jit(solution)/shard_map/ppermute | solution.py:433
  50.3 12.9 %collective-permute-start.11 = (bf16[2,160,640]{2,1,0:T(8,128)(2,1)}, bf16[2,160,640]{2,1,0:T(8,128)(2,1)S(1)}, u32[]{:S(2)}, u32[]{:S(2)}) collective-permute-start(bf16[2,160,640]{2,1,0:T(8,128)(2,1)} %get-tuple-element.51), channel_id=1, source_target_pairs={{0,16},{8,24},{16,32},{24,40},{32,48},{40,56},{48,0},{56,8},{64,80... | collective-permute-start | bytes 1228808 | tf_op jit(solution)/shard_map/ppermute | solution.py:421
  50.3 12.8 %collective-permute-start.12 = (bf16[2,160,640]{2,1,0:T(8,128)(2,1)}, bf16[2,160,640]{2,1,0:T(8,128)(2,1)S(1)}, u32[]{:S(2)}, u32[]{:S(2)}) collective-permute-start(bf16[2,160,640]{2,1,0:T(8,128)(2,1)} %get-tuple-element.52), channel_id=1, source_target_pairs={{0,48},{8,56},{16,0},{24,8},{32,16},{40,24},{48,32},{56,40},{64,11... | collective-permute-start | bytes 1228808 | tf_op jit(solution)/shard_map/ppermute | solution.py:421
  53.7 15.8 %collective-permute-start.5 = (f32[2,192,128]{2,1,0:T(8,128)}, f32[2,192,128]{2,1,0:T(8,128)S(1)}, u32[]{:S(2)}, u32[]{:S(2)}) collective-permute-start(f32[2,192,128]{2,1,0:T(8,128)} %slice_add_fusion), channel_id=1, source_target_pairs={{0,2},{1,3},{2,0},{3,1},{4,6},{5,7},{6,4},{7,5},{8,10},{9,11},{10,... | collective-permute-start | bytes 589832 | tf_op jit(solution)/shard_map/ppermute | solution.py:410
  58.0 23.1 %collective-permute-start.17 = (bf16[320,640]{1,0:T(8,128)(2,1)}, bf16[320,640]{1,0:T(8,128)(2,1)S(1)}, u32[]{:S(2)}, u32[]{:S(2)}) collective-permute-start(bf16[320,640]{1,0:T(8,128)(2,1)} %chip_sum.3), channel_id=1, source_target_pairs={{0,64},{8,72},{16,80},{24,88},{32,96},{40,104},{48,112},{56,120},{... | collective-permute-start | bytes 1228808 | tf_op jit(solution)/shard_map/ppermute | solution.py:435
  66.9 10.5 %collective-permute-start.13 = (bf16[160,640]{1,0:T(8,128)(2,1)}, bf16[160,640]{1,0:T(8,128)(2,1)S(1)}, u32[]{:S(2)}, u32[]{:S(2)}) collective-permute-start(bf16[160,640]{1,0:T(8,128)(2,1)} %get-tuple-element.53), channel_id=1, source_target_pairs={{0,16},{8,24},{16,32},{24,40},{32,48},{40,56},{48,0},{56,8},{64,80... | collective-permute-start | bytes 614408 | tf_op jit(solution)/shard_map/ppermute | solution.py:437
  66.9 10.5 %collective-permute-start.14 = (bf16[160,640]{1,0:T(8,128)(2,1)}, bf16[160,640]{1,0:T(8,128)(2,1)S(1)}, u32[]{:S(2)}, u32[]{:S(2)}) collective-permute-start(bf16[160,640]{1,0:T(8,128)(2,1)} %get-tuple-element.54), channel_id=1, source_target_pairs={{0,48},{8,56},{16,0},{24,8},{32,16},{40,24},{48,32},{56,40},{64,11... | collective-permute-start | bytes 614408 | tf_op jit(solution)/shard_map/ppermute | solution.py:437
  70.2 3.5 %collective-permute-start.6 = (f32[1,192,128]{2,1,0:T(8,128)S(1)}, f32[1,192,128]{2,1,0:T(8,128)S(1)}, u32[]{:S(2)}, u32[]{:S(2)}) collective-permute-start(f32[1,192,128]{2,1,0:T(8,128)S(1)} %get-tuple-element.81), channel_id=1, source_target_pairs={{0,1},{1,0},{2,3},{3,2},{4,5},{5,4},{6,7},{7,6},{8,9},{9,8},{10,11... | collective-permute-start | bytes 294920 | tf_op jit(solution)/shard_map/ppermute | solution.py:410
  86.0 8.5 %collective-permute-start.19 = (bf16[320,640]{1,0:T(8,128)(2,1)}, bf16[320,640]{1,0:T(8,128)(2,1)S(1)}, u32[]{:S(2)}, u32[]{:S(2)}) collective-permute-start(bf16[320,640]{1,0:T(8,128)(2,1)} %get-tuple-element.62.refs_0_), channel_id=1, source_target_pairs={{0,64},{8,72},{16,80},{24,88},{32,96},{40,104},{48,112},{56,120},{... | collective-permute-start | bytes 1228808 | tf_op jit(solution)/shard_map/ppermute | solution.py:443
  88.3 3.5 %collective-permute-start.7 = (f32[1,192,128]{2,1,0:T(8,128)S(1)}, f32[1,192,128]{2,1,0:T(8,128)S(1)}, u32[]{:S(2)}, u32[]{:S(2)}) collective-permute-start(f32[1,192,128]{2,1,0:T(8,128)S(1)} %copy-done.10), channel_id=1, source_target_pairs={{0,1},{1,0},{2,3},{3,2},{4,5},{5,4},{6,7},{7,6},{8,9},{9,8},{10,11... | collective-permute-start | bytes 294920 | tf_op jit(solution)/shard_map/ppermute | solution.py:410
  89.1 18.0 %collective-permute-start.23 = (bf16[320,640]{1,0:T(8,128)(2,1)}, bf16[320,640]{1,0:T(8,128)(2,1)S(1)}, u32[]{:S(2)}, u32[]{:S(2)}) collective-permute-start(bf16[320,640]{1,0:T(8,128)(2,1)} %get-tuple-element.62.refs_0_), channel_id=1, source_target_pairs={{0,48},{8,56},{16,0},{24,8},{32,16},{40,24},{48,32},{56,40},{64,11... | collective-permute-start | bytes 1228808 | tf_op jit(solution)/shard_map/ppermute | solution.py:444
  89.1 18.0 %collective-permute-start.22 = (bf16[320,640]{1,0:T(8,128)(2,1)}, bf16[320,640]{1,0:T(8,128)(2,1)S(1)}, u32[]{:S(2)}, u32[]{:S(2)}) collective-permute-start(bf16[320,640]{1,0:T(8,128)(2,1)} %get-tuple-element.62.refs_0_), channel_id=1, source_target_pairs={{0,16},{8,24},{16,32},{24,40},{32,48},{40,56},{48,0},{56,8},{64,80... | collective-permute-start | bytes 1228808 | tf_op jit(solution)/shard_map/ppermute | solution.py:444
  95.3 16.4 %collective-permute-start.21 = (bf16[320,640]{1,0:T(8,128)(2,1)}, bf16[320,640]{1,0:T(8,128)(2,1)S(1)}, u32[]{:S(2)}, u32[]{:S(2)}) collective-permute-start(bf16[320,640]{1,0:T(8,128)(2,1)} %gate.2.refs_3_), channel_id=1, source_target_pairs={{0,48},{8,56},{16,0},{24,8},{32,16},{40,24},{48,32},{56,40},{64,11... | collective-permute-start | bytes 1228808 | tf_op jit(solution)/shard_map/ppermute | solution.py:452
  95.3 16.4 %collective-permute-start.20 = (bf16[320,640]{1,0:T(8,128)(2,1)}, bf16[320,640]{1,0:T(8,128)(2,1)S(1)}, u32[]{:S(2)}, u32[]{:S(2)}) collective-permute-start(bf16[320,640]{1,0:T(8,128)(2,1)} %gate.2.refs_3_), channel_id=1, source_target_pairs={{0,16},{8,24},{16,32},{24,40},{32,48},{40,56},{48,0},{56,8},{64,80... | collective-permute-start | bytes 1228808 | tf_op jit(solution)/shard_map/ppermute | solution.py:452
  96.7 7.8 %collective-permute-start.8 = (f32[2,192,128]{2,1,0:T(8,128)}, f32[2,192,128]{2,1,0:T(8,128)S(1)}, u32[]{:S(2)}, u32[]{:S(2)}) collective-permute-start(f32[2,192,128]{2,1,0:T(8,128)} %join.6.unread_ref.refs_0_.refs_1_), channel_id=1, source_target_pairs={{0,2},{1,3},{2,0},{3,1},{4,6},{5,7},{6,4},{7,5},{8,10},{9,11},{10,... | collective-permute-start | bytes 589832 | tf_op jit(solution)/shard_map/ppermute | solution.py:410
  107.0 11.0 %collective-permute-start.18 = (f32[4,192,128]{2,1,0:T(8,128)}, f32[4,192,128]{2,1,0:T(8,128)S(1)}, u32[]{:S(2)}, u32[]{:S(2)}) collective-permute-start(f32[4,192,128]{2,1,0:T(8,128)} %join.7), channel_id=1, source_target_pairs={{0,4},{1,5},{2,6},{3,7},{4,0},{5,1},{6,2},{7,3},{8,12},{9,13},{10,... | collective-permute-start | bytes 1179656 | tf_op jit(solution)/shard_map/ppermute | solution.py:410
  110.5 13.8 %collective-permute-start.25 = (bf16[192,640]{1,0:T(8,128)(2,1)}, bf16[192,640]{1,0:T(8,128)(2,1)S(1)}, u32[]{:S(2)}, u32[]{:S(2)}) collective-permute-start(bf16[192,640]{1,0:T(8,128)(2,1)} %get-tuple-element.71), channel_id=1, source_target_pairs={{0,48},{8,56},{16,0},{24,8},{32,16},{40,24},{48,32},{56,40},{64,11... | collective-permute-start | bytes 737288 | tf_op jit(solution)/shard_map/ppermute | solution.py:450
  115.1 9.2 %collective-permute-start.26 = (bf16[192,640]{1,0:T(8,128)(2,1)}, bf16[192,640]{1,0:T(8,128)(2,1)S(1)}, u32[]{:S(2)}, u32[]{:S(2)}) collective-permute-start(bf16[192,640]{1,0:T(8,128)(2,1)} %get-tuple-element.63.refs_0_), channel_id=1, source_target_pairs={{0,16},{8,24},{16,32},{24,40},{32,48},{40,56},{48,0},{56,8},{64,80... | collective-permute-start | bytes 737288 | tf_op jit(solution)/shard_map/ppermute | solution.py:454
  115.4 8.9 %collective-permute-start.24 = (bf16[128,640]{1,0:T(8,128)(2,1)}, bf16[128,640]{1,0:T(8,128)(2,1)S(1)}, u32[]{:S(2)}, u32[]{:S(2)}) collective-permute-start(bf16[128,640]{1,0:T(8,128)(2,1)} %get-tuple-element.70), channel_id=1, source_target_pairs={{0,16},{8,24},{16,32},{24,40},{32,48},{40,56},{48,0},{56,8},{64,80... | collective-permute-start | bytes 491528 | tf_op jit(solution)/shard_map/ppermute | solution.py:450
  115.4 8.9 %collective-permute-start.27 = (bf16[128,640]{1,0:T(8,128)(2,1)}, bf16[128,640]{1,0:T(8,128)(2,1)S(1)}, u32[]{:S(2)}, u32[]{:S(2)}) collective-permute-start(bf16[128,640]{1,0:T(8,128)(2,1)} %get-tuple-element.72), channel_id=1, source_target_pairs={{0,48},{8,56},{16,0},{24,8},{32,16},{40,24},{48,32},{56,40},{64,11... | collective-permute-start | bytes 491528 | tf_op jit(solution)/shard_map/ppermute | solution.py:454
  125.1 13.3 %collective-permute-start.28 = (bf16[320,640]{1,0:T(8,128)(2,1)}, bf16[320,640]{1,0:T(8,128)(2,1)S(1)}, u32[]{:S(2)}, u32[]{:S(2)}) collective-permute-start(bf16[320,640]{1,0:T(8,128)(2,1)} %get-tuple-element.73.refs_0_), channel_id=1, source_target_pairs={{0,8},{8,0},{16,24},{24,16},{32,40},{40,32},{48,56},{56,48},{64,72... | collective-permute-start | bytes 1228808 | tf_op jit(solution)/shard_map/ppermute | solution.py:459
  134.8 3.1 %collective-permute-start.36 = (bf16[192,640]{1,0:T(8,128)(2,1)}, bf16[192,640]{1,0:T(8,128)(2,1)S(1)}, u32[]{:S(2)}, u32[]{:S(2)}) collective-permute-start(bf16[192,640]{1,0:T(8,128)(2,1)} %copy-done.12), channel_id=1, source_target_pairs={{0,8},{8,0},{16,24},{24,16},{32,40},{40,32},{48,56},{56,48},{64,72... | collective-permute-start | bytes 737288 | tf_op jit(solution)/shard_map/ppermute | solution.py:459
  134.8 3.4 %collective-permute-start.35 = (bf16[192,640]{1,0:T(8,128)(2,1)}, bf16[192,640]{1,0:T(8,128)(2,1)S(1)}, u32[]{:S(2)}, u32[]{:S(2)}) collective-permute-start(bf16[192,640]{1,0:T(8,128)(2,1)} %get-tuple-element.80.refs_7_), channel_id=1, source_target_pairs={{0,8},{8,0},{16,24},{24,16},{32,40},{40,32},{48,56},{56,48},{64,72... | collective-permute-start | bytes 737288 | tf_op jit(solution)/shard_map/ppermute | solution.py:459
  138.2 2.8 %collective-permute-start.32 = (bf16[320,640]{1,0:T(8,128)(2,1)}, bf16[320,640]{1,0:T(8,128)(2,1)S(1)}, u32[]{:S(2)}, u32[]{:S(2)}) collective-permute-start(bf16[320,640]{1,0:T(8,128)(2,1)} %get-tuple-element.77.refs_4_), channel_id=1, source_target_pairs={{0,8},{8,0},{16,24},{24,16},{32,40},{40,32},{48,56},{56,48},{64,72... | collective-permute-start | bytes 1228808 | tf_op jit(solution)/shard_map/ppermute | solution.py:459
  138.4 3.2 %collective-permute-start.33 = (bf16[320,640]{1,0:T(8,128)(2,1)}, bf16[320,640]{1,0:T(8,128)(2,1)S(1)}, u32[]{:S(2)}, u32[]{:S(2)}) collective-permute-start(bf16[320,640]{1,0:T(8,128)(2,1)} %get-tuple-element.78.refs_5_), channel_id=1, source_target_pairs={{0,8},{8,0},{16,24},{24,16},{32,40},{40,32},{48,56},{56,48},{64,72... | collective-permute-start | bytes 1228808 | tf_op jit(solution)/shard_map/ppermute | solution.py:459
  (51 other events, 136.4 us)

commit v5 on v4

--- a/solution.py
+++ b/solution.py
@@ -102,17 +102,20 @@
     return keep.reshape(N_Y, N_XH, ROWS // 2, PAIR), sent.reshape(N_Y, N_XH, ROWS // 2, PAIR)
 
 
-def outer_kernel(pos_ref, own_ref, far_ref, anchor_ref, momentum_ref, unread_ref, new_anchor, new_momentum, params, native, fresh):
+def outer_kernel(pos_ref, keep, got, up, down, up2, down2, far_ref, anchor_ref, momentum_ref, unread_ref, *refs):
+    del unread_ref
+    new_anchor, new_momentum, params, native, fresh, own_ref = refs
+    chip_kernel(keep, got, up, down, up2, down2, own_ref)
     low_lane = lax.broadcasted_iota(jnp.int32, (64, 128), 1) < 64
     first_core = pos_ref[0] == 0
     for block in range(ROWS // QBLOCK):
         message = slice(block * 64, block * 64 + 64)
-        total = own_ref[message].astype(f32) + far_ref[message].astype(f32)
-        rest = total[:, 512:640]
+        both = own_ref[message] + far_ref[message].astype(f32)
+        rest = both[:, 512:640]
         for half, tail in ((0, rest), (1, pltpu.roll(rest, 64, 1))):
             rows = slice(block * 128 + half * 64, block * 128 + half * 64 + 64)
-            main0 = total[:, half * 256 : half * 256 + 128]
-            main1 = total[:, half * 256 + 128 : half * 256 + 256]
+            main0 = both[:, half * 256 : half * 256 + 128]
+            main1 = both[:, half * 256 + 128 : half * 256 + 256]
             turn0, turn1 = pltpu.roll(main0, 64, 1), pltpu.roll(main1, 64, 1)
             native[rows, 0:128] = jnp.where(first_core, main0, jnp.where(low_lane, tail, turn0))
             native[rows, 128:256] = jnp.where(first_core, main1, jnp.where(low_lane, turn0, turn1))
@@ -139,22 +142,33 @@
         params[message, 512:640] = jnp.where(low_lane, top, bottom).astype(bf16)
 
 
-def outer_update(pos, own, far, anchor, momentum, after):
-    held = pl.BlockSpec(memory_space=pltpu.VMEM)
+def outer_update(pos, keep, got, up, down, up2, down2, far, anchor, momentum, after):
+    _, _, rows, columns = keep.shape
+    came = pl.BlockSpec((1, rows // 2, columns), lambda i: (1, 0, 0))
+    part = pl.BlockSpec((rows // 2, columns), lambda i: (0, 0))
+    block = pl.BlockSpec((rows, columns), lambda i: (0, 0))
+    plain = pl.BlockSpec((ROWS, COL), lambda i: (0, 0))
     return pl.pallas_call(
         outer_kernel,
-        in_specs=[pl.BlockSpec(memory_space=pltpu.SMEM)] + [held] * 4 + [unread],
-        out_specs=[held] * 3,
-        scratch_shapes=[pltpu.VMEM((ROWS, 384), f32), pltpu.VMEM((ROWS, 384), f32)],
+        grid=(1,),
+        in_specs=[pl.BlockSpec(memory_space=pltpu.SMEM)]
+        + [spot(0, 0, rows, columns)] * 2
+        + [came, came, part, part, block, plain, plain, unread],
+        out_specs=[plain, plain, block],
+        scratch_shapes=[
+            pltpu.VMEM((ROWS, 384), f32),
+            pltpu.VMEM((ROWS, 384), f32),
+            pltpu.VMEM((rows, columns), f32),
+        ],
         out_shape=[
             jax.ShapeDtypeStruct((ROWS, COL), f32),
             jax.ShapeDtypeStruct((ROWS, COL), f32),
-            jax.ShapeDtypeStruct((ROWS // 2, PAIR), bf16),
+            jax.ShapeDtypeStruct((rows, columns), bf16),
         ],
         compiler_params=limit,
         cost_estimate=brief,
         name="outer_update",
-    )(pos, own, far, anchor, momentum, after)
+    )(pos, keep, got, up, down, up2, down2, far, anchor, momentum, after)
 
 
 def place_kernel(chips, pos_ref, *refs):
@@ -437,8 +451,9 @@
     own_up, own_down = send(own[0], perm=to_y(1)), send(own[1], perm=to_y(-1))
     q0 = token_sums(near[0:1] + away[0:1] + away2[0:1], away1, latents.T, target.T, [], width, tokens)
     q1 = across(q0, 1)
-    own = chip_sum(keep, got, up[0], down[0], own_up, own_down, 0, f32)
-    new_anchor, new_momentum, n0 = outer_update(pos, own, far, anchor, momentum, q0)
+    new_anchor, new_momentum, n0 = outer_update(
+        pos, keep, got, up[0], down[0], own_up, own_down, far, anchor, momentum, q0
+    )
 
     n1 = send(n0, perm=to_x)
     up0, down0 = send(n0, perm=to_y(1)), send(n0, perm=to_y(-1))

time: 152 us -> 150 us (0.987)
  Pallas kernels: 62.2 us -> 60.1 us
    pallas_call x2 -> x1, Pallas kernels: 4.84 us -> 2.36 us  [chip_sum(): pl.pallas_call(chip_kernel, grid=(1,), in_specs=[spot(0, x, rows, columns...]
  transfers between devices with their start and end apart: 38 -> 38, of which waited for: 12 -> 12; matrix products, arithmetic and copies ran while one was open for 6% -> 6% of each run, Pallas kernels for 24% -> 23%
where the time goes in v5:
time: 150 us; the launch traced here: 149 us
  Pallas kernels  60.1 us (40%)
  starting transfers between devices  46 us (31%)
  local copies, waits for them, and re-layouts  24.5 us (16%)
  waiting for transfers between devices  14.5 us (10%)
  other arithmetic  2.33 us (2%)
    unnamed x92, local copies, waits for them, and re-layouts  19.6 us
    ppermute x10, starting transfers between devices, per_device(): theirs = [to_sibling(part) for part in mine]  12.1 us
    pallas_call x1, Pallas kernels, quantize(): pl.pallas_call(quant_kernel, grid_spec=pltpu.PrefetchScalarGridSpec(num_s...  11.7 us
    ppermute x9, starting transfers between devices, across(): return lax.ppermute(value, 'fsdp', [(i, i ^ bit) for i in range(N_FSDP)])  11.1 us
    pallas_call x1, Pallas kernels, place(): pl.pallas_call(functools.partial(place_kernel, chips), grid_spec=pltpu.Pr...  8.57 us
    pallas_call x4, Pallas kernels, join(): pl.pallas_call(functools.partial(join_kernel, len(after)), in_specs=[pl.B...  6.09 us
    pallas_call x1, Pallas kernels, finish(): pl.pallas_call(functools.partial(finish_kernel, len(after)), in_specs=[pl...  5.44 us
    ppermute x2, starting transfers between devices, ring(): send(messages[1], perm=to_y(-1))  5.37 us
  transfers between devices with their start and end apart: 38, of which 12 were waited for; matrix products, arithmetic and copies ran while one was open for 6% of the time, Pallas kernels for 23%

profile of v5, /device:TPU:1, one launch (start us, length us, event | category | flops | bytes accessed | tf_op | source)
XLA Modules:
  0.0 148.5 jit_solution(9422752866416840453)
XLA Ops:
  1.3 11.7 %quantize.1 = (bf16[8,320,640]{2,1,0:T(8,128)(2,1)}, bf16[8,320,640]{2,1,0:T(8,128)(2,1)}) custom-call(s32[3]{0:T(128)} %pad_add_fusion.pos_ref, bf16[640,5120]{1,0:T(8,128)(2,1)} %start_ref.1, bf16[640,5120]{1,0:T(8,128)(2,1)} %bitcast.38), custom_call_target="tpu_custom_call" | custom-call | flops 1 | bytes 1 | tf_op jit(solution)/shard_map/quantize/pallas_call | solution.py:89
  14.8 1.8 %collective-permute-start = (f32[1,16,128]{2,1,0:T(8,128)S(1)}, f32[1,16,128]{2,1,0:T(8,128)S(1)}, u32[]{:S(2)}, u32[]{:S(2)}) collective-permute-start(f32[1,16,128]{2,1,0:T(8,128)S(1)} %maximum_bitcast_fusion.refs_0_), channel_id=1, source_target_pairs={{0,1},{1,0},{2,3},{3,2},{4,5},{5,4},{6,7},{7,6},{8,9},{9,8},{10,11... | collective-permute-start | bytes 24584 | tf_op jit(solution)/shard_map/ppermute | solution.py:424
  19.5 3.4 %collective-permute-start.1 = (f32[2,16,128]{2,1,0:T(8,128)}, f32[2,16,128]{2,1,0:T(8,128)S(1)}, u32[]{:S(2)}, u32[]{:S(2)}) collective-permute-start(f32[2,16,128]{2,1,0:T(8,128)} %join.4.refs_0_), channel_id=1, source_target_pairs={{0,2},{1,3},{2,0},{3,1},{4,6},{5,7},{6,4},{7,5},{8,10},{9,11},{10,... | collective-permute-start | bytes 49160 | tf_op jit(solution)/shard_map/ppermute | solution.py:424
  22.9 1.7 %copy-done = bf16[4,2,320,640]{3,2,1,0:T(8,128)(2,1)} copy-done((bf16[4,2,320,640]{3,2,1,0:T(8,128)(2,1)}, bf16[4,2,320,640]{3,2,1,0:T(8,128)(2,1)S(1)}, u32[]{:S(2)}) %copy-start) | copy-done | bytes 3276824
  24.6 2.4 %first_messages.2 = (bf16[2,160,640]{2,1,0:T(8,128)(2,1)}, bf16[2,160,640]{2,1,0:T(8,128)(2,1)}) custom-call(bf16[4,2,320,640]{3,2,1,0:T(8,128)(2,1)} %bitcast.26, bf16[4,2,320,640]{3,2,1,0:T(8,128)(2,1)} %copy-done, bf16[4,2,320,640]{3,2,1,0:T(8,128)(2,1)} %bitcast.27, bf16[4,2,320,640]{3,2,1,0:T(8,128)(2,1)} %copy-done, bf16[4,2,320,640]{3,2,1,0:T(8,128)(2,1)} %bitcast.28, ...), custom_call_target="tpu_custom_call" | custom-call | flops 1 | bytes 1 | tf_op jit(solution)/shard_map/first_messages/pallas_call | solution.py:326
  30.2 2.7 %collective-permute-start.10 = (bf16[2,160,640]{2,1,0:T(8,128)(2,1)}, bf16[2,160,640]{2,1,0:T(8,128)(2,1)S(1)}, u32[]{:S(2)}, u32[]{:S(2)}) collective-permute-start(bf16[2,160,640]{2,1,0:T(8,128)(2,1)} %get-tuple-element.49), channel_id=1, source_target_pairs={{0,48},{8,56},{16,0},{24,8},{32,16},{40,24},{48,32},{56,40},{64,11... | collective-permute-start | bytes 1228808 | tf_op jit(solution)/shard_map/ppermute | solution.py:435
  33.6 4.9 %weight_products.1 = (f32[4,192,128]{2,1,0:T(8,128)}, f32[4,192,128]{2,1,0:T(8,128)}, f32[32,640]{1,0:T(8,128)}, f32[64,640]{1,0:T(8,128)}, f32[32,256]{1,0:T(8,128)}) custom-call(f32[4,16,128]{2,1,0:T(8,128)} %join.5.near_heads, f32[4,16,128]{2,1,0:T(8,128)} %copy-done.41, f32[64,640]{1,0:T(8,128)} %bitcast.45, f32[64,640]{1,0:T(8,128)} %bitcast.47, ...), custom_call_target="tpu_custom_call" | custom-call | flops 1 | bytes 1 | tf_op jit(solution)/shard_map/weight_products/pallas_call | solution.py:663
  38.7 1.6 %collective-permute-done.10.down = bf16[2,160,640]{2,1,0:T(8,128)(2,1)S(1)} collective-permute-done((bf16[2,160,640]{2,1,0:T(8,128)(2,1)}, bf16[2,160,640]{2,1,0:T(8,128)(2,1)S(1)}, u32[]{:S(2)}, u32[]{:S(2)}) %collective-permute-start.10) | collective-permute-done | bytes 409632 | tf_op jit(solution)/shard_map/ppermute | solution.py:435
  40.3 3.0 %collective-permute-done.9.up = bf16[2,160,640]{2,1,0:T(8,128)(2,1)S(1)} collective-permute-done((bf16[2,160,640]{2,1,0:T(8,128)(2,1)}, bf16[2,160,640]{2,1,0:T(8,128)(2,1)S(1)}, u32[]{:S(2)}, u32[]{:S(2)}) %collective-permute-start.9) | collective-permute-done | bytes 409632 | tf_op jit(solution)/shard_map/ppermute | solution.py:435
  44.1 2.2 %second_messages.2 = (bf16[160,640]{1,0:T(8,128)(2,1)}, bf16[160,640]{1,0:T(8,128)(2,1)}) custom-call(bf16[4,2,320,640]{3,2,1,0:T(8,128)(2,1)} %bitcast.29, bf16[4,2,320,640]{3,2,1,0:T(8,128)(2,1)} %copy-done, bf16[4,2,320,640]{3,2,1,0:T(8,128)(2,1)} %bitcast.30, bf16[4,2,320,640]{3,2,1,0:T(8,128)(2,1)} %copy-done, bf16[2,160,640]{2,1,0:T(8,128)(2,1)} %copy-done.9, ...), custom_call_target="tpu_custom_call" | custom-call | flops 1 | bytes 1 | tf_op jit(solution)/shard_map/second_messages/pallas_call | solution.py:353
  47.8 2.4 %first_messages.3 = (bf16[2,160,640]{2,1,0:T(8,128)(2,1)}, bf16[2,160,640]{2,1,0:T(8,128)(2,1)}) custom-call(bf16[4,2,320,640]{3,2,1,0:T(8,128)(2,1)} %bitcast.31, bf16[4,2,320,640]{3,2,1,0:T(8,128)(2,1)} %copy-done, bf16[4,2,320,640]{3,2,1,0:T(8,128)(2,1)} %bitcast.32, bf16[4,2,320,640]{3,2,1,0:T(8,128)(2,1)} %copy-done, bf16[4,2,320,640]{3,2,1,0:T(8,128)(2,1)} %bitcast.33, ...), custom_call_target="tpu_custom_call" | custom-call | flops 1 | bytes 1 | tf_op jit(solution)/shard_map/first_messages/pallas_call | solution.py:326
  50.3 2.6 %collective-permute-start.12 = (bf16[2,160,640]{2,1,0:T(8,128)(2,1)}, bf16[2,160,640]{2,1,0:T(8,128)(2,1)S(1)}, u32[]{:S(2)}, u32[]{:S(2)}) collective-permute-start(bf16[2,160,640]{2,1,0:T(8,128)(2,1)} %get-tuple-element.52), channel_id=1, source_target_pairs={{0,48},{8,56},{16,0},{24,8},{32,16},{40,24},{48,32},{56,40},{64,11... | collective-permute-start | bytes 1228808 | tf_op jit(solution)/shard_map/ppermute | solution.py:435
  55.6 2.4 %chip_sum.1 = bf16[320,640]{1,0:T(8,128)(2,1)} custom-call(bf16[4,2,320,640]{3,2,1,0:T(8,128)(2,1)} %bitcast.34, bf16[4,2,320,640]{3,2,1,0:T(8,128)(2,1)} %copy-done, bf16[2,160,640]{2,1,0:T(8,128)(2,1)} %copy-done.9, bf16[2,160,640]{2,1,0:T(8,128)(2,1)} %copy-done.8, bf16[160,640]{1,0:T(8,128)(2,1)} %copy-done.36, bf16[160,640]{1,0:T(8,128)(2,1)} %copy-done.35), custom_call_target="tpu_custom_call" | custom-call | flops 1 | bytes 1 | tf_op jit(solution)/shard_map/chip_sum/pallas_call | solution.py:376
  58.0 2.5 %collective-permute-start.17 = (bf16[320,640]{1,0:T(8,128)(2,1)}, bf16[320,640]{1,0:T(8,128)(2,1)S(1)}, u32[]{:S(2)}, u32[]{:S(2)}) collective-permute-start(bf16[320,640]{1,0:T(8,128)(2,1)} %chip_sum.1), channel_id=1, source_target_pairs={{0,64},{8,72},{16,80},{24,88},{32,96},{40,104},{48,112},{56,120},{... | collective-permute-start | bytes 1228808 | tf_op jit(solution)/shard_map/ppermute | solution.py:449
  64.6 2.2 %second_messages.3 = (bf16[160,640]{1,0:T(8,128)(2,1)}, bf16[160,640]{1,0:T(8,128)(2,1)}) custom-call(bf16[4,2,320,640]{3,2,1,0:T(8,128)(2,1)} %bitcast.35, bf16[4,2,320,640]{3,2,1,0:T(8,128)(2,1)} %copy-done, bf16[4,2,320,640]{3,2,1,0:T(8,128)(2,1)} %bitcast.36, bf16[4,2,320,640]{3,2,1,0:T(8,128)(2,1)} %copy-done, bf16[2,160,640]{2,1,0:T(8,128)(2,1)} %copy-done.6, ...), custom_call_target="tpu_custom_call" | custom-call | flops 1 | bytes 1 | tf_op jit(solution)/shard_map/second_messages/pallas_call | solution.py:353
  66.8 2.7 %collective-permute-start.14 = (bf16[160,640]{1,0:T(8,128)(2,1)}, bf16[160,640]{1,0:T(8,128)(2,1)S(1)}, u32[]{:S(2)}, u32[]{:S(2)}) collective-permute-start(bf16[160,640]{1,0:T(8,128)(2,1)} %get-tuple-element.54), channel_id=1, source_target_pairs={{0,48},{8,56},{16,0},{24,8},{32,16},{40,24},{48,32},{56,40},{64,11... | collective-permute-start | bytes 614408 | tf_op jit(solution)/shard_map/ppermute | solution.py:451
  70.9 2.7 %collective-permute-done.6.away_ref = f32[1,192,128]{2,1,0:T(8,128)S(1)} collective-permute-done((f32[1,192,128]{2,1,0:T(8,128)S(1)}, f32[1,192,128]{2,1,0:T(8,128)S(1)}, u32[]{:S(2)}, u32[]{:S(2)}) %collective-permute-start.6) | collective-permute-done | bytes 98336 | tf_op jit(solution)/shard_map/ppermute | solution.py:424
  74.3 3.0 %token_sums.1.refs_0_.unread_ref.parts0 = f32[1,192,128]{2,1,0:T(8,128)} custom-call(f32[1,192,128]{2,1,0:T(8,128)} %get-tuple-element.82.own_ref, f32[1,192,128]{2,1,0:T(8,128)} %copy-done.39, bf16[64,2048]{1,0:T(8,128)(2,1)} %bitcast.49, bf16[64,2048]{1,0:T(8,128)(2,1)} %bitcast.50), custom_call_target="tpu_custom_call" | custom-call | flops 1 | bytes 1 | tf_op jit(solution)/shard_map/token_sums/pallas_call | solution.py:681
  78.8 4.3 %outer_update.1 = (f32[640,320]{1,0:T(8,128)}, f32[640,320]{1,0:T(8,128)}, bf16[320,640]{1,0:T(8,128)(2,1)}) custom-call(s32[3]{0:T(128)} %pad_add_fusion.pos_ref, bf16[4,2,320,640]{3,2,1,0:T(8,128)(2,1)} %bitcast.37, bf16[4,2,320,640]{3,2,1,0:T(8,128)(2,1)} %copy-done, bf16[2,160,640]{2,1,0:T(8,128)(2,1)} %copy-done.6, bf16[2,160,640]{2,1,0:T(8,128)(2,1)} %copy-done.7, ...), custom_call_target="tpu_custom_call" | custom-call | flops 1 | bytes 1 | tf_op jit(solution)/shard_map/outer_update/pallas_call | solution.py:151
  83.1 2.3 %collective-permute-start.19 = (bf16[320,640]{1,0:T(8,128)(2,1)}, bf16[320,640]{1,0:T(8,128)(2,1)S(1)}, u32[]{:S(2)}, u32[]{:S(2)}) collective-permute-start(bf16[320,640]{1,0:T(8,128)(2,1)} %get-tuple-element.62.refs_0_), channel_id=1, source_target_pairs={{0,64},{8,72},{16,80},{24,88},{32,96},{40,104},{48,112},{56,120},{... | collective-permute-start | bytes 1228808 | tf_op jit(solution)/shard_map/ppermute | solution.py:458
  89.6 1.6 %join.6.unread_ref.refs_0_.refs_1_ = f32[2,192,128]{2,1,0:T(8,128)} custom-call(f32[1,192,128]{2,1,0:T(8,128)} %token_sums.1.refs_0_.unread_ref.parts0, f32[1,192,128]{2,1,0:T(8,128)} %copy-done.26), custom_call_target="tpu_custom_call" | custom-call | flops 1 | bytes 1 | tf_op jit(solution)/shard_map/join/pallas_call | solution.py:256
  93.9 2.4 %collective-permute-start.8 = (f32[2,192,128]{2,1,0:T(8,128)}, f32[2,192,128]{2,1,0:T(8,128)S(1)}, u32[]{:S(2)}, u32[]{:S(2)}) collective-permute-start(f32[2,192,128]{2,1,0:T(8,128)} %join.6.unread_ref.refs_0_.refs_1_), channel_id=1, source_target_pairs={{0,2},{1,3},{2,0},{3,1},{4,6},{5,7},{6,4},{7,5},{8,10},{9,11},{10,... | collective-permute-start | bytes 589832 | tf_op jit(solution)/shard_map/ppermute | solution.py:424
  96.3 2.4 %copy.33 = f32[640,320]{0,1:T(8,128)} copy(f32[640,320]{1,0:T(8,128)} %get-tuple-element.56) | data formatting | bytes 1638400 | tf_op jit(solution)/shard_map/outer_update/pallas_call | solution.py:151
  98.7 2.4 %copy.34 = f32[640,320]{0,1:T(8,128)} copy(f32[640,320]{1,0:T(8,128)} %get-tuple-element.57) | data formatting | bytes 1638400 | tf_op jit(solution)/shard_map/outer_update/pallas_call | solution.py:151
  102.4 1.8 %join.7 = f32[4,192,128]{2,1,0:T(8,128)} custom-call(f32[2,192,128]{2,1,0:T(8,128)} %join.6.unread_ref.refs_0_.refs_1_, f32[2,192,128]{2,1,0:T(8,128)} %copy-done.16, f32[8,128]{1,0:T(8,128)} %get-tuple-element.58.refs_2_.refs_11_.refs_21_), custom_call_target="tpu_custom_call" | custom-call | flops 1 | bytes 1 | tf_op jit(solution)/shard_map/join/pallas_call | solution.py:256
  105.7 1.9 %parts.3 = (bf16[128,640]{1,0:T(8,128)(2,1)}, bf16[192,640]{1,0:T(8,128)(2,1)}) custom-call(bf16[320,640]{1,0:T(8,128)(2,1)} %copy-done.2, bf16[320,640]{1,0:T(8,128)(2,1)} %copy-done.1), custom_call_target="tpu_custom_call" | custom-call | flops 1 | bytes 1 | tf_op jit(solution)/shard_map/parts/pallas_call | solution.py:237
  110.4 1.9 %parts.2 = (bf16[192,640]{1,0:T(8,128)(2,1)}, bf16[128,640]{1,0:T(8,128)(2,1)}) custom-call(bf16[320,640]{1,0:T(8,128)(2,1)} %copy-done.4, bf16[320,640]{1,0:T(8,128)(2,1)} %copy-done.3), custom_call_target="tpu_custom_call" | custom-call | flops 1 | bytes 1 | tf_op jit(solution)/shard_map/parts/pallas_call | solution.py:237
  112.6 2.6 %collective-permute-start.27 = (bf16[128,640]{1,0:T(8,128)(2,1)}, bf16[128,640]{1,0:T(8,128)(2,1)S(1)}, u32[]{:S(2)}, u32[]{:S(2)}) collective-permute-start(bf16[128,640]{1,0:T(8,128)(2,1)} %get-tuple-element.72), channel_id=1, source_target_pairs={{0,48},{8,56},{16,0},{24,8},{32,16},{40,24},{48,32},{56,40},{64,11... | collective-permute-start | bytes 491528 | tf_op jit(solution)/shard_map/ppermute | solution.py:469
  116.0 5.4 %finish.1 = (f32[64,640]{1,0:T(8,128)}, f32[64,640]{1,0:T(8,128)}, f32[2,640]{1,0:T(2,128)}, f32[256,640]{1,0:T(8,128)}) custom-call(f32[1,192,128]{2,1,0:T(8,128)} %token_sums.1.refs_0_.unread_ref.parts0, f32[1,192,128]{2,1,0:T(8,128)} %copy-done.26, f32[2,192,128]{2,1,0:T(8,128)} %copy-done.16, f32[4,192,128]{2,1,0:T(8,128)} %copy-done.30, ...), custom_call_target="tpu_custom_call" | custom-call | flops 1 | bytes 1 | tf_op jit(solution)/shard_map/finish/pallas_call | solution.py:694
  122.3 9.7 %collective-permute-start.28 = (bf16[320,640]{1,0:T(8,128)(2,1)}, bf16[320,640]{1,0:T(8,128)(2,1)S(1)}, u32[]{:S(2)}, u32[]{:S(2)}) collective-permute-start(bf16[320,640]{1,0:T(8,128)(2,1)} %get-tuple-element.73.refs_0_), channel_id=1, source_target_pairs={{0,8},{8,0},{16,24},{24,16},{32,40},{40,32},{48,56},{56,48},{64,72... | collective-permute-start | bytes 1228808 | tf_op jit(solution)/shard_map/ppermute | solution.py:474
  133.0 1.5 %collective-permute-done.37.refs_19_ = bf16[128,640]{1,0:T(8,128)(2,1)S(1)} collective-permute-done((bf16[128,640]{1,0:T(8,128)(2,1)}, bf16[128,640]{1,0:T(8,128)(2,1)S(1)}, u32[]{:S(2)}, u32[]{:S(2)}) %collective-permute-start.37) | collective-permute-done | bytes 163872 | tf_op jit(solution)/shard_map/ppermute | solution.py:474
  139.8 8.6 %place.1 = bf16[640,5120]{1,0:T(8,128)(2,1)} custom-call(s32[3]{0:T(128)} %pad_add_fusion.pos_ref, bf16[320,640]{1,0:T(8,128)(2,1)} %get-tuple-element.73.refs_0_, bf16[320,640]{1,0:T(8,128)(2,1)} %get-tuple-element.74.refs_1_, bf16[320,640]{1,0:T(8,128)(2,1)} %get-tuple-element.75.refs_2_, bf16[320,640]{1,0:T(8,128)(2,1)} %get-tuple-element.76.refs_3_, ...), custom_call_target="tpu_custom_call" | custom-call | flops 1 | bytes 1 | tf_op jit(solution)/shard_map/place/pallas_call | solution.py:214
  (169 shorter events, 42.6 us)
Async XLA Ops:
  13.0 10.0 %collective-permute-start.2 = (bf16[4,2,320,640]{3,2,1,0:T(8,128)(2,1)}, bf16[4,2,320,640]{3,2,1,0:T(8,128)(2,1)S(1)}, u32[]{:S(2)}, u32[]{:S(2)}) collective-permute-start(bf16[4,2,320,640]{3,2,1,0:T(8,128)(2,1)} %bitcast.54), channel_id=1, source_target_pairs={{0,8},{8,0},{16,24},{24,16},{32,40},{40,32},{48,56},{56,48},{64,72... | collective-permute-start | bytes 9830408 | tf_op jit(solution)/shard_map/ppermute | solution.py:429
  19.5 7.6 %collective-permute-start.1 = (f32[2,16,128]{2,1,0:T(8,128)}, f32[2,16,128]{2,1,0:T(8,128)S(1)}, u32[]{:S(2)}, u32[]{:S(2)}) collective-permute-start(f32[2,16,128]{2,1,0:T(8,128)} %join.4.refs_0_), channel_id=1, source_target_pairs={{0,2},{1,3},{2,0},{3,1},{4,6},{5,7},{6,4},{7,5},{8,10},{9,11},{10,... | collective-permute-start | bytes 49160 | tf_op jit(solution)/shard_map/ppermute | solution.py:424
  29.0 4.0 %collective-permute-start.3 = (f32[4,16,128]{2,1,0:T(8,128)}, f32[4,16,128]{2,1,0:T(8,128)S(1)}, u32[]{:S(2)}, u32[]{:S(2)}) collective-permute-start(f32[4,16,128]{2,1,0:T(8,128)} %join.5.near_heads), channel_id=1, source_target_pairs={{0,4},{1,5},{2,6},{3,7},{4,0},{5,1},{6,2},{7,3},{8,12},{9,13},{10,... | collective-permute-start | bytes 98312 | tf_op jit(solution)/shard_map/ppermute | solution.py:424
  30.2 10.1 %collective-permute-start.10 = (bf16[2,160,640]{2,1,0:T(8,128)(2,1)}, bf16[2,160,640]{2,1,0:T(8,128)(2,1)S(1)}, u32[]{:S(2)}, u32[]{:S(2)}) collective-permute-start(bf16[2,160,640]{2,1,0:T(8,128)(2,1)} %get-tuple-element.49), channel_id=1, source_target_pairs={{0,48},{8,56},{16,0},{24,8},{32,16},{40,24},{48,32},{56,40},{64,11... | collective-permute-start | bytes 1228808 | tf_op jit(solution)/shard_map/ppermute | solution.py:435
  33.0 10.4 %collective-permute-start.9 = (bf16[2,160,640]{2,1,0:T(8,128)(2,1)}, bf16[2,160,640]{2,1,0:T(8,128)(2,1)S(1)}, u32[]{:S(2)}, u32[]{:S(2)}) collective-permute-start(bf16[2,160,640]{2,1,0:T(8,128)(2,1)} %get-tuple-element.46.refs_2_.refs_0_), channel_id=1, source_target_pairs={{0,16},{8,24},{16,32},{24,40},{32,48},{40,56},{48,0},{56,8},{64,80... | collective-permute-start | bytes 1228808 | tf_op jit(solution)/shard_map/ppermute | solution.py:435
  38.5 14.4 %collective-permute-start.4 = (f32[4,192,128]{2,1,0:T(8,128)}, f32[4,192,128]{2,1,0:T(8,128)S(1)}, u32[]{:S(2)}, u32[]{:S(2)}) collective-permute-start(f32[4,192,128]{2,1,0:T(8,128)} %get-tuple-element.48), channel_id=1, source_target_pairs={{0,4},{1,5},{2,6},{3,7},{4,0},{5,1},{6,2},{7,3},{8,12},{9,13},{10,... | collective-permute-start | bytes 1179656 | tf_op jit(solution)/shard_map/ppermute | solution.py:424
  46.3 8.0 %collective-permute-start.16 = (bf16[160,640]{1,0:T(8,128)(2,1)}, bf16[160,640]{1,0:T(8,128)(2,1)S(1)}, u32[]{:S(2)}, u32[]{:S(2)}) collective-permute-start(bf16[160,640]{1,0:T(8,128)(2,1)} %get-tuple-element.55), channel_id=1, source_target_pairs={{0,48},{8,56},{16,0},{24,8},{32,16},{40,24},{48,32},{56,40},{64,11... | collective-permute-start | bytes 614408 | tf_op jit(solution)/shard_map/ppermute | solution.py:447
  47.3 6.9 %collective-permute-start.15 = (bf16[160,640]{1,0:T(8,128)(2,1)}, bf16[160,640]{1,0:T(8,128)(2,1)S(1)}, u32[]{:S(2)}, u32[]{:S(2)}) collective-permute-start(bf16[160,640]{1,0:T(8,128)(2,1)} %get-tuple-element.50.refs_6_), channel_id=1, source_target_pairs={{0,16},{8,24},{16,32},{24,40},{32,48},{40,56},{48,0},{56,8},{64,80... | collective-permute-start | bytes 614408 | tf_op jit(solution)/shard_map/ppermute | solution.py:447
  50.2 12.9 %collective-permute-start.11 = (bf16[2,160,640]{2,1,0:T(8,128)(2,1)}, bf16[2,160,640]{2,1,0:T(8,128)(2,1)S(1)}, u32[]{:S(2)}, u32[]{:S(2)}) collective-permute-start(bf16[2,160,640]{2,1,0:T(8,128)(2,1)} %get-tuple-element.51), channel_id=1, source_target_pairs={{0,16},{8,24},{16,32},{24,40},{32,48},{40,56},{48,0},{56,8},{64,80... | collective-permute-start | bytes 1228808 | tf_op jit(solution)/shard_map/ppermute | solution.py:435
  50.3 12.8 %collective-permute-start.12 = (bf16[2,160,640]{2,1,0:T(8,128)(2,1)}, bf16[2,160,640]{2,1,0:T(8,128)(2,1)S(1)}, u32[]{:S(2)}, u32[]{:S(2)}) collective-permute-start(bf16[2,160,640]{2,1,0:T(8,128)(2,1)} %get-tuple-element.52), channel_id=1, source_target_pairs={{0,48},{8,56},{16,0},{24,8},{32,16},{40,24},{48,32},{56,40},{64,11... | collective-permute-start | bytes 1228808 | tf_op jit(solution)/shard_map/ppermute | solution.py:435
  53.7 15.8 %collective-permute-start.5 = (f32[2,192,128]{2,1,0:T(8,128)}, f32[2,192,128]{2,1,0:T(8,128)S(1)}, u32[]{:S(2)}, u32[]{:S(2)}) collective-permute-start(f32[2,192,128]{2,1,0:T(8,128)} %slice_add_fusion), channel_id=1, source_target_pairs={{0,2},{1,3},{2,0},{3,1},{4,6},{5,7},{6,4},{7,5},{8,10},{9,11},{10,... | collective-permute-start | bytes 589832 | tf_op jit(solution)/shard_map/ppermute | solution.py:424
  58.0 19.3 %collective-permute-start.17 = (bf16[320,640]{1,0:T(8,128)(2,1)}, bf16[320,640]{1,0:T(8,128)(2,1)S(1)}, u32[]{:S(2)}, u32[]{:S(2)}) collective-permute-start(bf16[320,640]{1,0:T(8,128)(2,1)} %chip_sum.1), channel_id=1, source_target_pairs={{0,64},{8,72},{16,80},{24,88},{32,96},{40,104},{48,112},{56,120},{... | collective-permute-start | bytes 1228808 | tf_op jit(solution)/shard_map/ppermute | solution.py:449
  66.8 10.5 %collective-permute-start.13 = (bf16[160,640]{1,0:T(8,128)(2,1)}, bf16[160,640]{1,0:T(8,128)(2,1)S(1)}, u32[]{:S(2)}, u32[]{:S(2)}) collective-permute-start(bf16[160,640]{1,0:T(8,128)(2,1)} %get-tuple-element.53), channel_id=1, source_target_pairs={{0,16},{8,24},{16,32},{24,40},{32,48},{40,56},{48,0},{56,8},{64,80... | collective-permute-start | bytes 614408 | tf_op jit(solution)/shard_map/ppermute | solution.py:451
  66.8 10.5 %collective-permute-start.14 = (bf16[160,640]{1,0:T(8,128)(2,1)}, bf16[160,640]{1,0:T(8,128)(2,1)S(1)}, u32[]{:S(2)}, u32[]{:S(2)}) collective-permute-start(bf16[160,640]{1,0:T(8,128)(2,1)} %get-tuple-element.54), channel_id=1, source_target_pairs={{0,48},{8,56},{16,0},{24,8},{32,16},{40,24},{48,32},{56,40},{64,11... | collective-permute-start | bytes 614408 | tf_op jit(solution)/shard_map/ppermute | solution.py:451
  70.2 3.5 %collective-permute-start.6 = (f32[1,192,128]{2,1,0:T(8,128)S(1)}, f32[1,192,128]{2,1,0:T(8,128)S(1)}, u32[]{:S(2)}, u32[]{:S(2)}) collective-permute-start(f32[1,192,128]{2,1,0:T(8,128)S(1)} %get-tuple-element.81), channel_id=1, source_target_pairs={{0,1},{1,0},{2,3},{3,2},{4,5},{5,4},{6,7},{7,6},{8,9},{9,8},{10,11... | collective-permute-start | bytes 294920 | tf_op jit(solution)/shard_map/ppermute | solution.py:424
  83.1 8.5 %collective-permute-start.19 = (bf16[320,640]{1,0:T(8,128)(2,1)}, bf16[320,640]{1,0:T(8,128)(2,1)S(1)}, u32[]{:S(2)}, u32[]{:S(2)}) collective-permute-start(bf16[320,640]{1,0:T(8,128)(2,1)} %get-tuple-element.62.refs_0_), channel_id=1, source_target_pairs={{0,64},{8,72},{16,80},{24,88},{32,96},{40,104},{48,112},{56,120},{... | collective-permute-start | bytes 1228808 | tf_op jit(solution)/shard_map/ppermute | solution.py:458
  85.5 3.5 %collective-permute-start.7 = (f32[1,192,128]{2,1,0:T(8,128)S(1)}, f32[1,192,128]{2,1,0:T(8,128)S(1)}, u32[]{:S(2)}, u32[]{:S(2)}) collective-permute-start(f32[1,192,128]{2,1,0:T(8,128)S(1)} %copy-done.10), channel_id=1, source_target_pairs={{0,1},{1,0},{2,3},{3,2},{4,5},{5,4},{6,7},{7,6},{8,9},{9,8},{10,11... | collective-permute-start | bytes 294920 | tf_op jit(solution)/shard_map/ppermute | solution.py:424
  86.2 18.0 %collective-permute-start.23 = (bf16[320,640]{1,0:T(8,128)(2,1)}, bf16[320,640]{1,0:T(8,128)(2,1)S(1)}, u32[]{:S(2)}, u32[]{:S(2)}) collective-permute-start(bf16[320,640]{1,0:T(8,128)(2,1)} %get-tuple-element.62.refs_0_), channel_id=1, source_target_pairs={{0,48},{8,56},{16,0},{24,8},{32,16},{40,24},{48,32},{56,40},{64,11... | collective-permute-start | bytes 1228808 | tf_op jit(solution)/shard_map/ppermute | solution.py:459
  86.2 18.0 %collective-permute-start.22 = (bf16[320,640]{1,0:T(8,128)(2,1)}, bf16[320,640]{1,0:T(8,128)(2,1)S(1)}, u32[]{:S(2)}, u32[]{:S(2)}) collective-permute-start(bf16[320,640]{1,0:T(8,128)(2,1)} %get-tuple-element.62.refs_0_), channel_id=1, source_target_pairs={{0,16},{8,24},{16,32},{24,40},{32,48},{40,56},{48,0},{56,8},{64,80... | collective-permute-start | bytes 1228808 | tf_op jit(solution)/shard_map/ppermute | solution.py:459
  92.4 16.4 %collective-permute-start.21 = (bf16[320,640]{1,0:T(8,128)(2,1)}, bf16[320,640]{1,0:T(8,128)(2,1)S(1)}, u32[]{:S(2)}, u32[]{:S(2)}) collective-permute-start(bf16[320,640]{1,0:T(8,128)(2,1)} %gate.2.refs_3_), channel_id=1, source_target_pairs={{0,48},{8,56},{16,0},{24,8},{32,16},{40,24},{48,32},{56,40},{64,11... | collective-permute-start | bytes 1228808 | tf_op jit(solution)/shard_map/ppermute | solution.py:467
  92.4 16.4 %collective-permute-start.20 = (bf16[320,640]{1,0:T(8,128)(2,1)}, bf16[320,640]{1,0:T(8,128)(2,1)S(1)}, u32[]{:S(2)}, u32[]{:S(2)}) collective-permute-start(bf16[320,640]{1,0:T(8,128)(2,1)} %gate.2.refs_3_), channel_id=1, source_target_pairs={{0,16},{8,24},{16,32},{24,40},{32,48},{40,56},{48,0},{56,8},{64,80... | collective-permute-start | bytes 1228808 | tf_op jit(solution)/shard_map/ppermute | solution.py:467
  93.9 7.8 %collective-permute-start.8 = (f32[2,192,128]{2,1,0:T(8,128)}, f32[2,192,128]{2,1,0:T(8,128)S(1)}, u32[]{:S(2)}, u32[]{:S(2)}) collective-permute-start(f32[2,192,128]{2,1,0:T(8,128)} %join.6.unread_ref.refs_0_.refs_1_), channel_id=1, source_target_pairs={{0,2},{1,3},{2,0},{3,1},{4,6},{5,7},{6,4},{7,5},{8,10},{9,11},{10,... | collective-permute-start | bytes 589832 | tf_op jit(solution)/shard_map/ppermute | solution.py:424
  104.2 11.0 %collective-permute-start.18 = (f32[4,192,128]{2,1,0:T(8,128)}, f32[4,192,128]{2,1,0:T(8,128)S(1)}, u32[]{:S(2)}, u32[]{:S(2)}) collective-permute-start(f32[4,192,128]{2,1,0:T(8,128)} %join.7), channel_id=1, source_target_pairs={{0,4},{1,5},{2,6},{3,7},{4,0},{5,1},{6,2},{7,3},{8,12},{9,13},{10,... | collective-permute-start | bytes 1179656 | tf_op jit(solution)/shard_map/ppermute | solution.py:424
  107.6 13.8 %collective-permute-start.25 = (bf16[192,640]{1,0:T(8,128)(2,1)}, bf16[192,640]{1,0:T(8,128)(2,1)S(1)}, u32[]{:S(2)}, u32[]{:S(2)}) collective-permute-start(bf16[192,640]{1,0:T(8,128)(2,1)} %get-tuple-element.71), channel_id=1, source_target_pairs={{0,48},{8,56},{16,0},{24,8},{32,16},{40,24},{48,32},{56,40},{64,11... | collective-permute-start | bytes 737288 | tf_op jit(solution)/shard_map/ppermute | solution.py:465
  112.3 9.2 %collective-permute-start.26 = (bf16[192,640]{1,0:T(8,128)(2,1)}, bf16[192,640]{1,0:T(8,128)(2,1)S(1)}, u32[]{:S(2)}, u32[]{:S(2)}) collective-permute-start(bf16[192,640]{1,0:T(8,128)(2,1)} %get-tuple-element.63.refs_0_), channel_id=1, source_target_pairs={{0,16},{8,24},{16,32},{24,40},{32,48},{40,56},{48,0},{56,8},{64,80... | collective-permute-start | bytes 737288 | tf_op jit(solution)/shard_map/ppermute | solution.py:469
  112.5 8.9 %collective-permute-start.24 = (bf16[128,640]{1,0:T(8,128)(2,1)}, bf16[128,640]{1,0:T(8,128)(2,1)S(1)}, u32[]{:S(2)}, u32[]{:S(2)}) collective-permute-start(bf16[128,640]{1,0:T(8,128)(2,1)} %get-tuple-element.70), channel_id=1, source_target_pairs={{0,16},{8,24},{16,32},{24,40},{32,48},{40,56},{48,0},{56,8},{64,80... | collective-permute-start | bytes 491528 | tf_op jit(solution)/shard_map/ppermute | solution.py:465
  112.6 8.9 %collective-permute-start.27 = (bf16[128,640]{1,0:T(8,128)(2,1)}, bf16[128,640]{1,0:T(8,128)(2,1)S(1)}, u32[]{:S(2)}, u32[]{:S(2)}) collective-permute-start(bf16[128,640]{1,0:T(8,128)(2,1)} %get-tuple-element.72), channel_id=1, source_target_pairs={{0,48},{8,56},{16,0},{24,8},{32,16},{40,24},{48,32},{56,40},{64,11... | collective-permute-start | bytes 491528 | tf_op jit(solution)/shard_map/ppermute | solution.py:469
  122.3 13.3 %collective-permute-start.28 = (bf16[320,640]{1,0:T(8,128)(2,1)}, bf16[320,640]{1,0:T(8,128)(2,1)S(1)}, u32[]{:S(2)}, u32[]{:S(2)}) collective-permute-start(bf16[320,640]{1,0:T(8,128)(2,1)} %get-tuple-element.73.refs_0_), channel_id=1, source_target_pairs={{0,8},{8,0},{16,24},{24,16},{32,40},{40,32},{48,56},{56,48},{64,72... | collective-permute-start | bytes 1228808 | tf_op jit(solution)/shard_map/ppermute | solution.py:474
  132.0 3.1 %collective-permute-start.36 = (bf16[192,640]{1,0:T(8,128)(2,1)}, bf16[192,640]{1,0:T(8,128)(2,1)S(1)}, u32[]{:S(2)}, u32[]{:S(2)}) collective-permute-start(bf16[192,640]{1,0:T(8,128)(2,1)} %copy-done.12), channel_id=1, source_target_pairs={{0,8},{8,0},{16,24},{24,16},{32,40},{40,32},{48,56},{56,48},{64,72... | collective-permute-start | bytes 737288 | tf_op jit(solution)/shard_map/ppermute | solution.py:474
  132.0 3.4 %collective-permute-start.35 = (bf16[192,640]{1,0:T(8,128)(2,1)}, bf16[192,640]{1,0:T(8,128)(2,1)S(1)}, u32[]{:S(2)}, u32[]{:S(2)}) collective-permute-start(bf16[192,640]{1,0:T(8,128)(2,1)} %get-tuple-element.80.refs_7_), channel_id=1, source_target_pairs={{0,8},{8,0},{16,24},{24,16},{32,40},{40,32},{48,56},{56,48},{64,72... | collective-permute-start | bytes 737288 | tf_op jit(solution)/shard_map/ppermute | solution.py:474
  135.4 2.8 %collective-permute-start.32 = (bf16[320,640]{1,0:T(8,128)(2,1)}, bf16[320,640]{1,0:T(8,128)(2,1)S(1)}, u32[]{:S(2)}, u32[]{:S(2)}) collective-permute-start(bf16[320,640]{1,0:T(8,128)(2,1)} %get-tuple-element.77.refs_4_), channel_id=1, source_target_pairs={{0,8},{8,0},{16,24},{24,16},{32,40},{40,32},{48,56},{56,48},{64,72... | collective-permute-start | bytes 1228808 | tf_op jit(solution)/shard_map/ppermute | solution.py:474
  135.7 3.2 %collective-permute-start.33 = (bf16[320,640]{1,0:T(8,128)(2,1)}, bf16[320,640]{1,0:T(8,128)(2,1)S(1)}, u32[]{:S(2)}, u32[]{:S(2)}) collective-permute-start(bf16[320,640]{1,0:T(8,128)(2,1)} %get-tuple-element.78.refs_5_), channel_id=1, source_target_pairs={{0,8},{8,0},{16,24},{24,16},{32,40},{40,32},{48,56},{56,48},{64,72... | collective-permute-start | bytes 1228808 | tf_op jit(solution)/shard_map/ppermute | solution.py:474
  (51 other events, 133.8 us)

commit v6 on v5

--- a/solution.py
+++ b/solution.py
@@ -28,7 +28,7 @@
 ROUND = 1.5 * 2.0**23
 NUDGE = 1.0 + 2.0**-21
 
-limit = pltpu.CompilerParams(vmem_limit_bytes=56 * 2**20)
+limit = pltpu.CompilerParams(vmem_limit_bytes=62 * 2**20)
 brief = pl.CostEstimate(flops=1, bytes_accessed=1, transcendentals=0)
 unread = pl.BlockSpec(memory_space=pl.ANY)
 

time: 150 us -> 150 us (level)
  other arithmetic: 2.33 us -> 4.27 us
  local copies, waits for them, and re-layouts: 24.5 us -> 22.8 us
    unnamed x92 -> x74, local copies, waits for them, and re-layouts: 19.6 us -> 17.9 us
  transfers between devices with their start and end apart: 38 -> 38, of which waited for: 12 -> 11; matrix products, arithmetic and copies ran while one was open for 6% -> 8% of each run, Pallas kernels for 23% -> 23%
where the time goes in v6:
time: 150 us; the launch traced here: 149 us
  Pallas kernels  60.1 us (40%)
  starting transfers between devices  45.2 us (30%)
  local copies, waits for them, and re-layouts  22.8 us (15%)
  waiting for transfers between devices  15.8 us (11%)
  other arithmetic  4.27 us (3%)
    unnamed x74, local copies, waits for them, and re-layouts  17.9 us
    ppermute x10, starting transfers between devices, per_device(): theirs = [to_sibling(part) for part in mine]  12.4 us
    pallas_call x1, Pallas kernels, quantize(): pl.pallas_call(quant_kernel, grid_spec=pltpu.PrefetchScalarGridSpec(num_s...  11.7 us
    ppermute x9, starting transfers between devices, across(): return lax.ppermute(value, 'fsdp', [(i, i ^ bit) for i in range(N_FSDP)])  11.3 us
    pallas_call x1, Pallas kernels, place(): pl.pallas_call(functools.partial(place_kernel, chips), grid_spec=pltpu.Pr...  8.59 us
    pallas_call x4, Pallas kernels, join(): pl.pallas_call(functools.partial(join_kernel, len(after)), in_specs=[pl.B...  6.09 us
    pallas_call x1, Pallas kernels, finish(): pl.pallas_call(functools.partial(finish_kernel, len(after)), in_specs=[pl...  5.44 us
    ppermute x2, starting transfers between devices, ring(): send(messages[1], perm=to_y(-1))  5.37 us
  transfers between devices with their start and end apart: 38, of which 11 were waited for; matrix products, arithmetic and copies ran while one was open for 8% of the time, Pallas kernels for 23%

profile of v6, /device:TPU:1, one launch (start us, length us, event | category | flops | bytes accessed | tf_op | source)
XLA Modules:
  0.0 149.3 jit_solution(3290854814454864174)
XLA Ops:
  1.3 11.7 %quantize.1 = (bf16[8,320,640]{2,1,0:T(8,128)(2,1)}, bf16[8,320,640]{2,1,0:T(8,128)(2,1)}) custom-call(s32[3]{0:T(128)} %pad_add_fusion.pos_ref, bf16[640,5120]{1,0:T(8,128)(2,1)} %start_ref.1, bf16[640,5120]{1,0:T(8,128)(2,1)} %bitcast.38), custom_call_target="tpu_custom_call" | custom-call | flops 1 | bytes 1 | tf_op jit(solution)/shard_map/quantize/pallas_call | solution.py:89
  14.8 1.8 %collective-permute-start = (f32[1,16,128]{2,1,0:T(8,128)S(1)}, f32[1,16,128]{2,1,0:T(8,128)S(1)}, u32[]{:S(2)}, u32[]{:S(2)}) collective-permute-start(f32[1,16,128]{2,1,0:T(8,128)S(1)} %maximum_bitcast_fusion.refs_0_), channel_id=1, source_target_pairs={{0,1},{1,0},{2,3},{3,2},{4,5},{5,4},{6,7},{7,6},{8,9},{9,8},{10,11... | collective-permute-start | bytes 24584 | tf_op jit(solution)/shard_map/ppermute | solution.py:424
  19.5 3.4 %collective-permute-start.1 = (f32[2,16,128]{2,1,0:T(8,128)}, f32[2,16,128]{2,1,0:T(8,128)S(1)}, u32[]{:S(2)}, u32[]{:S(2)}) collective-permute-start(f32[2,16,128]{2,1,0:T(8,128)} %join.4.refs_0_), channel_id=1, source_target_pairs={{0,2},{1,3},{2,0},{3,1},{4,6},{5,7},{6,4},{7,5},{8,10},{9,11},{10,... | collective-permute-start | bytes 49160 | tf_op jit(solution)/shard_map/ppermute | solution.py:424
  23.0 2.4 %first_messages.2 = (bf16[2,160,640]{2,1,0:T(8,128)(2,1)}, bf16[2,160,640]{2,1,0:T(8,128)(2,1)}) custom-call(bf16[4,2,320,640]{3,2,1,0:T(8,128)(2,1)} %bitcast.26, bf16[4,2,320,640]{3,2,1,0:T(8,128)(2,1)} %collective-permute-done.2.refs_1_.refs_3_.refs_5_.got1.got3.got, bf16[4,2,320,640]{3,2,1,0:T(8,128)(2,1)} %bitcast.27, ...), custom_call_target="tpu_custom_call" | custom-call | flops 1 | bytes 1 | tf_op jit(solution)/shard_map/first_messages/pallas_call | solution.py:326
  28.6 2.7 %collective-permute-start.10 = (bf16[2,160,640]{2,1,0:T(8,128)(2,1)}, bf16[2,160,640]{2,1,0:T(8,128)(2,1)S(1)}, u32[]{:S(2)}, u32[]{:S(2)}) collective-permute-start(bf16[2,160,640]{2,1,0:T(8,128)(2,1)} %get-tuple-element.49), channel_id=1, source_target_pairs={{0,48},{8,56},{16,0},{24,8},{32,16},{40,24},{48,32},{56,40},{64,11... | collective-permute-start | bytes 1228808 | tf_op jit(solution)/shard_map/ppermute | solution.py:435
  31.9 4.9 %weight_products.1 = (f32[4,192,128]{2,1,0:T(8,128)}, f32[4,192,128]{2,1,0:T(8,128)}, f32[32,640]{1,0:T(8,128)}, f32[64,640]{1,0:T(8,128)}, f32[32,256]{1,0:T(8,128)}) custom-call(f32[4,16,128]{2,1,0:T(8,128)} %join.5.near_heads, f32[4,16,128]{2,1,0:T(8,128)} %copy-done.32, f32[64,640]{1,0:T(8,128)} %bitcast.45, f32[64,640]{1,0:T(8,128)} %bitcast.47, ...), custom_call_target="tpu_custom_call" | custom-call | flops 1 | bytes 1 | tf_op jit(solution)/shard_map/weight_products/pallas_call | solution.py:663
  38.7 3.0 %collective-permute-done.9.up = bf16[2,160,640]{2,1,0:T(8,128)(2,1)S(1)} collective-permute-done((bf16[2,160,640]{2,1,0:T(8,128)(2,1)}, bf16[2,160,640]{2,1,0:T(8,128)(2,1)S(1)}, u32[]{:S(2)}, u32[]{:S(2)}) %collective-permute-start.9) | collective-permute-done | bytes 409632 | tf_op jit(solution)/shard_map/ppermute | solution.py:435
  42.4 2.2 %second_messages.2 = (bf16[160,640]{1,0:T(8,128)(2,1)}, bf16[160,640]{1,0:T(8,128)(2,1)}) custom-call(bf16[4,2,320,640]{3,2,1,0:T(8,128)(2,1)} %bitcast.29, bf16[4,2,320,640]{3,2,1,0:T(8,128)(2,1)} %collective-permute-done.2.refs_1_.refs_3_.refs_5_.got1.got3.got, bf16[4,2,320,640]{3,2,1,0:T(8,128)(2,1)} %bitcast.30, ...), custom_call_target="tpu_custom_call" | custom-call | flops 1 | bytes 1 | tf_op jit(solution)/shard_map/second_messages/pallas_call | solution.py:353
  46.1 2.4 %first_messages.3 = (bf16[2,160,640]{2,1,0:T(8,128)(2,1)}, bf16[2,160,640]{2,1,0:T(8,128)(2,1)}) custom-call(bf16[4,2,320,640]{3,2,1,0:T(8,128)(2,1)} %bitcast.31, bf16[4,2,320,640]{3,2,1,0:T(8,128)(2,1)} %collective-permute-done.2.refs_1_.refs_3_.refs_5_.got1.got3.got, bf16[4,2,320,640]{3,2,1,0:T(8,128)(2,1)} %bitcast.32, ...), custom_call_target="tpu_custom_call" | custom-call | flops 1 | bytes 1 | tf_op jit(solution)/shard_map/first_messages/pallas_call | solution.py:326
  48.6 2.6 %collective-permute-start.12 = (bf16[2,160,640]{2,1,0:T(8,128)(2,1)}, bf16[2,160,640]{2,1,0:T(8,128)(2,1)S(1)}, u32[]{:S(2)}, u32[]{:S(2)}) collective-permute-start(bf16[2,160,640]{2,1,0:T(8,128)(2,1)} %get-tuple-element.52), channel_id=1, source_target_pairs={{0,48},{8,56},{16,0},{24,8},{32,16},{40,24},{48,32},{56,40},{64,11... | collective-permute-start | bytes 1228808 | tf_op jit(solution)/shard_map/ppermute | solution.py:435
  51.3 1.6 %slice_add_fusion = f32[2,192,128]{2,1,0:T(8,128)} fusion(f32[4,192,128]{2,1,0:T(8,128)} %collective-permute-done.4, f32[4,192,128]{2,1,0:T(8,128)S(1)} %copy-done.22), kind=kLoop, calls=%fused_computation | loop fusion | flops 49152 | bytes 589824 | tf_op jit(solution)/shard_map/add | solution.py:443
  53.9 2.4 %chip_sum.1 = bf16[320,640]{1,0:T(8,128)(2,1)} custom-call(bf16[4,2,320,640]{3,2,1,0:T(8,128)(2,1)} %bitcast.34, bf16[4,2,320,640]{3,2,1,0:T(8,128)(2,1)} %collective-permute-done.2.refs_1_.refs_3_.refs_5_.got1.got3.got, bf16[2,160,640]{2,1,0:T(8,128)(2,1)} %copy-done.8, bf16[2,160,640]{2,1,0:T(8,128)(2,1)} %copy-done.7, ...), custom_call_target="tpu_custom_call" | custom-call | flops 1 | bytes 1 | tf_op jit(solution)/shard_map/chip_sum/pallas_call | solution.py:376
  56.2 2.5 %collective-permute-start.17 = (bf16[320,640]{1,0:T(8,128)(2,1)}, bf16[320,640]{1,0:T(8,128)(2,1)}, u32[]{:S(2)}, u32[]{:S(2)}) collective-permute-start(bf16[320,640]{1,0:T(8,128)(2,1)} %chip_sum.1), channel_id=1, source_target_pairs={{0,64},{8,72},{16,80},{24,88},{32,96},{40,104},{48,112},{56,120},{... | collective-permute-start | bytes 1228808 | tf_op jit(solution)/shard_map/ppermute | solution.py:449
  60.0 2.4 %copy.30.refs_1_.momentum_ref = f32[640,320]{1,0:T(8,128)} copy(f32[640,320]{0,1:T(8,128)} %param.19) | data formatting | bytes 1638400 | tf_op args[8]
  64.0 2.2 %second_messages.3 = (bf16[160,640]{1,0:T(8,128)(2,1)}, bf16[160,640]{1,0:T(8,128)(2,1)}) custom-call(bf16[4,2,320,640]{3,2,1,0:T(8,128)(2,1)} %bitcast.35, bf16[4,2,320,640]{3,2,1,0:T(8,128)(2,1)} %collective-permute-done.2.refs_1_.refs_3_.refs_5_.got1.got3.got, bf16[4,2,320,640]{3,2,1,0:T(8,128)(2,1)} %bitcast.36, ...), custom_call_target="tpu_custom_call" | custom-call | flops 1 | bytes 1 | tf_op jit(solution)/shard_map/second_messages/pallas_call | solution.py:353
  66.2 2.7 %collective-permute-start.14 = (bf16[160,640]{1,0:T(8,128)(2,1)}, bf16[160,640]{1,0:T(8,128)(2,1)S(1)}, u32[]{:S(2)}, u32[]{:S(2)}) collective-permute-start(bf16[160,640]{1,0:T(8,128)(2,1)} %get-tuple-element.54), channel_id=1, source_target_pairs={{0,48},{8,56},{16,0},{24,8},{32,16},{40,24},{48,32},{56,40},{64,11... | collective-permute-start | bytes 614408 | tf_op jit(solution)/shard_map/ppermute | solution.py:451
  68.8 1.7 %slice_add_fusion.1 = (f32[1,192,128]{2,1,0:T(8,128)S(1)}, f32[1,192,128]{2,1,0:T(8,128)}) fusion(f32[2,192,128]{2,1,0:T(8,128)} %collective-permute-done.5, f32[4,192,128]{2,1,0:T(8,128)} %collective-permute-done.4, f32[4,192,128]{2,1,0:T(8,128)S(1)} %copy-done.22), kind=kLoop, calls=%fused_computation.2 | loop fusion | flops 98304 | bytes 786432 | tf_op jit(solution)/shard_map/add | solution.py:444
  71.3 2.7 %collective-permute-done.6.away_ref = f32[1,192,128]{2,1,0:T(8,128)S(1)} collective-permute-done((f32[1,192,128]{2,1,0:T(8,128)S(1)}, f32[1,192,128]{2,1,0:T(8,128)S(1)}, u32[]{:S(2)}, u32[]{:S(2)}) %collective-permute-start.6) | collective-permute-done | bytes 98336 | tf_op jit(solution)/shard_map/ppermute | solution.py:424
  74.7 3.0 %token_sums.1.refs_0_.unread_ref.parts0 = f32[1,192,128]{2,1,0:T(8,128)} custom-call(f32[1,192,128]{2,1,0:T(8,128)} %get-tuple-element.82.own_ref, f32[1,192,128]{2,1,0:T(8,128)} %copy-done.30, bf16[64,2048]{1,0:T(8,128)(2,1)} %bitcast.49, bf16[64,2048]{1,0:T(8,128)(2,1)} %bitcast.50), custom_call_target="tpu_custom_call" | custom-call | flops 1 | bytes 1 | tf_op jit(solution)/shard_map/token_sums/pallas_call | solution.py:681
  79.1 4.4 %outer_update.1 = (f32[640,320]{1,0:T(8,128)}, f32[640,320]{1,0:T(8,128)}, bf16[320,640]{1,0:T(8,128)(2,1)}) custom-call(s32[3]{0:T(128)} %pad_add_fusion.pos_ref, bf16[4,2,320,640]{3,2,1,0:T(8,128)(2,1)} %bitcast.37, bf16[4,2,320,640]{3,2,1,0:T(8,128)(2,1)} %collective-permute-done.2.refs_1_.refs_3_.refs_5_.got1.got3.got, bf16[2,160,640]{2,1,0:T(8,128)(2,1)} %copy-done.5, ...), custom_call_target="tpu_custom_call" | custom-call | flops 1 | bytes 1 | tf_op jit(solution)/shard_map/outer_update/pallas_call | solution.py:151
  88.6 1.6 %join.6.unread_ref.refs_0_.refs_1_ = f32[2,192,128]{2,1,0:T(8,128)} custom-call(f32[1,192,128]{2,1,0:T(8,128)} %token_sums.1.refs_0_.unread_ref.parts0, f32[1,192,128]{2,1,0:T(8,128)} %copy-done.21), custom_call_target="tpu_custom_call" | custom-call | flops 1 | bytes 1 | tf_op jit(solution)/shard_map/join/pallas_call | solution.py:256
  90.2 1.7 %collective-permute-done.19.refs_0_ = bf16[320,640]{1,0:T(8,128)(2,1)S(1)} collective-permute-done((bf16[320,640]{1,0:T(8,128)(2,1)}, bf16[320,640]{1,0:T(8,128)(2,1)S(1)}, u32[]{:S(2)}, u32[]{:S(2)}) %collective-permute-start.19) | collective-permute-done | bytes 409632 | tf_op jit(solution)/shard_map/ppermute | solution.py:458
  94.2 2.3 %collective-permute-start.8 = (f32[2,192,128]{2,1,0:T(8,128)}, f32[2,192,128]{2,1,0:T(8,128)S(1)}, u32[]{:S(2)}, u32[]{:S(2)}) collective-permute-start(f32[2,192,128]{2,1,0:T(8,128)} %join.6.unread_ref.refs_0_.refs_1_), channel_id=1, source_target_pairs={{0,2},{1,3},{2,0},{3,1},{4,6},{5,7},{6,4},{7,5},{8,10},{9,11},{10,... | collective-permute-start | bytes 589832 | tf_op jit(solution)/shard_map/ppermute | solution.py:424
  96.5 2.4 %copy.33 = f32[640,320]{0,1:T(8,128)} copy(f32[640,320]{1,0:T(8,128)} %get-tuple-element.56) | data formatting | bytes 1638400 | tf_op jit(solution)/shard_map/outer_update/pallas_call | solution.py:151
  98.9 2.4 %copy.34 = f32[640,320]{0,1:T(8,128)} copy(f32[640,320]{1,0:T(8,128)} %get-tuple-element.57) | data formatting | bytes 1638400 | tf_op jit(solution)/shard_map/outer_update/pallas_call | solution.py:151
  102.6 1.8 %join.7 = f32[4,192,128]{2,1,0:T(8,128)} custom-call(f32[2,192,128]{2,1,0:T(8,128)} %join.6.unread_ref.refs_0_.refs_1_, f32[2,192,128]{2,1,0:T(8,128)} %copy-done.14, f32[8,128]{1,0:T(8,128)} %get-tuple-element.58.refs_2_.refs_11_.refs_21_), custom_call_target="tpu_custom_call" | custom-call | flops 1 | bytes 1 | tf_op jit(solution)/shard_map/join/pallas_call | solution.py:256
  105.9 1.9 %parts.3 = (bf16[128,640]{1,0:T(8,128)(2,1)}, bf16[192,640]{1,0:T(8,128)(2,1)}) custom-call(bf16[320,640]{1,0:T(8,128)(2,1)} %copy-done.1, bf16[320,640]{1,0:T(8,128)(2,1)} %copy-done), custom_call_target="tpu_custom_call" | custom-call | flops 1 | bytes 1 | tf_op jit(solution)/shard_map/parts/pallas_call | solution.py:237
  110.6 1.9 %parts.2 = (bf16[192,640]{1,0:T(8,128)(2,1)}, bf16[128,640]{1,0:T(8,128)(2,1)}) custom-call(bf16[320,640]{1,0:T(8,128)(2,1)} %copy-done.3, bf16[320,640]{1,0:T(8,128)(2,1)} %copy-done.2), custom_call_target="tpu_custom_call" | custom-call | flops 1 | bytes 1 | tf_op jit(solution)/shard_map/parts/pallas_call | solution.py:237
  112.8 2.6 %collective-permute-start.27 = (bf16[128,640]{1,0:T(8,128)(2,1)}, bf16[128,640]{1,0:T(8,128)(2,1)S(1)}, u32[]{:S(2)}, u32[]{:S(2)}) collective-permute-start(bf16[128,640]{1,0:T(8,128)(2,1)} %get-tuple-element.72), channel_id=1, source_target_pairs={{0,48},{8,56},{16,0},{24,8},{32,16},{40,24},{48,32},{56,40},{64,11... | collective-permute-start | bytes 491528 | tf_op jit(solution)/shard_map/ppermute | solution.py:469
  116.2 5.4 %finish.1 = (f32[64,640]{1,0:T(8,128)}, f32[64,640]{1,0:T(8,128)}, f32[2,640]{1,0:T(2,128)}, f32[256,640]{1,0:T(8,128)}) custom-call(f32[1,192,128]{2,1,0:T(8,128)} %token_sums.1.refs_0_.unread_ref.parts0, f32[1,192,128]{2,1,0:T(8,128)} %copy-done.21, f32[2,192,128]{2,1,0:T(8,128)} %copy-done.14, f32[4,192,128]{2,1,0:T(8,128)} %copy-done.23, ...), custom_call_target="tpu_custom_call" | custom-call | flops 1 | bytes 1 | tf_op jit(solution)/shard_map/finish/pallas_call | solution.py:694
  122.5 9.9 %collective-permute-start.28 = (bf16[320,640]{1,0:T(8,128)(2,1)}, bf16[320,640]{1,0:T(8,128)(2,1)S(1)}, u32[]{:S(2)}, u32[]{:S(2)}) collective-permute-start(bf16[320,640]{1,0:T(8,128)(2,1)} %get-tuple-element.73.refs_0_), channel_id=1, source_target_pairs={{0,8},{8,0},{16,24},{24,16},{32,40},{40,32},{48,56},{56,48},{64,72... | collective-permute-start | bytes 1228808 | tf_op jit(solution)/shard_map/ppermute | solution.py:474
  140.6 8.6 %place.1 = bf16[640,5120]{1,0:T(8,128)(2,1)} custom-call(s32[3]{0:T(128)} %pad_add_fusion.pos_ref, bf16[320,640]{1,0:T(8,128)(2,1)} %get-tuple-element.73.refs_0_, bf16[320,640]{1,0:T(8,128)(2,1)} %get-tuple-element.74.refs_1_, bf16[320,640]{1,0:T(8,128)(2,1)} %get-tuple-element.75.refs_2_, bf16[320,640]{1,0:T(8,128)(2,1)} %get-tuple-element.76.refs_3_, ...), custom_call_target="tpu_custom_call" | custom-call | flops 1 | bytes 1 | tf_op jit(solution)/shard_map/place/pallas_call | solution.py:214
  (151 shorter events, 42.8 us)
Async XLA Ops:
  13.0 10.0 %collective-permute-start.2 = (bf16[4,2,320,640]{3,2,1,0:T(8,128)(2,1)}, bf16[4,2,320,640]{3,2,1,0:T(8,128)(2,1)}, u32[]{:S(2)}, u32[]{:S(2)}) collective-permute-start(bf16[4,2,320,640]{3,2,1,0:T(8,128)(2,1)} %bitcast.54), channel_id=1, source_target_pairs={{0,8},{8,0},{16,24},{24,16},{32,40},{40,32},{48,56},{56,48},{64,72... | collective-permute-start | bytes 9830408 | tf_op jit(solution)/shard_map/ppermute | solution.py:429
  19.5 5.9 %collective-permute-start.1 = (f32[2,16,128]{2,1,0:T(8,128)}, f32[2,16,128]{2,1,0:T(8,128)S(1)}, u32[]{:S(2)}, u32[]{:S(2)}) collective-permute-start(f32[2,16,128]{2,1,0:T(8,128)} %join.4.refs_0_), channel_id=1, source_target_pairs={{0,2},{1,3},{2,0},{3,1},{4,6},{5,7},{6,4},{7,5},{8,10},{9,11},{10,... | collective-permute-start | bytes 49160 | tf_op jit(solution)/shard_map/ppermute | solution.py:424
  27.4 4.0 %collective-permute-start.3 = (f32[4,16,128]{2,1,0:T(8,128)}, f32[4,16,128]{2,1,0:T(8,128)S(1)}, u32[]{:S(2)}, u32[]{:S(2)}) collective-permute-start(f32[4,16,128]{2,1,0:T(8,128)} %join.5.near_heads), channel_id=1, source_target_pairs={{0,4},{1,5},{2,6},{3,7},{4,0},{5,1},{6,2},{7,3},{8,12},{9,13},{10,... | collective-permute-start | bytes 98312 | tf_op jit(solution)/shard_map/ppermute | solution.py:424
  28.6 10.1 %collective-permute-start.10 = (bf16[2,160,640]{2,1,0:T(8,128)(2,1)}, bf16[2,160,640]{2,1,0:T(8,128)(2,1)S(1)}, u32[]{:S(2)}, u32[]{:S(2)}) collective-permute-start(bf16[2,160,640]{2,1,0:T(8,128)(2,1)} %get-tuple-element.49), channel_id=1, source_target_pairs={{0,48},{8,56},{16,0},{24,8},{32,16},{40,24},{48,32},{56,40},{64,11... | collective-permute-start | bytes 1228808 | tf_op jit(solution)/shard_map/ppermute | solution.py:435
  31.3 10.4 %collective-permute-start.9 = (bf16[2,160,640]{2,1,0:T(8,128)(2,1)}, bf16[2,160,640]{2,1,0:T(8,128)(2,1)S(1)}, u32[]{:S(2)}, u32[]{:S(2)}) collective-permute-start(bf16[2,160,640]{2,1,0:T(8,128)(2,1)} %get-tuple-element.46.refs_2_.refs_0_), channel_id=1, source_target_pairs={{0,16},{8,24},{16,32},{24,40},{32,48},{40,56},{48,0},{56,8},{64,80... | collective-permute-start | bytes 1228808 | tf_op jit(solution)/shard_map/ppermute | solution.py:435
  36.8 14.5 %collective-permute-start.4 = (f32[4,192,128]{2,1,0:T(8,128)}, f32[4,192,128]{2,1,0:T(8,128)}, u32[]{:S(2)}, u32[]{:S(2)}) collective-permute-start(f32[4,192,128]{2,1,0:T(8,128)} %get-tuple-element.48), channel_id=1, source_target_pairs={{0,4},{1,5},{2,6},{3,7},{4,0},{5,1},{6,2},{7,3},{8,12},{9,13},{10,... | collective-permute-start | bytes 1179656 | tf_op jit(solution)/shard_map/ppermute | solution.py:424
  44.7 9.2 %collective-permute-start.16 = (bf16[160,640]{1,0:T(8,128)(2,1)}, bf16[160,640]{1,0:T(8,128)(2,1)}, u32[]{:S(2)}, u32[]{:S(2)}) collective-permute-start(bf16[160,640]{1,0:T(8,128)(2,1)} %get-tuple-element.55), channel_id=1, source_target_pairs={{0,48},{8,56},{16,0},{24,8},{32,16},{40,24},{48,32},{56,40},{64,11... | collective-permute-start | bytes 614408 | tf_op jit(solution)/shard_map/ppermute | solution.py:447
  45.7 8.2 %collective-permute-start.15 = (bf16[160,640]{1,0:T(8,128)(2,1)}, bf16[160,640]{1,0:T(8,128)(2,1)}, u32[]{:S(2)}, u32[]{:S(2)}) collective-permute-start(bf16[160,640]{1,0:T(8,128)(2,1)} %get-tuple-element.50.refs_6_), channel_id=1, source_target_pairs={{0,16},{8,24},{16,32},{24,40},{32,48},{40,56},{48,0},{56,8},{64,80... | collective-permute-start | bytes 614408 | tf_op jit(solution)/shard_map/ppermute | solution.py:447
  48.6 13.9 %collective-permute-start.11 = (bf16[2,160,640]{2,1,0:T(8,128)(2,1)}, bf16[2,160,640]{2,1,0:T(8,128)(2,1)S(1)}, u32[]{:S(2)}, u32[]{:S(2)}) collective-permute-start(bf16[2,160,640]{2,1,0:T(8,128)(2,1)} %get-tuple-element.51), channel_id=1, source_target_pairs={{0,16},{8,24},{16,32},{24,40},{32,48},{40,56},{48,0},{56,8},{64,80... | collective-permute-start | bytes 1228808 | tf_op jit(solution)/shard_map/ppermute | solution.py:435
  48.6 13.8 %collective-permute-start.12 = (bf16[2,160,640]{2,1,0:T(8,128)(2,1)}, bf16[2,160,640]{2,1,0:T(8,128)(2,1)S(1)}, u32[]{:S(2)}, u32[]{:S(2)}) collective-permute-start(bf16[2,160,640]{2,1,0:T(8,128)(2,1)} %get-tuple-element.52), channel_id=1, source_target_pairs={{0,48},{8,56},{16,0},{24,8},{32,16},{40,24},{48,32},{56,40},{64,11... | collective-permute-start | bytes 1228808 | tf_op jit(solution)/shard_map/ppermute | solution.py:435
  52.9 15.9 %collective-permute-start.5 = (f32[2,192,128]{2,1,0:T(8,128)}, f32[2,192,128]{2,1,0:T(8,128)}, u32[]{:S(2)}, u32[]{:S(2)}) collective-permute-start(f32[2,192,128]{2,1,0:T(8,128)} %slice_add_fusion), channel_id=1, source_target_pairs={{0,2},{1,3},{2,0},{3,1},{4,6},{5,7},{6,4},{7,5},{8,10},{9,11},{10,... | collective-permute-start | bytes 589832 | tf_op jit(solution)/shard_map/ppermute | solution.py:424
  56.2 21.4 %collective-permute-start.17 = (bf16[320,640]{1,0:T(8,128)(2,1)}, bf16[320,640]{1,0:T(8,128)(2,1)}, u32[]{:S(2)}, u32[]{:S(2)}) collective-permute-start(bf16[320,640]{1,0:T(8,128)(2,1)} %chip_sum.1), channel_id=1, source_target_pairs={{0,64},{8,72},{16,80},{24,88},{32,96},{40,104},{48,112},{56,120},{... | collective-permute-start | bytes 1228808 | tf_op jit(solution)/shard_map/ppermute | solution.py:449
  66.2 11.5 %collective-permute-start.13 = (bf16[160,640]{1,0:T(8,128)(2,1)}, bf16[160,640]{1,0:T(8,128)(2,1)S(1)}, u32[]{:S(2)}, u32[]{:S(2)}) collective-permute-start(bf16[160,640]{1,0:T(8,128)(2,1)} %get-tuple-element.53), channel_id=1, source_target_pairs={{0,16},{8,24},{16,32},{24,40},{32,48},{40,56},{48,0},{56,8},{64,80... | collective-permute-start | bytes 614408 | tf_op jit(solution)/shard_map/ppermute | solution.py:451
  66.2 11.5 %collective-permute-start.14 = (bf16[160,640]{1,0:T(8,128)(2,1)}, bf16[160,640]{1,0:T(8,128)(2,1)S(1)}, u32[]{:S(2)}, u32[]{:S(2)}) collective-permute-start(bf16[160,640]{1,0:T(8,128)(2,1)} %get-tuple-element.54), channel_id=1, source_target_pairs={{0,48},{8,56},{16,0},{24,8},{32,16},{40,24},{48,32},{56,40},{64,11... | collective-permute-start | bytes 614408 | tf_op jit(solution)/shard_map/ppermute | solution.py:451
  70.5 3.5 %collective-permute-start.6 = (f32[1,192,128]{2,1,0:T(8,128)S(1)}, f32[1,192,128]{2,1,0:T(8,128)S(1)}, u32[]{:S(2)}, u32[]{:S(2)}) collective-permute-start(f32[1,192,128]{2,1,0:T(8,128)S(1)} %get-tuple-element.81), channel_id=1, source_target_pairs={{0,1},{1,0},{2,3},{3,2},{4,5},{5,4},{6,7},{7,6},{8,9},{9,8},{10,11... | collective-permute-start | bytes 294920 | tf_op jit(solution)/shard_map/ppermute | solution.py:424
  83.4 8.5 %collective-permute-start.19 = (bf16[320,640]{1,0:T(8,128)(2,1)}, bf16[320,640]{1,0:T(8,128)(2,1)S(1)}, u32[]{:S(2)}, u32[]{:S(2)}) collective-permute-start(bf16[320,640]{1,0:T(8,128)(2,1)} %get-tuple-element.62.refs_0_), channel_id=1, source_target_pairs={{0,64},{8,72},{16,80},{24,88},{32,96},{40,104},{48,112},{56,120},{... | collective-permute-start | bytes 1228808 | tf_op jit(solution)/shard_map/ppermute | solution.py:458
  84.5 3.5 %collective-permute-start.7 = (f32[1,192,128]{2,1,0:T(8,128)S(1)}, f32[1,192,128]{2,1,0:T(8,128)S(1)}, u32[]{:S(2)}, u32[]{:S(2)}) collective-permute-start(f32[1,192,128]{2,1,0:T(8,128)S(1)} %copy-done.9), channel_id=1, source_target_pairs={{0,1},{1,0},{2,3},{3,2},{4,5},{5,4},{6,7},{7,6},{8,9},{9,8},{10,11... | collective-permute-start | bytes 294920 | tf_op jit(solution)/shard_map/ppermute | solution.py:424
  85.2 19.2 %collective-permute-start.23 = (bf16[320,640]{1,0:T(8,128)(2,1)}, bf16[320,640]{1,0:T(8,128)(2,1)S(1)}, u32[]{:S(2)}, u32[]{:S(2)}) collective-permute-start(bf16[320,640]{1,0:T(8,128)(2,1)} %get-tuple-element.62.refs_0_), channel_id=1, source_target_pairs={{0,48},{8,56},{16,0},{24,8},{32,16},{40,24},{48,32},{56,40},{64,11... | collective-permute-start | bytes 1228808 | tf_op jit(solution)/shard_map/ppermute | solution.py:459
  85.2 19.2 %collective-permute-start.22 = (bf16[320,640]{1,0:T(8,128)(2,1)}, bf16[320,640]{1,0:T(8,128)(2,1)S(1)}, u32[]{:S(2)}, u32[]{:S(2)}) collective-permute-start(bf16[320,640]{1,0:T(8,128)(2,1)} %get-tuple-element.62.refs_0_), channel_id=1, source_target_pairs={{0,16},{8,24},{16,32},{24,40},{32,48},{40,56},{48,0},{56,8},{64,80... | collective-permute-start | bytes 1228808 | tf_op jit(solution)/shard_map/ppermute | solution.py:459
  92.8 16.3 %collective-permute-start.21 = (bf16[320,640]{1,0:T(8,128)(2,1)}, bf16[320,640]{1,0:T(8,128)(2,1)S(1)}, u32[]{:S(2)}, u32[]{:S(2)}) collective-permute-start(bf16[320,640]{1,0:T(8,128)(2,1)} %gate.2.refs_3_), channel_id=1, source_target_pairs={{0,48},{8,56},{16,0},{24,8},{32,16},{40,24},{48,32},{56,40},{64,11... | collective-permute-start | bytes 1228808 | tf_op jit(solution)/shard_map/ppermute | solution.py:467
  92.8 16.3 %collective-permute-start.20 = (bf16[320,640]{1,0:T(8,128)(2,1)}, bf16[320,640]{1,0:T(8,128)(2,1)S(1)}, u32[]{:S(2)}, u32[]{:S(2)}) collective-permute-start(bf16[320,640]{1,0:T(8,128)(2,1)} %gate.2.refs_3_), channel_id=1, source_target_pairs={{0,16},{8,24},{16,32},{24,40},{32,48},{40,56},{48,0},{56,8},{64,80... | collective-permute-start | bytes 1228808 | tf_op jit(solution)/shard_map/ppermute | solution.py:467
  94.2 7.7 %collective-permute-start.8 = (f32[2,192,128]{2,1,0:T(8,128)}, f32[2,192,128]{2,1,0:T(8,128)S(1)}, u32[]{:S(2)}, u32[]{:S(2)}) collective-permute-start(f32[2,192,128]{2,1,0:T(8,128)} %join.6.unread_ref.refs_0_.refs_1_), channel_id=1, source_target_pairs={{0,2},{1,3},{2,0},{3,1},{4,6},{5,7},{6,4},{7,5},{8,10},{9,11},{10,... | collective-permute-start | bytes 589832 | tf_op jit(solution)/shard_map/ppermute | solution.py:424
  104.4 11.0 %collective-permute-start.18 = (f32[4,192,128]{2,1,0:T(8,128)}, f32[4,192,128]{2,1,0:T(8,128)S(1)}, u32[]{:S(2)}, u32[]{:S(2)}) collective-permute-start(f32[4,192,128]{2,1,0:T(8,128)} %join.7), channel_id=1, source_target_pairs={{0,4},{1,5},{2,6},{3,7},{4,0},{5,1},{6,2},{7,3},{8,12},{9,13},{10,... | collective-permute-start | bytes 1179656 | tf_op jit(solution)/shard_map/ppermute | solution.py:424
  107.9 13.8 %collective-permute-start.25 = (bf16[192,640]{1,0:T(8,128)(2,1)}, bf16[192,640]{1,0:T(8,128)(2,1)S(1)}, u32[]{:S(2)}, u32[]{:S(2)}) collective-permute-start(bf16[192,640]{1,0:T(8,128)(2,1)} %get-tuple-element.71), channel_id=1, source_target_pairs={{0,48},{8,56},{16,0},{24,8},{32,16},{40,24},{48,32},{56,40},{64,11... | collective-permute-start | bytes 737288 | tf_op jit(solution)/shard_map/ppermute | solution.py:465
  112.5 9.2 %collective-permute-start.26 = (bf16[192,640]{1,0:T(8,128)(2,1)}, bf16[192,640]{1,0:T(8,128)(2,1)S(1)}, u32[]{:S(2)}, u32[]{:S(2)}) collective-permute-start(bf16[192,640]{1,0:T(8,128)(2,1)} %get-tuple-element.63.refs_0_), channel_id=1, source_target_pairs={{0,16},{8,24},{16,32},{24,40},{32,48},{40,56},{48,0},{56,8},{64,80... | collective-permute-start | bytes 737288 | tf_op jit(solution)/shard_map/ppermute | solution.py:469
  112.7 8.9 %collective-permute-start.24 = (bf16[128,640]{1,0:T(8,128)(2,1)}, bf16[128,640]{1,0:T(8,128)(2,1)S(1)}, u32[]{:S(2)}, u32[]{:S(2)}) collective-permute-start(bf16[128,640]{1,0:T(8,128)(2,1)} %get-tuple-element.70), channel_id=1, source_target_pairs={{0,16},{8,24},{16,32},{24,40},{32,48},{40,56},{48,0},{56,8},{64,80... | collective-permute-start | bytes 491528 | tf_op jit(solution)/shard_map/ppermute | solution.py:465
  112.8 8.9 %collective-permute-start.27 = (bf16[128,640]{1,0:T(8,128)(2,1)}, bf16[128,640]{1,0:T(8,128)(2,1)S(1)}, u32[]{:S(2)}, u32[]{:S(2)}) collective-permute-start(bf16[128,640]{1,0:T(8,128)(2,1)} %get-tuple-element.72), channel_id=1, source_target_pairs={{0,48},{8,56},{16,0},{24,8},{32,16},{40,24},{48,32},{56,40},{64,11... | collective-permute-start | bytes 491528 | tf_op jit(solution)/shard_map/ppermute | solution.py:469
  122.5 14.8 %collective-permute-start.28 = (bf16[320,640]{1,0:T(8,128)(2,1)}, bf16[320,640]{1,0:T(8,128)(2,1)S(1)}, u32[]{:S(2)}, u32[]{:S(2)}) collective-permute-start(bf16[320,640]{1,0:T(8,128)(2,1)} %get-tuple-element.73.refs_0_), channel_id=1, source_target_pairs={{0,8},{8,0},{16,24},{24,16},{32,40},{40,32},{48,56},{56,48},{64,72... | collective-permute-start | bytes 1228808 | tf_op jit(solution)/shard_map/ppermute | solution.py:474
  132.5 4.4 %collective-permute-start.36 = (bf16[192,640]{1,0:T(8,128)(2,1)}, bf16[192,640]{1,0:T(8,128)(2,1)S(1)}, u32[]{:S(2)}, u32[]{:S(2)}) collective-permute-start(bf16[192,640]{1,0:T(8,128)(2,1)} %copy-done.11), channel_id=1, source_target_pairs={{0,8},{8,0},{16,24},{24,16},{32,40},{40,32},{48,56},{56,48},{64,72... | collective-permute-start | bytes 737288 | tf_op jit(solution)/shard_map/ppermute | solution.py:474
  132.5 4.8 %collective-permute-start.35 = (bf16[192,640]{1,0:T(8,128)(2,1)}, bf16[192,640]{1,0:T(8,128)(2,1)S(1)}, u32[]{:S(2)}, u32[]{:S(2)}) collective-permute-start(bf16[192,640]{1,0:T(8,128)(2,1)} %get-tuple-element.80.refs_7_), channel_id=1, source_target_pairs={{0,8},{8,0},{16,24},{24,16},{32,40},{40,32},{48,56},{56,48},{64,72... | collective-permute-start | bytes 737288 | tf_op jit(solution)/shard_map/ppermute | solution.py:474
  133.0 3.1 %collective-permute-start.34 = (bf16[128,640]{1,0:T(8,128)(2,1)}, bf16[128,640]{1,0:T(8,128)(2,1)S(1)}, u32[]{:S(2)}, u32[]{:S(2)}) collective-permute-start(bf16[128,640]{1,0:T(8,128)(2,1)} %get-tuple-element.79.refs_6_), channel_id=1, source_target_pairs={{0,8},{8,0},{16,24},{24,16},{32,40},{40,32},{48,56},{56,48},{64,72... | collective-permute-start | bytes 491528 | tf_op jit(solution)/shard_map/ppermute | solution.py:474
  137.4 3.2 %collective-permute-start.33 = (bf16[320,640]{1,0:T(8,128)(2,1)}, bf16[320,640]{1,0:T(8,128)(2,1)}, u32[]{:S(2)}, u32[]{:S(2)}) collective-permute-start(bf16[320,640]{1,0:T(8,128)(2,1)} %get-tuple-element.78.refs_5_), channel_id=1, source_target_pairs={{0,8},{8,0},{16,24},{24,16},{32,40},{40,32},{48,56},{56,48},{64,72... | collective-permute-start | bytes 1228808 | tf_op jit(solution)/shard_map/ppermute | solution.py:474
  (42 other events, 100.5 us)
